TPU v7x, 512 devices: a whole 4x8x8 slice. The times are simulated.
512 devices in a mesh: slab: 64 (over z_hi, y, core), dp: 8 (over z_lo, x).
Axes of the slice: x: 4, y: 8, z: 8 (z_hi: 4, z_lo: 2; z = z_hi * 2 + z_lo), core: 2. Of those that a mesh axis runs over, the one named last changes fastest.
Arguments:
- universe: bfloat16 [8, 4, 256, 4, 512], P('dp', None, 'slab'), may hold values from -6 to 6
- cotangent: bfloat16 [8, 64, 64, 1, 128], P('dp', None, 'slab'), may hold values from -0.15625 to 0.15625
- conv1_weight: bfloat16 [32, 108], replicated, may hold values from -0.625 to 0.625
- conv1_bias: float32 [32], replicated, may hold values from -3 to 3
- conv2_weight: bfloat16 [64, 864], replicated, may hold values from -0.21875 to 0.21875
- conv2_bias: float32 [64], replicated, may hold values from -3 to 3
- owners: int32 [460, 1], replicated, may hold values from 0 to 7; in each aligned block of 460 rows (0 to 459, 460 to 919, ...) at most 138 rows name the same one
- accumulated: float32 [1104, 128], P('dp'), may hold values from -1 to 1
Outputs:
- features: bfloat16 [8, 64, 64, 1, 128], P('dp', None, 'slab')
- owned: float32 [1104, 128], P('dp')
Inputs may be any that keep to these rules, and one draw needn't show every extreme that they name: `owners`: each index of dp owns at most 138 blocks, exactly 138 for one of them, and at least one for each.
All inputs are finite; a program needn't handle non-finite values.
Results may differ from a plain program's by a relative error of at most 0.0014.
The roundings to bfloat16 on the way count: a program that leaves them out, or rounds other values in their place, can miss the bound.
Values may be sent and summed in bfloat16 or wider, within the bound.
No kernel may reach another device: no remote copies, remote signals or barrier semaphores. Data moves between devices by JAX's collectives and lax.ppermute only.
A program may use at most 64 MiB of HBM per device.

v0:
```python
import jax
import jax.numpy as jnp
from jax import lax
from jax.sharding import PartitionSpec as P

NB = 460


SLOPE = 0.3
OFFSETS = [
    (first, second, third) for first in range(3) for second in range(3) for third in range(3)
]


def with_halo(block, sides, width):
    for axis, dim in sides:
        count = lax.axis_size(axis)
        forward = [(i, i + 1) for i in range(count - 1)]
        forward.append((count - 1, 0))
        backward = [(target, source) for source, target in forward]
        low = lax.ppermute(
            lax.slice_in_dim(block, block.shape[dim] - width, None, axis=dim), axis, forward
        )
        high = lax.ppermute(lax.slice_in_dim(block, 0, width, axis=dim), axis, backward)
        block = jnp.concatenate([low, block, high], axis=dim)
    return block


def pad_sides(field):
    return jnp.pad(field, ((0, 0), (0, 0), (1, 1), (1, 1)))


def tap_stack(padded, deep_rows, high_rows, wide_rows, flipped):
    pieces = [
        padded[:, first : first + deep_rows, second : second + high_rows, third : third + wide_rows]
        for first, second, third in OFFSETS
    ]
    if flipped:
        pieces = pieces[::-1]
    stacked = jnp.stack(pieces, axis=0)
    return stacked.reshape(27 * padded.shape[0], deep_rows * high_rows * wide_rows)


def average(field):
    chans, deep_rows, high_rows, wide_rows = field.shape
    return field.reshape(chans, deep_rows // 2, 2, high_rows // 2, 2, wide_rows // 2, 2).mean(
        axis=(2, 4, 6)
    )


def spread_back(field):
    return jnp.repeat(jnp.repeat(jnp.repeat(field, 2, axis=1), 2, axis=2), 2, axis=3) * 0.125


def leaky_relu(value):
    return jnp.where(value > 0, value, SLOPE * value)


def slope_mask(value):
    return jnp.where(value > 0, 1.0, SLOPE)


def place_blocks(owners, blocks, ranks, capacity):
    owner_of = owners[:, 0]
    member = (owner_of[:, None] == jnp.arange(ranks, dtype=jnp.int32)[None, :]).astype(jnp.int32)
    before = jnp.cumsum(member, axis=0) - member
    slot_index = jnp.sum(before * member, axis=1)
    target = owner_of * capacity + slot_index
    placing = (jnp.arange(ranks * capacity, dtype=jnp.int32)[:, None] == target[None, :]).astype(
        jnp.float32
    )
    return jnp.dot(placing, blocks, precision=lax.Precision.HIGHEST)


def body(
    universe, cotangent, conv1_weight, conv1_bias, conv2_weight, conv2_bias, owners, accumulated
):
    field = universe[0]
    chans_in, deep_rows, high_rows, wide_rows = field.shape
    chan_one = conv1_weight.shape[0]
    chan_two = conv2_weight.shape[0]
    half_deep, half_high, half_wide = (deep_rows // 2, high_rows // 2, wide_rows // 2)
    extended = with_halo(field, (("slab", 1),), 1)
    cols_one = tap_stack(pad_sides(extended), deep_rows, high_rows, wide_rows, False)
    pre_one = (
        jnp.dot(conv1_weight, cols_one, preferred_element_type=jnp.float32) + conv1_bias[:, None]
    )
    pre_one = pre_one.reshape(chan_one, deep_rows, high_rows, wide_rows)
    pooled = average(leaky_relu(pre_one)).astype(jnp.bfloat16)
    rimmed = with_halo(pooled, (("slab", 1),), 1)
    cols_two = tap_stack(pad_sides(rimmed), half_deep, half_high, half_wide, False)
    pre_two = (
        jnp.dot(conv2_weight, cols_two, preferred_element_type=jnp.float32) + conv2_bias[:, None]
    )
    pre_two = pre_two.reshape(chan_two, half_deep, half_high, half_wide)
    feature = average(leaky_relu(pre_two)).astype(jnp.bfloat16)
    delta_two = (spread_back(cotangent[0].astype(jnp.float32)) * slope_mask(pre_two)).astype(
        jnp.bfloat16
    )
    flat_two = delta_two.reshape(chan_two, -1)
    grad_w2 = jnp.einsum("oc,kc->ok", flat_two, cols_two, preferred_element_type=jnp.float32)
    grad_b2 = jnp.sum(flat_two.astype(jnp.float32), axis=1)
    delta_rim = with_halo(delta_two, (("slab", 1),), 1)
    cols_back = tap_stack(pad_sides(delta_rim), half_deep, half_high, half_wide, True)
    weight_back = (
        conv2_weight.reshape(chan_two, 27, chan_one)
        .transpose(2, 1, 0)
        .reshape(chan_one, 27 * chan_two)
    )
    back_pooled = jnp.dot(weight_back, cols_back, preferred_element_type=jnp.float32)
    back_pooled = back_pooled.reshape(chan_one, half_deep, half_high, half_wide)
    delta_one = (spread_back(back_pooled) * slope_mask(pre_one)).astype(jnp.bfloat16)
    flat_one = delta_one.reshape(chan_one, -1)
    grad_w1 = jnp.einsum("oc,kc->ok", flat_one, cols_one, preferred_element_type=jnp.float32)
    grad_b1 = jnp.sum(flat_one.astype(jnp.float32), axis=1)
    vector = jnp.concatenate([grad_w1.reshape(-1), grad_b1, grad_w2.reshape(-1), grad_b2])
    blocks = jnp.pad(vector, (0, NB * 128 - vector.shape[0])).reshape(NB, 128)
    ranks = lax.axis_size("dp")
    capacity = accumulated.shape[0]
    totals = lax.psum(blocks, "slab")
    packed = place_blocks(owners, totals, ranks, capacity)
    mine = lax.psum_scatter(packed, "dp", scatter_dimension=0, tiled=True)
    owned = accumulated + mine
    return (feature[None], owned)


def solution(mesh):
    in_specs = (
        P("dp", None, "slab", None, None),
        P("dp", None, "slab", None, None),
        P(),
        P(),
        P(),
        P(),
        P(),
        P("dp", None),
    )
    out_specs = (P("dp", None, "slab", None, None), P("dp", None))
    return jax.shard_map(body, mesh=mesh, in_specs=in_specs, out_specs=out_specs, check_vma=False)
```

profile of v0, /device:TPU:64, one launch (start us, length us, event | category | flops | bytes accessed | tf_op | source)
XLA Modules:
  0.0 733.3 jit_solution(869186729282681174)
XLA Ops:
  8.0 1.9 collective-permute-start
  9.9 12.4 %collective-permute-start.1 = (bf16[4,1,4,512]{3,2,1,0:T(4,128)(2,1)S(1)}, bf16[4,1,4,512]{3,2,1,0:T(4,128)(2,1)S(1)}, u32[]{:S(2)}, u32[]{:S(2)}) collective-permute-start(bf16[4,1,4,512]{3,2,1,0:T(4,128)(2,1)S(1)} %get-tuple-element.22), channel_id=1, source_target_pairs={{8,0},{16,8},{24,16},{32,24},{40,32},{48,40},{56,48},{64,56},{72,6... | collective-permute-start | bytes 49160 | tf_op jit(solution)/shard_map/ppermute | solution.py:24
  47.4 3.8 reshape.172
  51.7 2.6 copy.90
  54.3 6.5 fusion.2
  62.3 1.9 collective-permute-start.2
  64.2 8.0 %collective-permute-start.3 = (bf16[32,1,2,256]{0,3,2,1:T(8,128)(2,1)}, bf16[32,1,2,256]{0,3,2,1:T(8,128)(2,1)}, u32[]{:S(2)}, u32[]{:S(2)}) collective-permute-start(bf16[32,1,2,256]{0,3,2,1:T(8,128)(2,1)} %get-tuple-element.18), channel_id=1, source_target_pairs={{8,0},{16,8},{24,16},{32,24},{40,32},{48,40},{56,48},{64,56},{72,6... | collective-permute-start | bytes 98312 | tf_op jit(solution)/shard_map/ppermute | solution.py:24
  80.3 1.9 reshape.180
  105.7 8.2 %copy.91 = bf16[27,32,2,2,256]{4,3,2,1,0:T(2,128)(2,1)} copy(bf16[27,32,2,2,256]{1,4,3,2,0:T(8,128)(2,1)} %fusion.20) | data formatting | bytes 3538944 | tf_op jit(solution)/shard_map/stack | solution.py:40
  113.9 5.2 reshape.174
  119.1 3.3 convert_reduce_fusion.1
  124.3 1.9 collective-permute-start.4
  126.3 7.9 %collective-permute-start.5 = (bf16[64,1,2,256]{3,2,1,0:T(2,128)(2,1)}, bf16[64,1,2,256]{3,2,1,0:T(2,128)(2,1)}, u32[]{:S(2)}, u32[]{:S(2)}) collective-permute-start(bf16[64,1,2,256]{3,2,1,0:T(2,128)(2,1)} %get-tuple-element.20), channel_id=1, source_target_pairs={{8,0},{16,8},{24,16},{32,24},{40,32},{48,40},{56,48},{64,56},{72,6... | collective-permute-start | bytes 196616 | tf_op jit(solution)/shard_map/ppermute | solution.py:24
  134.1 2.9 fusion.62
  139.1 2.6 select_maximum_fusion.2
  166.6 8.9 %reshape.178 = bf16[1728,1024]{1,0:T(8,128)(2,1)} reshape(bf16[27,64,2,2,256]{4,3,2,1,0:T(2,128)(2,1)} %constant_dynamic-update-slice_fusion.27) | data formatting | bytes 7077888 | tf_op jit(solution)/shard_map/reshape | solution.py:41
  175.6 2.7 fusion.11
  178.8 3.4 broadcast_in_dim.44
  182.2 3.6 copy.99
  193.3 498.6 %all-reduce.9.cloned.1.call-done = f32[460,128]{1,0:T(8,128)} async-done(((f32[460,128]{1,0:T(8,128)}), f32[460,128]{1,0:T(8,128)}) %all-reduce.9.cloned.1.call-update) | async-done | bytes 235536 | tf_op jit(solution)/shard_map/psum | solution.py:120
  691.9 2.1 fusion.3
  694.0 23.7 %fusion = f32[144,128]{1,0:T(8,128)S(1)} fusion(f32[1104,128]{1,0:T(8,128)S(1)} %fusion.3), kind=kCustom, calls=%all-reduce-scatter | all-reduce-scatter fusion | flops 147457 | bytes 641024
  717.7 1.9 collective-permute-start.6
  720.3 5.2 collective-permute-done.6
  (159 shorter events, 97.2 us)
Async XLA Ops:
  7.2 44.1 %copy-start = (bf16[32,108]{1,0:T(8,128)(2,1)S(1)}, bf16[32,108]{1,0:T(8,128)(2,1)}, u32[]{:S(2)}) copy-start(bf16[32,108]{1,0:T(8,128)(2,1)} %param.10) | copy-start | bytes 20740
  7.2 684.7 %all-reduce.9.cloned.1.call-start = ((), (), s32[]{:S(2)}) async-start(), calls=%async_computation | async-start | bytes 475136 | tf_op jit(solution)/shard_map/psum | solution.py:120
  8.0 17.2 %collective-permute-start = (bf16[4,1,4,512]{3,2,1,0:T(4,128)(2,1)S(1)}, bf16[4,1,4,512]{3,2,1,0:T(4,128)(2,1)S(1)}, u32[]{:S(2)}, u32[]{:S(2)}) collective-permute-start(bf16[4,1,4,512]{3,2,1,0:T(4,128)(2,1)S(1)} %get-tuple-element.21), channel_id=1, source_target_pairs={{0,8},{8,16},{16,24},{24,32},{32,40},{40,48},{48,56},{56,64},{64,7... | collective-permute-start | bytes 49160 | tf_op jit(solution)/shard_map/ppermute | solution.py:21
  9.9 15.3 %collective-permute-start.1 = (bf16[4,1,4,512]{3,2,1,0:T(4,128)(2,1)S(1)}, bf16[4,1,4,512]{3,2,1,0:T(4,128)(2,1)S(1)}, u32[]{:S(2)}, u32[]{:S(2)}) collective-permute-start(bf16[4,1,4,512]{3,2,1,0:T(4,128)(2,1)S(1)} %get-tuple-element.22), channel_id=1, source_target_pairs={{8,0},{16,8},{24,16},{32,24},{40,32},{48,40},{56,48},{64,56},{72,6... | collective-permute-start | bytes 49160 | tf_op jit(solution)/shard_map/ppermute | solution.py:24
  26.9 24.4 %copy-start.11 = (f32[32]{0:T(128)S(1)}, f32[32]{0:T(128)}, u32[]{:S(2)}) copy-start(f32[32]{0:T(128)} %param.11) | copy-start | bytes 388
  54.3 18.0 %copy-start.9 = (s32[460,1]{0,1:T(1,128)S(1)}, s32[460,1]{0,1:T(1,128)}, u32[]{:S(2)}) copy-start(s32[460,1]{0,1:T(1,128)} %param.14) | copy-start | bytes 5524
  60.7 0.8 copy-start.1
  62.3 19.8 %collective-permute-start.2 = (bf16[32,1,2,256]{0,3,2,1:T(8,128)(2,1)}, bf16[32,1,2,256]{0,3,2,1:T(8,128)(2,1)}, u32[]{:S(2)}, u32[]{:S(2)}) collective-permute-start(bf16[32,1,2,256]{0,3,2,1:T(8,128)(2,1)} %get-tuple-element.17), channel_id=1, source_target_pairs={{0,8},{8,16},{16,24},{24,32},{32,40},{40,48},{48,56},{56,64},{64,7... | collective-permute-start | bytes 98312 | tf_op jit(solution)/shard_map/ppermute | solution.py:21
  64.2 17.9 %collective-permute-start.3 = (bf16[32,1,2,256]{0,3,2,1:T(8,128)(2,1)}, bf16[32,1,2,256]{0,3,2,1:T(8,128)(2,1)}, u32[]{:S(2)}, u32[]{:S(2)}) collective-permute-start(bf16[32,1,2,256]{0,3,2,1:T(8,128)(2,1)} %get-tuple-element.18), channel_id=1, source_target_pairs={{8,0},{16,8},{24,16},{32,24},{40,32},{48,40},{56,48},{64,56},{72,6... | collective-permute-start | bytes 98312 | tf_op jit(solution)/shard_map/ppermute | solution.py:24
  83.4 10.8 %copy-start.2 = (f32[32,2,2,256]{0,3,2,1:T(8,128)S(1)}, f32[32,2,2,256]{0,3,2,1:T(8,128)}, u32[]{:S(2)}) copy-start(f32[32,2,2,256]{0,3,2,1:T(8,128)} %copy-done.1) | copy-start | bytes 393220
  113.9 5.2 copy-start.6
  113.9 5.2 copy-start.12
  124.3 14.8 %collective-permute-start.4 = (bf16[64,1,2,256]{3,2,1,0:T(2,128)(2,1)}, bf16[64,1,2,256]{3,2,1,0:T(2,128)(2,1)}, u32[]{:S(2)}, u32[]{:S(2)}) collective-permute-start(bf16[64,1,2,256]{3,2,1,0:T(2,128)(2,1)} %get-tuple-element.19), channel_id=1, source_target_pairs={{0,8},{8,16},{16,24},{24,32},{32,40},{40,48},{48,56},{56,64},{64,7... | collective-permute-start | bytes 196616 | tf_op jit(solution)/shard_map/ppermute | solution.py:21
  126.3 12.8 %collective-permute-start.5 = (bf16[64,1,2,256]{3,2,1,0:T(2,128)(2,1)}, bf16[64,1,2,256]{3,2,1,0:T(2,128)(2,1)}, u32[]{:S(2)}, u32[]{:S(2)}) collective-permute-start(bf16[64,1,2,256]{3,2,1,0:T(2,128)(2,1)} %get-tuple-element.20), channel_id=1, source_target_pairs={{8,0},{16,8},{24,16},{32,24},{40,32},{48,40},{56,48},{64,56},{72,6... | collective-permute-start | bytes 196616 | tf_op jit(solution)/shard_map/ppermute | solution.py:24
  137.2 16.7 %copy-start.5 = (f32[64,256]{1,0:T(8,128)S(1)}, f32[64,256]{1,0:T(8,128)}, u32[]{:S(2)}) copy-start(f32[64,256]{1,0:T(8,128)} %copy.94) | copy-start | bytes 196612
  166.6 8.9 %copy-start.7 = (bf16[32,1728]{1,0:T(8,128)(2,1)S(1)}, bf16[32,1728]{1,0:T(8,128)(2,1)}, u32[]{:S(2)}) copy-start(bf16[32,1728]{1,0:T(8,128)(2,1)} %reshape.180) | copy-start | bytes 331780
  185.9 2.5 copy-start.4
  185.9 2.5 copy-start.10
  185.9 6.7 copy-start.3
  187.5 538.3 %copy-start.8 = (f32[138,128]{1,0:T(8,128)S(1)}, f32[138,128]{1,0:T(8,128)}, u32[]{:S(2)}) copy-start(f32[138,128]{1,0:T(8,128)} %param.15) | copy-start | bytes 211972
  717.7 7.8 %collective-permute-start.6 = (f32[42,128]{1,0:T(8,128)S(1)}, f32[42,128]{1,0:T(8,128)S(1)}, u32[]{:S(2)}, u32[]{:S(2)}) collective-permute-start(f32[42,128]{1,0:T(8,128)S(1)} %slice.446), channel_id=1, source_target_pairs={{0,1},{1,2},{2,3},{3,4},{4,5},{5,6},{6,7},{8,9},{9,10},{10,11},{11... | collective-permute-start | bytes 64520
Sparse Core Ops, SparseCore 0:
  190.8 501.0 all-reduce.8
where the time goes:
time: 735 us; the launch traced here: 733 us
  waiting for transfers between devices  504 us (69%)
  local copies, waits for them, and re-layouts  114 us (16%)
  starting transfers between devices  36 us (5%)
  other arithmetic  28.8 us (4%)
  blocking collectives  23.7 us (3%)
  between operations  15.1 us (2%)
  matrix products  12.1 us (2%)
    psum x1, waiting for transfers between devices, body(): totals = lax.psum(blocks, 'slab')  499 us
    unnamed x101, local copies, waits for them, and re-layouts  60 us
    ppermute x3, starting transfers between devices, with_halo(): lax.ppermute(lax.slice_in_dim(block, 0, width, axis=dim), axis, backward)  28.3 us
    unnamed x1, blocking collectives  23.7 us
    reshape x3, local copies, waits for them, and re-layouts, tap_stack(): stacked.reshape(27 * padded.shape[0], deep_rows * high_rows * wide_rows)  17.9 us
  transfers between devices with their start and end apart: 8, of which 2 were waited for; matrix products, arithmetic and copies ran while one was open for 3% of the time, Pallas kernels for 0%

commit v1 on v0

--- a/solution.py
+++ b/solution.py
@@ -60,16 +60,27 @@
     return jnp.where(value > 0, 1.0, SLOPE)
 
 
-def place_blocks(owners, blocks, ranks, capacity):
+def placing_matrix(owners, ranks, pitch):
     owner_of = owners[:, 0]
     member = (owner_of[:, None] == jnp.arange(ranks, dtype=jnp.int32)[None, :]).astype(jnp.int32)
     before = jnp.cumsum(member, axis=0) - member
     slot_index = jnp.sum(before * member, axis=1)
-    target = owner_of * capacity + slot_index
-    placing = (jnp.arange(ranks * capacity, dtype=jnp.int32)[:, None] == target[None, :]).astype(
+    target = owner_of * pitch + slot_index
+    return (jnp.arange(ranks * pitch, dtype=jnp.int32)[:, None] == target[None, :]).astype(
         jnp.float32
     )
-    return jnp.dot(placing, blocks, precision=lax.Precision.HIGHEST)
+
+
+def exchange(rows, axis):
+    return lax.all_to_all(rows, axis, 0, 0, tiled=True)
+
+
+def sum_to_owners(placed, ranks, slabs, share):
+    width = placed.shape[1]
+    mine = exchange(placed, "dp").reshape(ranks, -1, width).sum(axis=0)
+    mine = jnp.pad(mine, ((0, slabs * share - mine.shape[0]), (0, 0)))
+    part = exchange(mine, "slab").reshape(slabs, share, width).sum(axis=0)
+    return exchange(jnp.tile(part, (slabs, 1)), "slab")
 
 
 def body(
@@ -115,12 +126,13 @@
     grad_b1 = jnp.sum(flat_one.astype(jnp.float32), axis=1)
     vector = jnp.concatenate([grad_w1.reshape(-1), grad_b1, grad_w2.reshape(-1), grad_b2])
     blocks = jnp.pad(vector, (0, NB * 128 - vector.shape[0])).reshape(NB, 128)
-    ranks = lax.axis_size("dp")
+    ranks, slabs = lax.axis_size("dp"), lax.axis_size("slab")
     capacity = accumulated.shape[0]
-    totals = lax.psum(blocks, "slab")
-    packed = place_blocks(owners, totals, ranks, capacity)
-    mine = lax.psum_scatter(packed, "dp", scatter_dimension=0, tiled=True)
-    owned = accumulated + mine
+    pitch = -(-capacity // 16) * 16
+    placing = placing_matrix(owners, ranks, pitch)
+    placed = jnp.dot(placing, blocks, precision=lax.Precision.HIGHEST)
+    totals = sum_to_owners(placed, ranks, slabs, -(-pitch // slabs))
+    owned = accumulated + totals[:capacity]
     return (feature[None], owned)
 
 

time: 735 us -> 242 us (0.33)
  the two profiles are of different devices: /device:TPU:64 before, /device:TPU:1 now
where the time goes in v1:
time: 242 us; the launch traced here: 240 us
  local copies, waits for them, and re-layouts  113 us (47%)
  starting transfers between devices  47.7 us (20%)
  other arithmetic  30 us (12%)
  waiting for transfers between devices  24.2 us (10%)
  blocking collectives  12.7 us (5%)
  matrix products  11.2 us (5%)
    unnamed x100, local copies, waits for them, and re-layouts  58.4 us
    all_to_all x2, waiting for transfers between devices, exchange(): return lax.all_to_all(rows, axis, 0, 0, tiled=True)  24.2 us
    ppermute x3, starting transfers between devices, with_halo(): lax.ppermute(lax.slice_in_dim(block, 0, width, axis=dim), axis, backward)  22.1 us
    reshape x3, local copies, waits for them, and re-layouts, tap_stack(): stacked.reshape(27 * padded.shape[0], deep_rows * high_rows * wide_rows)  17.9 us
    all_to_all x2, starting transfers between devices, exchange(): return lax.all_to_all(rows, axis, 0, 0, tiled=True)  17.2 us
    all_to_all x1, blocking collectives, exchange(): return lax.all_to_all(rows, axis, 0, 0, tiled=True)  12.7 us
    another operation x4, local copies, waits for them, and re-layouts, tap_stack(): stacked = jnp.stack(pieces, axis=0)  10.5 us
    unnamed x8, other arithmetic  10.2 us
  transfers between devices with their start and end apart: 8, of which 2 were waited for; matrix products, arithmetic and copies ran while one was open for 9% of the time, Pallas kernels for 0%

profile of v1, /device:TPU:1, one launch (start us, length us, event | category | flops | bytes accessed | tf_op | source)
XLA Modules:
  0.0 240.0 jit_solution(9979245120286641181)
XLA Ops:
  1.5 4.6 %collective-permute-start = (bf16[4,1,4,512]{3,2,1,0:T(4,128)(2,1)S(1)}, bf16[4,1,4,512]{3,2,1,0:T(4,128)(2,1)S(1)}, u32[]{:S(2)}, u32[]{:S(2)}) collective-permute-start(bf16[4,1,4,512]{3,2,1,0:T(4,128)(2,1)S(1)} %get-tuple-element.21), channel_id=1, source_target_pairs={{0,8},{8,16},{16,24},{24,32},{32,40},{40,48},{48,56},{56,64},{64,7... | collective-permute-start | bytes 49160 | tf_op jit(solution)/shard_map/ppermute | solution.py:21
  6.1 6.1 %collective-permute-start.1 = (bf16[4,1,4,512]{3,2,1,0:T(4,128)(2,1)S(1)}, bf16[4,1,4,512]{3,2,1,0:T(4,128)(2,1)S(1)}, u32[]{:S(2)}, u32[]{:S(2)}) collective-permute-start(bf16[4,1,4,512]{3,2,1,0:T(4,128)(2,1)S(1)} %get-tuple-element.22), channel_id=1, source_target_pairs={{8,0},{16,8},{24,16},{32,24},{40,32},{48,40},{56,48},{64,56},{72,6... | collective-permute-start | bytes 49160 | tf_op jit(solution)/shard_map/ppermute | solution.py:24
  38.5 3.8 %reshape.206 = bf16[108,8192]{1,0:T(8,128)(2,1)S(1)} reshape(bf16[27,4,4,4,512]{4,3,2,1,0:T(4,128)(2,1)} %constant_dynamic-update-slice_fusion) | data formatting | bytes 3538944 | tf_op jit(solution)/shard_map/reshape | solution.py:41
  42.7 2.6 %copy.90 = f32[32,8192]{0,1:T(8,128)} copy(f32[32,8192]{1,0:T(8,128)S(1)} %fusion) | data formatting | bytes 2097152 | tf_op jit(solution)/shard_map/add | solution.py:97
  45.3 6.5 %fusion.1 = f32[32,2,2,256]{0,3,2,1:T(8,128)S(1)} fusion(f32[32,2,2,2,2,256,2]{0,6,5,4,3,2,1:T(2,128)} %bitcast.359), kind=kLoop, calls=%fused_computation.3 | loop fusion | flops 1015808 | bytes 1179648 | tf_op jit(solution)/shard_map/reduce_sum | solution.py:46
  53.4 1.9 collective-permute-start.2
  55.3 8.1 %collective-permute-start.3 = (bf16[32,1,2,256]{0,3,2,1:T(8,128)(2,1)}, bf16[32,1,2,256]{0,3,2,1:T(8,128)(2,1)}, u32[]{:S(2)}, u32[]{:S(2)}) collective-permute-start(bf16[32,1,2,256]{0,3,2,1:T(8,128)(2,1)} %get-tuple-element.18), channel_id=1, source_target_pairs={{8,0},{16,8},{24,16},{32,24},{40,32},{48,40},{56,48},{64,56},{72,6... | collective-permute-start | bytes 98312 | tf_op jit(solution)/shard_map/ppermute | solution.py:24
  71.4 1.9 reshape.214
  96.8 8.2 %copy.91 = bf16[27,32,2,2,256]{4,3,2,1,0:T(2,128)(2,1)} copy(bf16[27,32,2,2,256]{1,4,3,2,0:T(8,128)(2,1)} %fusion.21) | data formatting | bytes 3538944 | tf_op jit(solution)/shard_map/stack | solution.py:40
  105.0 5.2 %reshape.208 = bf16[864,1024]{1,0:T(8,128)(2,1)} reshape(bf16[27,32,2,2,256]{4,3,2,1,0:T(2,128)(2,1)} %copy.91) | data formatting | bytes 3538944 | tf_op jit(solution)/shard_map/reshape | solution.py:41
  110.2 3.3 %convert_reduce_fusion.1 = (f32[64]{0:T(128)}, bf16[64,1024]{1,0:T(8,128)(2,1)}, f32[64,1024]{1,0:T(8,128)S(1)}, f32[64,1024]{1,0:T(8,128)}) fusion(f32[64,1024]{1,0:T(8,128)S(1)} %copy.101, f32[64]{0:T(128)S(1)} %copy-done.13, bf16[64,864]{1,0:T(8,128)(2,1)S(1)} %copy-done.7, bf16[864,1024]{1,0:T(8,128)(2,1)} %reshape.208), kind=kOutput, calls=%fused_computation.100 | convolution fusion | flops 113704896 | bytes 2798080 | tf_op jit(solution)/shard_map/dot_general | solution.py:104
  115.4 1.9 collective-permute-start.4
  117.4 7.9 %collective-permute-start.5 = (bf16[64,1,2,256]{3,2,1,0:T(2,128)(2,1)}, bf16[64,1,2,256]{3,2,1,0:T(2,128)(2,1)}, u32[]{:S(2)}, u32[]{:S(2)}) collective-permute-start(bf16[64,1,2,256]{3,2,1,0:T(2,128)(2,1)} %get-tuple-element.20), channel_id=1, source_target_pairs={{8,0},{16,8},{24,16},{32,24},{40,32},{48,40},{56,48},{64,56},{72,6... | collective-permute-start | bytes 196616 | tf_op jit(solution)/shard_map/ppermute | solution.py:24
  125.2 2.9 %fusion.66 = f32[64,864]{1,0:T(8,128)} fusion(bf16[64,1024]{1,0:T(8,128)(2,1)} %get-tuple-element.13, bf16[864,1024]{1,0:T(8,128)(2,1)} %reshape.208), kind=kOutput, calls=%fused_computation.240 | convolution fusion | flops 113246208 | bytes 2121728 | tf_op jit(solution)/shard_map/oc,kc->ok/dot_general | solution.py:112
  130.2 2.6 %select_maximum_fusion.2 = bf16[64,4,4,258]{3,2,1,0:T(4,128)(2,1)S(1)} fusion(bf16[64,1,2,256]{3,2,1,0:T(2,128)(2,1)} %collective-permute-done.5, bf16[64,2,2,256]{3,2,1,0:T(2,128)(2,1)S(1)} %multiply_convert_fusion.4, bf16[64,1,2,256]{3,2,1,0:T(2,128)(2,1)} %collective-permute-done.4), kind=kLoop, calls=%fused_computation.34 | loop fusion | flops 5019648 | bytes 790528 | tf_op jit(solution)/shard_map/concatenate | solution.py:25
  157.7 8.9 %reshape.212 = bf16[1728,1024]{1,0:T(8,128)(2,1)} reshape(bf16[27,64,2,2,256]{4,3,2,1,0:T(2,128)(2,1)} %constant_dynamic-update-slice_fusion.27) | data formatting | bytes 7077888 | tf_op jit(solution)/shard_map/reshape | solution.py:41
  166.7 2.7 %fusion.13 = f32[32,1024]{1,0:T(8,128)S(1)} fusion(bf16[32,1728]{1,0:T(8,128)(2,1)S(1)} %copy-done.8, bf16[1728,1024]{1,0:T(8,128)(2,1)} %reshape.212), kind=kOutput, calls=%fused_computation.26 | convolution fusion | flops 113278976 | bytes 3780608 | tf_op jit(solution)/shard_map/dot_general | solution.py:121
  169.9 3.4 %broadcast_in_dim.44 = f32[32,4,4,256,2]{0,4,3,2,1:T(2,128)} broadcast(f32[32,4,4,256]{0,3,2,1:T(8,128)S(1)} %bitcast.360), dimensions={0,1,2,3} | broadcast | bytes 1572864 | tf_op jit(solution)/shard_map/broadcast_in_dim | solution.py:52
  173.3 3.6 %copy.99 = f32[32,8192]{1,0:T(8,128)} copy(f32[32,8192]{0,1:T(8,128)} %bitcast.358) | data formatting | bytes 2097152 | tf_op jit(solution)/shard_map/mul | solution.py:52
  182.2 12.7 %all_to_all.21 = f32[8,144,128]{2,1,0:T(8,128)S(1)} all-to-all(f32[8,144,128]{2,1,0:T(8,128)S(1)} %fusion.2), channel_id=1, replica_groups=mesh['slab'=64,'dp'=8] {'dp'}, dimensions={0} | all-to-all | bytes 1179648 | tf_op jit(solution)/shard_map/all_to_all | solution.py:75
  195.6 12.8 %all-to-all-start.1 = ((f32[64,3,128]{2,1,0:T(4,128)}), f32[64,3,128]{2,1,0:T(4,128)S(1)}, u32[]{:S(2)}, u32[]{:S(2)}) async-start(f32[64,3,128]{2,1,0:T(4,128)} %all_to_all.15), calls=%async_computation.1 | async-start | bytes 262144 | tf_op jit(solution)/shard_map/all_to_all | solution.py:75
  209.2 12.0 %all-to-all-done.1 = f32[64,3,128]{2,1,0:T(4,128)S(1)} async-done(((f32[64,3,128]{2,1,0:T(4,128)}), f32[64,3,128]{2,1,0:T(4,128)S(1)}, u32[]{:S(2)}, u32[]{:S(2)}) %all-to-all-start.1) | async-done | bytes 98336 | tf_op jit(solution)/shard_map/all_to_all | solution.py:75
  222.0 4.4 %all-to-all-start.2 = ((f32[64,3,128]{2,1,0:T(4,128)}), f32[64,3,128]{2,1,0:T(4,128)S(1)}, u32[]{:S(2)}, u32[]{:S(2)}) async-start(f32[64,3,128]{2,1,0:T(4,128)} %tile.2), calls=%async_computation.2 | async-start | bytes 262144 | tf_op jit(solution)/shard_map/all_to_all | solution.py:75
  227.1 12.2 %all-to-all-done.2 = f32[64,3,128]{2,1,0:T(4,128)S(1)} async-done(((f32[64,3,128]{2,1,0:T(4,128)}), f32[64,3,128]{2,1,0:T(4,128)S(1)}, u32[]{:S(2)}, u32[]{:S(2)}) %all-to-all-start.2) | async-done | bytes 98336 | tf_op jit(solution)/shard_map/all_to_all | solution.py:75
  (164 shorter events, 98.7 us)
Async XLA Ops:
  0.6 41.7 %copy-start = (bf16[32,108]{1,0:T(8,128)(2,1)S(1)}, bf16[32,108]{1,0:T(8,128)(2,1)}, u32[]{:S(2)}) copy-start(bf16[32,108]{1,0:T(8,128)(2,1)} %param.10) | copy-start | bytes 20740
  0.6 34.3 %copy-start.3 = (bf16[1,4,4,4,512]{4,3,2,1,0:T(4,128)(2,1)S(1)}, bf16[1,4,4,4,512]{4,3,2,1,0:T(4,128)(2,1)}, u32[]{:S(2)}) copy-start(bf16[1,4,4,4,512]{4,3,2,1,0:T(4,128)(2,1)} %param.8) | copy-start | bytes 196612
  1.5 15.6 %collective-permute-start = (bf16[4,1,4,512]{3,2,1,0:T(4,128)(2,1)S(1)}, bf16[4,1,4,512]{3,2,1,0:T(4,128)(2,1)S(1)}, u32[]{:S(2)}, u32[]{:S(2)}) collective-permute-start(bf16[4,1,4,512]{3,2,1,0:T(4,128)(2,1)S(1)} %get-tuple-element.21), channel_id=1, source_target_pairs={{0,8},{8,16},{16,24},{24,32},{32,40},{40,48},{48,56},{56,64},{64,7... | collective-permute-start | bytes 49160 | tf_op jit(solution)/shard_map/ppermute | solution.py:21
  6.1 11.0 %collective-permute-start.1 = (bf16[4,1,4,512]{3,2,1,0:T(4,128)(2,1)S(1)}, bf16[4,1,4,512]{3,2,1,0:T(4,128)(2,1)S(1)}, u32[]{:S(2)}, u32[]{:S(2)}) collective-permute-start(bf16[4,1,4,512]{3,2,1,0:T(4,128)(2,1)S(1)} %get-tuple-element.22), channel_id=1, source_target_pairs={{8,0},{16,8},{24,16},{32,24},{40,32},{48,40},{56,48},{64,56},{72,6... | collective-permute-start | bytes 49160 | tf_op jit(solution)/shard_map/ppermute | solution.py:24
  18.7 23.6 %copy-start.12 = (f32[32]{0:T(128)S(1)}, f32[32]{0:T(128)}, u32[]{:S(2)}) copy-start(f32[32]{0:T(128)} %param.11) | copy-start | bytes 388
  51.8 0.8 copy-start.1
  53.4 19.9 %collective-permute-start.2 = (bf16[32,1,2,256]{0,3,2,1:T(8,128)(2,1)}, bf16[32,1,2,256]{0,3,2,1:T(8,128)(2,1)}, u32[]{:S(2)}, u32[]{:S(2)}) collective-permute-start(bf16[32,1,2,256]{0,3,2,1:T(8,128)(2,1)} %get-tuple-element.17), channel_id=1, source_target_pairs={{0,8},{8,16},{16,24},{24,32},{32,40},{40,48},{48,56},{56,64},{64,7... | collective-permute-start | bytes 98312 | tf_op jit(solution)/shard_map/ppermute | solution.py:21
  55.3 18.0 %collective-permute-start.3 = (bf16[32,1,2,256]{0,3,2,1:T(8,128)(2,1)}, bf16[32,1,2,256]{0,3,2,1:T(8,128)(2,1)}, u32[]{:S(2)}, u32[]{:S(2)}) collective-permute-start(bf16[32,1,2,256]{0,3,2,1:T(8,128)(2,1)} %get-tuple-element.18), channel_id=1, source_target_pairs={{8,0},{16,8},{24,16},{32,24},{40,32},{48,40},{56,48},{64,56},{72,6... | collective-permute-start | bytes 98312 | tf_op jit(solution)/shard_map/ppermute | solution.py:24
  74.4 10.8 %copy-start.2 = (f32[32,2,2,256]{0,3,2,1:T(8,128)S(1)}, f32[32,2,2,256]{0,3,2,1:T(8,128)}, u32[]{:S(2)}) copy-start(f32[32,2,2,256]{0,3,2,1:T(8,128)} %copy-done.1) | copy-start | bytes 393220
  105.0 5.2 %copy-start.7 = (bf16[64,864]{1,0:T(8,128)(2,1)S(1)}, bf16[64,864]{1,0:T(8,128)(2,1)}, u32[]{:S(2)}) copy-start(bf16[64,864]{1,0:T(8,128)(2,1)} %param.12) | copy-start | bytes 331780
  105.0 5.2 %copy-start.13 = (f32[64]{0:T(128)S(1)}, f32[64]{0:T(128)}, u32[]{:S(2)}) copy-start(f32[64]{0:T(128)} %param.13) | copy-start | bytes 772
  115.4 14.8 %collective-permute-start.4 = (bf16[64,1,2,256]{3,2,1,0:T(2,128)(2,1)}, bf16[64,1,2,256]{3,2,1,0:T(2,128)(2,1)}, u32[]{:S(2)}, u32[]{:S(2)}) collective-permute-start(bf16[64,1,2,256]{3,2,1,0:T(2,128)(2,1)} %get-tuple-element.19), channel_id=1, source_target_pairs={{0,8},{8,16},{16,24},{24,32},{32,40},{40,48},{48,56},{56,64},{64,7... | collective-permute-start | bytes 196616 | tf_op jit(solution)/shard_map/ppermute | solution.py:21
  117.4 12.8 %collective-permute-start.5 = (bf16[64,1,2,256]{3,2,1,0:T(2,128)(2,1)}, bf16[64,1,2,256]{3,2,1,0:T(2,128)(2,1)}, u32[]{:S(2)}, u32[]{:S(2)}) collective-permute-start(bf16[64,1,2,256]{3,2,1,0:T(2,128)(2,1)} %get-tuple-element.20), channel_id=1, source_target_pairs={{8,0},{16,8},{24,16},{32,24},{40,32},{48,40},{56,48},{64,56},{72,6... | collective-permute-start | bytes 196616 | tf_op jit(solution)/shard_map/ppermute | solution.py:24
  128.3 16.7 %copy-start.6 = (f32[64,256]{1,0:T(8,128)S(1)}, f32[64,256]{1,0:T(8,128)}, u32[]{:S(2)}) copy-start(f32[64,256]{1,0:T(8,128)} %copy.94) | copy-start | bytes 196612
  157.7 8.9 %copy-start.8 = (bf16[32,1728]{1,0:T(8,128)(2,1)S(1)}, bf16[32,1728]{1,0:T(8,128)(2,1)}, u32[]{:S(2)}) copy-start(bf16[32,1728]{1,0:T(8,128)(2,1)} %reshape.214) | copy-start | bytes 331780
  177.0 2.5 %copy-start.5 = (f32[55296]{0:T(1024)S(1)}, f32[55296]{0:T(1024)}, u32[]{:S(2)}) copy-start(f32[55296]{0:T(1024)} %reshape.216) | copy-start | bytes 663556
  177.0 2.5 %copy-start.11 = (f32[64]{0:T(128)S(1)}, f32[64]{0:T(128)}, u32[]{:S(2)}) copy-start(f32[64]{0:T(128)} %get-tuple-element.12) | copy-start | bytes 772
  177.0 4.1 %copy-start.10 = (s32[460]{0:T(512)S(1)}, s32[460]{0:T(512)}, u32[]{:S(2)}) copy-start(s32[460]{0:T(512)} %multiply_add_fusion.1) | copy-start | bytes 5524
  178.6 29.9 %copy-start.4 = (f32[64,1024]{1,0:T(8,128)S(1)}, f32[64,1024]{1,0:T(8,128)}, u32[]{:S(2)}) copy-start(f32[64,1024]{1,0:T(8,128)} %get-tuple-element.23) | copy-start | bytes 786436
  179.3 60.1 %copy-start.9 = (f32[138,128]{1,0:T(8,128)S(1)}, f32[138,128]{1,0:T(8,128)}, u32[]{:S(2)}) copy-start(f32[138,128]{1,0:T(8,128)} %param.15) | copy-start | bytes 211972
  195.6 25.6 %all-to-all-start.1 = ((f32[64,3,128]{2,1,0:T(4,128)}), f32[64,3,128]{2,1,0:T(4,128)S(1)}, u32[]{:S(2)}, u32[]{:S(2)}) async-start(f32[64,3,128]{2,1,0:T(4,128)} %all_to_all.15), calls=%async_computation.1 | async-start | bytes 262144 | tf_op jit(solution)/shard_map/all_to_all | solution.py:75
  222.0 17.3 %all-to-all-start.2 = ((f32[64,3,128]{2,1,0:T(4,128)}), f32[64,3,128]{2,1,0:T(4,128)S(1)}, u32[]{:S(2)}, u32[]{:S(2)}) async-start(f32[64,3,128]{2,1,0:T(4,128)} %tile.2), calls=%async_computation.2 | async-start | bytes 262144 | tf_op jit(solution)/shard_map/all_to_all | solution.py:75

commit v2 on v1

v2 whole, which is shorter than its diff:
```python
import jax
import jax.numpy as jnp
import numpy as np
from jax import lax
from jax.experimental import pallas as pl
from jax.experimental.pallas import tpu as pltpu
from jax.sharding import PartitionSpec as P

NB = 460
NB_PAD = 512
SLOPE = 0.3
BF16 = jnp.bfloat16
F32 = jnp.float32
VMEM_LIMIT = 48 * 1024 * 1024


def tap_selection():
    select = np.zeros((108, 384), np.float32)
    for first in range(3):
        for second in range(3):
            for third in range(3):
                for chan in range(4):
                    lane = (third * 16 + chan * 4 + second - 1) % 128
                    select[(9 * first + 3 * second + third) * 4 + chan, first * 128 + lane] = 1.0
    return select


def dot(left, right, precision=None):
    return jnp.dot(left, right, preferred_element_type=F32, precision=precision)


def dot_lanes(left, right):
    return lax.dot_general(left, right, (((1,), (1,)), ((), ())), preferred_element_type=F32)


def lanes_of(shape):
    return lax.broadcasted_iota(jnp.int32, shape, 1)


def turned(value, shift):
    shift = shift % 128
    return pltpu.roll(value, shift, 1) if shift else value


def from_left(value):
    return jnp.where(lanes_of(value.shape) == 0, 0.0, pltpu.roll(value, 1, 1))


def from_right(value):
    return jnp.where(lanes_of(value.shape) == 127, 0.0, pltpu.roll(value, 127, 1))


def leaky_relu(value):
    return jnp.where(value > 0, value, SLOPE * value)


def slope_mask(value):
    return jnp.where(value > 0, 1.0, SLOPE)


def weights_kernel(w1_ref, select_ref, w2_ref, big1_ref, big2_ref, back_ref, comb_ref):
    base = dot(w1_ref[...], select_ref[...])
    y_of = lanes_of((32, 128)) % 4
    for y in range(4):
        near = jnp.abs(y_of - y) <= 1
        for r in range(4):
            for first in range(3):
                part = turned(base[:, first * 128 : first * 128 + 128], r * 16 + y)
                big1_ref[(y * 4 + r) * 32 : (y * 4 + r) * 32 + 32, first * 128 : first * 128 + 128] = (
                    jnp.where(near, part, 0.0).astype(BF16)
                )
    group = lanes_of((64, 128)) // 32

    def gathered(taps):
        result = jnp.zeros((64, 128), F32)
        for place, tap in enumerate(taps):
            if tap is not None:
                column = w2_ref[:, tap // 4 * 128 : tap // 4 * 128 + 128].astype(F32)
                result = jnp.where(group == place, turned(column, (place - tap) * 32), result)
        return result

    for first in range(3):
        for second in range(3):
            for ph in range(2):
                taps = [
                    (first * 3 + second) * 3 + col - ph if 0 <= col - ph <= 2 else None
                    for col in range(4)
                ]
                tile = gathered(taps).astype(BF16)
                for y in range(2):
                    other = y + second - 1
                    if 0 <= other < 2:
                        big2_ref[
                            (y * 2 + ph) * 64 : (y * 2 + ph) * 64 + 64,
                            first * 256 + other * 128 : first * 256 + other * 128 + 128,
                        ] = tile
    for first in range(3):
        for other in range(2):
            for pair in range(2):
                tiles = []
                for col in (2 * pair, 2 * pair + 1):
                    taps = [
                        ((2 - first) * 3 + 1 - (other - y)) * 3 + 2 - (col - ph)
                        if 0 <= col - ph <= 2
                        else None
                        for y in range(2)
                        for ph in range(2)
                    ]
                    tiles.append(gathered(taps))
                at = first * 512 + other * 256 + pair * 128
                back_ref[:, at : at + 128] = jnp.concatenate(tiles, axis=0).T.astype(BF16)
    for col in range(6):
        cell = lax.broadcasted_iota(jnp.int32, (512, 128), 0)
        comb_ref[:, col * 128 : col * 128 + 128] = jnp.where(
            cell == 4 * lanes_of((512, 128)) + col - 1, 1.0, 0.0
        ).astype(BF16)


def main_kernel(
    prev_ref,
    own_ref,
    next_ref,
    after_ref,
    big1_ref,
    big2_ref,
    back_ref,
    comb_ref,
    bias1_ref,
    bias2_ref,
    target_ref,
    select_ref,
    feature_ref,
    placed_ref,
    field_ref,
    pooled_ref,
    delta2_ref,
    pre_ref,
    delta1_ref,
    blocks_ref,
    order_ref,
):
    source = jnp.concatenate(
        [prev_ref[16:64, :], own_ref[0:64, :], next_ref[0:64, :], after_ref[0:48, :]], axis=0
    )
    for layer in range(14):
        field_ref[layer * 128 + 96 : layer * 128 + 128, :] = jnp.zeros((32, 128), BF16)
    for col in range(6):
        part = dot(source, comb_ref[:, col * 128 : col * 128 + 128]).astype(BF16)
        for layer in range(14):
            at = layer * 128 + col * 16
            field_ref[at : at + 16, :] = part[layer * 16 : layer * 16 + 16, :]

    bias1 = jnp.broadcast_to(bias1_ref[...], (32, 128))
    for half in range(6):
        sums = [None] * 4
        for deep in range(2):
            at = (2 * half + deep) * 128
            conv = dot(big1_ref[...], field_ref[at : at + 384, :])
            for y in range(4):
                for r in range(4):
                    block = conv[(y * 4 + r) * 32 : (y * 4 + r) * 32 + 32, :] + bias1
                    if half in (2, 3):
                        row = (2 * (half - 2) + deep) * 512 + (y * 4 + r) * 32
                        pre_ref[row : row + 32, :] = block
                    value = leaky_relu(block)
                    slot = y // 2 * 2 + r // 2
                    sums[slot] = value if sums[slot] is None else sums[slot] + value
        for y in range(2):
            even = (sums[2 * y] * 0.125).astype(BF16).astype(F32)
            odd = (sums[2 * y + 1] * 0.125).astype(BF16).astype(F32)
            at = half * 256 + y * 128
            pooled_ref[at : at + 128, :] = jnp.concatenate(
                [from_left(odd), even, odd, from_right(even)], axis=0
            ).astype(BF16)

    bias2 = jnp.broadcast_to(bias2_ref[...], (64, 128))
    total = jnp.zeros((64, 128), F32)
    for half in range(4):
        conv = dot(big2_ref[...], pooled_ref[half * 256 : half * 256 + 768, :])
        upstream_ref = own_ref if half < 2 else next_ref
        upstream = (
            jnp.concatenate(
                [upstream_ref[64:80, u * 128 : u * 128 + 128] for u in range(4)], axis=0
            ).astype(F32)
            * 0.125
        )
        for y in range(2):
            deltas = []
            for ph in range(2):
                block = conv[(y * 2 + ph) * 64 : (y * 2 + ph) * 64 + 64, :] + bias2
                if half < 2:
                    total = total + leaky_relu(block)
                deltas.append((upstream * slope_mask(block)).astype(BF16).astype(F32))
            at = half * 512 + y * 256
            delta2_ref[at : at + 256, :] = jnp.concatenate(
                [from_left(deltas[1]), deltas[0], deltas[1], from_right(deltas[0])], axis=0
            ).astype(BF16)
    feature = total * 0.125
    for u in range(4):
        order_ref[pl.ds(u, 16, stride=4), :] = feature[u * 16 : u * 16 + 16, :]
    feature_ref[...] = order_ref[...].astype(BF16)

    ones = jnp.ones((8, 128), BF16)
    grad2 = None
    bias_sum2 = None
    for half in (1, 2):
        delta = jnp.concatenate(
            [
                delta2_ref[half * 512 + 64 : half * 512 + 192, :],
                delta2_ref[half * 512 + 320 : half * 512 + 448, :],
            ],
            axis=0,
        )
        term = dot_lanes(delta, pooled_ref[half * 256 : half * 256 + 768, :])
        bias_term = dot_lanes(ones, delta)
        grad2 = term if grad2 is None else grad2 + term
        bias_sum2 = bias_term if bias_sum2 is None else bias_sum2 + bias_term

    grad1 = None
    bias_sum1 = None
    for half in (1, 2):
        back = dot(back_ref[...], delta2_ref[(half - 1) * 512 : (half + 2) * 512, :]) * 0.125
        for deep in range(2):
            number = 2 * (half - 1) + deep
            for y in range(4):
                for r in range(4):
                    row = number * 512 + (y * 4 + r) * 32
                    slot = (y // 2 * 2 + r // 2) * 32
                    delta1_ref[row : row + 32, :] = (
                        back[slot : slot + 32, :] * slope_mask(pre_ref[row : row + 32, :])
                    ).astype(BF16)
            delta = delta1_ref[number * 512 : number * 512 + 512, :]
            at = (number + 4) * 128
            term = dot_lanes(delta, field_ref[at : at + 384, :])
            bias_term = dot_lanes(ones, delta)
            grad1 = term if grad1 is None else grad1 + term
            bias_sum1 = bias_term if bias_sum1 is None else bias_sum1 + bias_term

    exact = lax.Precision.HIGHEST
    q = lax.broadcasted_iota(jnp.int32, (512, 128), 0)
    bias_row1 = dot(bias_sum1, jnp.where(q % 32 == lanes_of((512, 128)), 1.0, 0.0), exact)
    q = lax.broadcasted_iota(jnp.int32, (256, 128), 0)
    lane = 32 + 4 * (q % 16) + q % 64 // 16
    bias_row2 = dot(bias_sum2, jnp.where(lane == lanes_of((256, 128)), 1.0, 0.0), exact)

    y_of = lanes_of((32, 128)) % 4
    parts = []
    for first in range(3):
        part = jnp.zeros((32, 128), F32)
        for y in range(4):
            near = jnp.abs(y_of - y) <= 1
            for r in range(4):
                row = (y * 4 + r) * 32
                block = grad1[row : row + 32, first * 128 : first * 128 + 128]
                part = part + turned(jnp.where(near, block, 0.0), -(r * 16 + y))
        parts.append(part)
    flat1 = dot(jnp.concatenate(parts, axis=1), select_ref[...], exact)
    rows = [None] * 28
    lane8 = lanes_of((8, 128))
    for o in range(32):
        begin = o * 108 // 128
        shift = o * 108 % 128
        moved = turned(flat1[o // 8 * 8 : o // 8 * 8 + 8, :], shift)
        for row, kept in ((begin, lane8 >= shift), (begin + 1, lane8 < shift)):
            if row == begin or shift + 108 > 128:
                term = jnp.where(kept, moved, 0.0)[o % 8 : o % 8 + 1, :]
                rows[row] = term if rows[row] is None else rows[row] + term
    for row in range(27):
        blocks_ref[row : row + 1, :] = rows[row]

    taps = []
    for first in range(3):
        for second in range(3):
            part = None
            for y in range(2):
                other = y + second - 1
                if 0 <= other < 2:
                    for ph in range(2):
                        row = (y * 2 + ph) * 64
                        at = first * 256 + other * 128
                        block = turned(grad2[row : row + 64, at : at + 128], -ph * 32)
                        part = block if part is None else part + block
            taps.append(part)
    group = lanes_of((16, 128)) // 32

    def chunk(number, place):
        u, tap = (number - 1) // 27, (number - 1) % 27
        return turned(taps[tap // 3][u * 16 : u * 16 + 16, :], (place - tap % 3) * 32)

    last = pltpu.roll(chunk(108, 0), 1, 0)
    row_of = lax.broadcasted_iota(jnp.int32, (16, 128), 0)
    for k in range(27):
        if k == 0:
            value = jnp.where(row_of == 0, jnp.broadcast_to(bias_row1[0:1, :], (16, 128)), last)
        else:
            value = chunk(4 * k, 0)
        for place in range(1, 4):
            value = jnp.where(group == place, chunk(4 * k + place, place), value)
        blocks_ref[pl.ds(27 + k, 16, stride=27), :] = value
    blocks_ref[459:460, :] = jnp.where(lanes_of((1, 128)) < 32, last[0:1, :], bias_row2[0:1, :])
    blocks_ref[NB:NB_PAD, :] = jnp.zeros((NB_PAD - NB, 128), F32)

    blocks = blocks_ref[...]
    high = blocks.astype(BF16)
    rest = blocks - high.astype(F32)
    middle = rest.astype(BF16)
    low = (rest - middle.astype(F32)).astype(BF16)
    terms = jnp.concatenate([high, middle, low], axis=1)
    target = target_ref[...]
    for tile in range(placed_ref.shape[0] // 128):
        row_at = lax.broadcasted_iota(jnp.int32, (128, NB_PAD), 0) + tile * 128
        placing = jnp.where(row_at == target, 1.0, 0.0).astype(BF16)
        moved = dot(placing, terms)
        placed_ref[tile * 128 : tile * 128 + 128, :] = (
            moved[:, 0:128] + moved[:, 128:256] + moved[:, 256:384]
        )


def whole():
    return pl.BlockSpec(memory_space=pltpu.VMEM)


def expand_weights(w1, w2_padded):
    return pl.pallas_call(
        weights_kernel,
        out_shape=(
            jax.ShapeDtypeStruct((512, 384), BF16),
            jax.ShapeDtypeStruct((256, 768), BF16),
            jax.ShapeDtypeStruct((128, 1536), BF16),
            jax.ShapeDtypeStruct((512, 768), BF16),
        ),
        in_specs=[whole()] * 3,
        out_specs=(whole(),) * 4,
        compiler_params=pltpu.CompilerParams(vmem_limit_bytes=VMEM_LIMIT),
        cost_estimate=pl.CostEstimate(flops=1 << 26, bytes_accessed=4 << 20, transcendentals=0),
    )(w1, jnp.asarray(tap_selection(), BF16), w2_padded)


def forward_backward(packed, weights, bias1, bias2, target, placed_rows):
    return pl.pallas_call(
        main_kernel,
        out_shape=(
            jax.ShapeDtypeStruct((64, 128), BF16),
            jax.ShapeDtypeStruct((placed_rows, 128), F32),
        ),
        in_specs=[whole()] * 12,
        out_specs=(whole(),) * 2,
        scratch_shapes=[
            pltpu.VMEM((14 * 128, 128), BF16),
            pltpu.VMEM((6 * 256, 128), BF16),
            pltpu.VMEM((4 * 512, 128), BF16),
            pltpu.VMEM((4 * 512, 128), F32),
            pltpu.VMEM((4 * 512, 128), BF16),
            pltpu.VMEM((NB_PAD, 128), F32),
            pltpu.VMEM((64, 128), F32),
        ],
        compiler_params=pltpu.CompilerParams(vmem_limit_bytes=VMEM_LIMIT),
        cost_estimate=pl.CostEstimate(flops=1 << 31, bytes_accessed=4 << 20, transcendentals=0),
    )(
        *packed,
        *weights,
        bias1,
        bias2,
        target,
        jnp.asarray(np.pad(tap_selection().T, ((0, 0), (0, 20))), F32),
    )


def block_targets(owners, ranks, pitch):
    owner_of = owners[:, 0]
    member = (owner_of[:, None] == jnp.arange(ranks, dtype=jnp.int32)[None, :]).astype(jnp.int32)
    before = jnp.cumsum(member, axis=0) - member
    slot_index = jnp.sum(before * member, axis=1)
    target = owner_of * pitch + slot_index
    return jnp.pad(target[None, :], ((0, 0), (0, NB_PAD - NB)), constant_values=-1)


def exchange(rows, axis):
    return lax.all_to_all(rows, axis, 0, 0, tiled=True)


def sum_to_owners(placed, ranks, slabs, share):
    width = placed.shape[1]
    mine = exchange(placed, "dp").reshape(ranks, -1, width).sum(axis=0)
    mine = jnp.pad(mine, ((0, slabs * share - mine.shape[0]), (0, 0)))
    part = exchange(mine, "slab").reshape(slabs, share, width).sum(axis=0)
    return exchange(jnp.tile(part, (slabs, 1)), "slab")


def body(
    universe, cotangent, conv1_weight, conv1_bias, conv2_weight, conv2_bias, owners, accumulated
):
    ranks, slabs = lax.axis_size("dp"), lax.axis_size("slab")
    packed = jnp.concatenate(
        [universe[0].transpose(1, 0, 2, 3).reshape(64, 512), cotangent.reshape(16, 512)], axis=0
    )

    def from_slab(distance):
        pairs = [(i, (i - distance) % slabs) for i in range(slabs)]
        return lax.ppermute(packed, "slab", pairs)

    spans = (from_slab(-1), packed, from_slab(1), from_slab(2))
    w2 = conv2_weight.reshape(16, 4, 864).transpose(1, 0, 2).reshape(64, 864)
    weights = expand_weights(conv1_weight, jnp.pad(w2, ((0, 0), (0, 32))))
    bias2 = conv2_bias.reshape(16, 4).T.reshape(64, 1)
    capacity = accumulated.shape[0]
    step = max(16, 128 // ranks)
    pitch = -(-capacity // step) * step
    target = block_targets(owners, ranks, pitch)
    feature, placed = forward_backward(
        spans, weights, conv1_bias.reshape(32, 1), bias2, target, ranks * pitch
    )
    totals = sum_to_owners(placed, ranks, slabs, -(-pitch // slabs))
    owned = accumulated + totals[:capacity]
    return (feature.reshape(1, 64, 1, 1, 128), owned)


def solution(mesh):
    in_specs = (
        P("dp", None, "slab", None, None),
        P("dp", None, "slab", None, None),
        P(),
        P(),
        P(),
        P(),
        P(),
        P("dp", None),
    )
    out_specs = (P("dp", None, "slab", None, None), P("dp", None))
    return jax.shard_map(body, mesh=mesh, in_specs=in_specs, out_specs=out_specs, check_vma=False)
```

time: 242 us -> 86 us (0.36)
  local copies, waits for them, and re-layouts: 113 us -> 5.35 us
  blocking collectives: 12.7 us -> 51 us
  other arithmetic: 30 us -> 2.06 us
  starting transfers between devices: 47.7 us -> 20.1 us
  waiting for transfers between devices: 24.2 us -> 0.01 us
  matrix products: 11.2 us -> 0 us
  Pallas kernels: 0 us -> 6.09 us
    unnamed x100 -> x17, local copies, waits for them, and re-layouts: 58.4 us -> 2.97 us
    all_to_all x1 -> x3, blocking collectives: 12.7 us -> 51 us  [exchange(): return lax.all_to_all(rows, axis, 0, 0, tiled=True)]
    all_to_all x2 -> x0, waiting for transfers between devices: 24.2 us -> none  [exchange(): return lax.all_to_all(rows, axis, 0, 0, tiled=True)]
    reshape x6 -> x7, local copies, waits for them, and re-layouts: 21.7 us -> 1.06 us  [the longest x1 0.74 us: body(): cotangent.reshape(16, 512)]
    all_to_all x2 -> x0, starting transfers between devices: 17.2 us -> none  [exchange(): return lax.all_to_all(rows, axis, 0, 0, tiled=True)]
    dot_general x6 -> x0, matrix products: 11.2 us -> none  [the longest x1 3.34 us: body(): jnp.dot(conv2_weight, cols_two, preferred_element_type=jnp.float32)]
    another operation x5 -> x1, local copies, waits for them, and re-layouts: 10.5 us -> 0.01 us  [the longest x4 10.5 us: tap_stack(): stacked = jnp.stack(pieces, axis=0)]
    ppermute x6 -> x3, starting transfers between devices: 30.5 us -> 20.1 us  [from_slab(): return lax.ppermute(packed, 'slab', pairs)]
  transfers between devices with their start and end apart: 8 -> 3, of which waited for: 2 -> 0; matrix products, arithmetic and copies ran while one was open for 9% -> 2% of each run, Pallas kernels for 0% -> 1%
where the time goes in v2:
time: 86 us; the launch traced here: 85.5 us
  blocking collectives  51 us (59%)
  starting transfers between devices  20.1 us (23%)
  Pallas kernels  6.09 us (7%)
  local copies, waits for them, and re-layouts  5.35 us (6%)
  other arithmetic  2.06 us (2%)
  between operations  0.9 us (1%)
    all_to_all x3, blocking collectives, exchange(): return lax.all_to_all(rows, axis, 0, 0, tiled=True)  51 us
    ppermute x3, starting transfers between devices, from_slab(): return lax.ppermute(packed, 'slab', pairs)  20.1 us
    pallas_call x1, Pallas kernels, forward_backward(): pl.pallas_call(main_kernel, out_shape=(jax.ShapeDtypeStruct((64, 128), BF...  4.9 us
    unnamed x17, local copies, waits for them, and re-layouts  2.97 us
  transfers between devices with their start and end apart: 3, of which 0 were waited for; matrix products, arithmetic and copies ran while one was open for 2% of the time, Pallas kernels for 1%

profile of v2, /device:TPU:1, one launch (start us, length us, event | category | flops | bytes accessed | tf_op | source)
XLA Modules:
  0.0 85.5 jit_solution(8821562330307518060)
XLA Ops:
  0.6 0.7 reshape.75
  1.4 0.9 %copy.17 = bf16[4,4,4,512]{3,2,1,0:T(4,128)(2,1)S(1)} copy(bf16[4,4,4,512]{3,2,0,1:T(4,128)(2,1)} %bitcast.26) | data formatting | bytes 131072 | tf_op jit(solution)/shard_map/transpose | solution.py:395
  2.3 14.5 %collective-permute-start.2 = (bf16[80,512]{1,0:T(8,128)(2,1)S(1)}, bf16[80,512]{1,0:T(8,128)(2,1)S(1)}, u32[]{:S(2)}, u32[]{:S(2)}) collective-permute-start(bf16[80,512]{1,0:T(8,128)(2,1)S(1)} %constant_dynamic-update-slice_fusion.own_ref), channel_id=1, source_target_pairs={{0,496},{8,504},{16,0},{24,8},{32,16},{40,24},{48,32},{56,40},{64,... | collective-permute-start | bytes 245768 | tf_op jit(solution)/shard_map/ppermute | solution.py:400
  16.8 2.9 %collective-permute-start.1 = (bf16[80,512]{1,0:T(8,128)(2,1)S(1)}, bf16[80,512]{1,0:T(8,128)(2,1)S(1)}, u32[]{:S(2)}, u32[]{:S(2)}) collective-permute-start(bf16[80,512]{1,0:T(8,128)(2,1)S(1)} %constant_dynamic-update-slice_fusion.own_ref), channel_id=1, source_target_pairs={{0,504},{8,0},{16,8},{24,16},{32,24},{40,32},{48,40},{56,48},{64,5... | collective-permute-start | bytes 245768 | tf_op jit(solution)/shard_map/ppermute | solution.py:400
  19.7 2.7 %collective-permute-start = (bf16[80,512]{1,0:T(8,128)(2,1)S(1)}, bf16[80,512]{1,0:T(8,128)(2,1)S(1)}, u32[]{:S(2)}, u32[]{:S(2)}) collective-permute-start(bf16[80,512]{1,0:T(8,128)(2,1)S(1)} %constant_dynamic-update-slice_fusion.own_ref), channel_id=1, source_target_pairs={{0,8},{8,16},{16,24},{24,32},{32,40},{40,48},{48,56},{56,64},{64,7... | collective-permute-start | bytes 245768 | tf_op jit(solution)/shard_map/ppermute | solution.py:400
  22.5 1.1 %reduce-window.6 = s32[8,4,128]{2,0,1:T(8,128)S(1)} reduce-window(s32[8,4,128]{2,0,1:T(8,128)S(1)} %convert_bitcast_fusion, s32[]{:T(128)} %constant.18.clone.1), window={size=1x1x128 pad=0_0x0_0x127_0}, to_apply=%region_0.1 | reduce-window | flops 520192 | bytes 32772 | tf_op jit(solution)/shard_map/reduce-window
  23.6 0.2 slice_reduce_fusion
  23.9 0.1 add_bitcast_fusion
  24.0 0.6 copy-done.6
  24.6 0.1 reshape.79
  24.7 0.1 copy.19
  24.8 0.7 copy-done.7
  25.5 0.1 copy.20.bias1_ref
  25.6 0.1 reshape.85.bias2_ref
  25.7 0.0 copy-start.2
  25.8 0.8 copy-done.2
  26.6 1.2 %shard_map.113 = (bf16[512,384]{1,0:T(8,128)(2,1)S(1)}, bf16[256,768]{1,0:T(8,128)(2,1)S(1)}, bf16[128,1536]{1,0:T(8,128)(2,1)S(1)}, bf16[512,768]{1,0:T(8,128)(2,1)S(1)}) custom-call(bf16[32,108]{1,0:T(8,128)(2,1)S(1)} %copy-done, bf16[108,384]{1,0:T(8,128)(2,1)S(1)} %copy-done.2, bf16[64,896]{1,0:T(8,128)(2,1)S(1)} %pad.16.w2_ref), custom_call_target="tpu_custom_call" | custom-call | flops 67108864 | bytes 4194304 | tf_op jit(solution)/shard_map/pallas_call | solution.py:324
  27.8 4.9 %shard_map.114 = (bf16[64,128]{1,0:T(8,128)(2,1)}, f32[1152,128]{1,0:T(8,128)S(1)}) custom-call(bf16[80,512]{1,0:T(8,128)(2,1)S(1)} %collective-permute-done.prev_ref, bf16[80,512]{1,0:T(8,128)(2,1)S(1)} %constant_dynamic-update-slice_fusion.own_ref, bf16[80,512]{1,0:T(8,128)(2,1)S(1)} %collective-permute-done.1.next_ref, ...), custom_call_target="tpu_custom_call" | custom-call | flops 2147483648 | bytes 4194304 | tf_op jit(solution)/shard_map/pallas_call | solution.py:340
  32.7 12.7 %all_to_all.24 = f32[8,144,128]{2,1,0:T(8,128)S(1)} all-to-all(f32[8,144,128]{2,1,0:T(8,128)S(1)} %bitcast.24), channel_id=1, replica_groups=mesh['slab'=64,'dp'=8] {'dp'}, dimensions={0} | all-to-all | bytes 1179648 | tf_op jit(solution)/shard_map/all_to_all | solution.py:379
  45.6 21.4 %all_to_all.25 = f32[64,3,128]{2,1,0:T(4,128)S(1)} all-to-all(f32[64,3,128]{2,1,0:T(4,128)S(1)} %all_to_all.18), channel_id=1, replica_groups=mesh['slab'=64,'dp'=8] {'slab'}, dimensions={0} | all-to-all | bytes 196608 | tf_op jit(solution)/shard_map/all_to_all | solution.py:379
  67.0 0.1 reduce_sum.32
  67.1 16.9 %all_to_all.26 = f32[64,3,128]{2,1,0:T(4,128)S(1)} all-to-all(f32[64,3,128]{2,1,0:T(4,128)S(1)} %tile.2), channel_id=1, replica_groups=mesh['slab'=64,'dp'=8] {'slab'}, dimensions={0} | all-to-all | bytes 196608 | tf_op jit(solution)/shard_map/all_to_all | solution.py:379
  84.0 0.8 copy-done.4
  84.9 0.6 add.20
  (33 shorter events, 0.4 us)
Async XLA Ops:
  2.3 20.1 %copy-start.5 = (s32[460,1]{0,1:T(1,128)S(1)}, s32[460,1]{0,1:T(1,128)}, u32[]{:S(2)}) copy-start(s32[460,1]{0,1:T(1,128)} %param.16) | copy-start | bytes 5524
  2.3 23.3 %copy-start.3 = (bf16[64,864]{1,0:T(8,128)(2,1)S(1)}, bf16[64,864]{1,0:T(8,128)(2,1)}, u32[]{:S(2)}) copy-start(bf16[64,864]{1,0:T(8,128)(2,1)} %param.14) | copy-start | bytes 331780
  2.3 25.5 %collective-permute-start.2 = (bf16[80,512]{1,0:T(8,128)(2,1)S(1)}, bf16[80,512]{1,0:T(8,128)(2,1)S(1)}, u32[]{:S(2)}, u32[]{:S(2)}) collective-permute-start(bf16[80,512]{1,0:T(8,128)(2,1)S(1)} %constant_dynamic-update-slice_fusion.own_ref), channel_id=1, source_target_pairs={{0,496},{8,504},{16,0},{24,8},{32,16},{40,24},{48,32},{56,40},{64,... | collective-permute-start | bytes 245768 | tf_op jit(solution)/shard_map/ppermute | solution.py:400
  16.8 10.9 %collective-permute-start.1 = (bf16[80,512]{1,0:T(8,128)(2,1)S(1)}, bf16[80,512]{1,0:T(8,128)(2,1)S(1)}, u32[]{:S(2)}, u32[]{:S(2)}) collective-permute-start(bf16[80,512]{1,0:T(8,128)(2,1)S(1)} %constant_dynamic-update-slice_fusion.own_ref), channel_id=1, source_target_pairs={{0,504},{8,0},{16,8},{24,16},{32,24},{40,32},{48,40},{56,48},{64,5... | collective-permute-start | bytes 245768 | tf_op jit(solution)/shard_map/ppermute | solution.py:400
  19.7 8.1 %collective-permute-start = (bf16[80,512]{1,0:T(8,128)(2,1)S(1)}, bf16[80,512]{1,0:T(8,128)(2,1)S(1)}, u32[]{:S(2)}, u32[]{:S(2)}) collective-permute-start(bf16[80,512]{1,0:T(8,128)(2,1)S(1)} %constant_dynamic-update-slice_fusion.own_ref), channel_id=1, source_target_pairs={{0,8},{8,16},{16,24},{24,32},{32,40},{40,48},{48,56},{56,64},{64,7... | collective-permute-start | bytes 245768 | tf_op jit(solution)/shard_map/ppermute | solution.py:400
  24.0 0.7 copy-start.6
  24.8 0.7 copy-start.7
  25.7 0.9 %copy-start.2 = (bf16[108,384]{1,0:T(8,128)(2,1)S(1)}, bf16[108,384]{1,0:T(8,128)(2,1)}, u32[]{:S(2)}) copy-start(bf16[108,384]{1,0:T(8,128)(2,1)} %constant.21.clone.select_ref) | copy-start | bytes 248836
  25.7 0.8 copy-start
  25.8 2.1 %copy-start.1 = (f32[384,128]{1,0:T(8,128)S(1)}, f32[384,128]{1,0:T(8,128)}, u32[]{:S(2)}) copy-start(f32[384,128]{1,0:T(8,128)} %constant.22.clone.select_ref) | copy-start | bytes 589828
  84.0 0.9 %copy-start.4 = (f32[138,128]{1,0:T(8,128)S(1)}, f32[138,128]{1,0:T(8,128)}, u32[]{:S(2)}) copy-start(f32[138,128]{1,0:T(8,128)} %param.17) | copy-start | bytes 211972

commit v3 on v2

--- a/solution.py
+++ b/solution.py
@@ -4,6 +4,7 @@
 from jax import lax
 from jax.experimental import pallas as pl
 from jax.experimental.pallas import tpu as pltpu
+from jax.sharding import Mesh
 from jax.sharding import PartitionSpec as P
 
 NB = 460
@@ -50,6 +51,10 @@
     return jnp.where(lanes_of(value.shape) == 127, 0.0, pltpu.roll(value, 127, 1))
 
 
+def side_by_side(ref, at, step, rows):
+    return jnp.concatenate([ref[at : at + rows, :], ref[at + step : at + step + rows, :]], axis=1)
+
+
 def leaky_relu(value):
     return jnp.where(value > 0, value, SLOPE * value)
 
@@ -58,7 +63,46 @@
     return jnp.where(value > 0, 1.0, SLOPE)
 
 
-def weights_kernel(w1_ref, select_ref, w2_ref, big1_ref, big2_ref, back_ref, comb_ref):
+def channel_order():
+    row = lax.broadcasted_iota(jnp.int32, (64, 64), 0)
+    return jnp.where(lanes_of((64, 64)) == 4 * (row % 16) + row // 16, 1.0, 0.0)
+
+
+def weights_kernel(
+    rank_ref,
+    w1_ref,
+    select_ref,
+    w2_ref,
+    bias1_ref,
+    bias2_ref,
+    owners_ref,
+    accumulated_ref,
+    big1_ref,
+    big2_ref,
+    back_ref,
+    comb_ref,
+    wide1_ref,
+    wide2_ref,
+    target_ref,
+    kept_ref,
+    ordered_ref,
+):
+    kept_ref[...] = accumulated_ref[...]
+    ordered_ref[:, 768:896] = jnp.zeros((64, 128), F32)
+    ordered_ref[:, 0:864] = dot(channel_order().astype(BF16), w2_ref[...])
+    place = lax.broadcasted_iota(jnp.int32, (32, 32), 0) == lanes_of((32, 32))
+    column = jnp.sum(jnp.where(place, bias1_ref[...], 0.0), axis=1, keepdims=True)
+    wide1_ref[...] = jnp.broadcast_to(column, (32, 128))
+    column = jnp.sum(channel_order() * bias2_ref[...], axis=1, keepdims=True)
+    wide2_ref[...] = jnp.broadcast_to(column, (64, 128))
+
+    mine = owners_ref[...] == rank_ref[0]
+    member = jnp.broadcast_to(jnp.where(mine, 1.0, 0.0), (8, NB)).astype(BF16)
+    earlier = lax.broadcasted_iota(jnp.int32, (NB, NB), 0) < lanes_of((NB, NB))
+    before = dot(member, jnp.where(earlier, 1.0, 0.0).astype(BF16))[0:1, :]
+    target_ref[:, 384:NB_PAD] = jnp.full((1, 128), -1, jnp.int32)
+    target_ref[:, 0:NB] = jnp.where(mine, before.astype(jnp.int32), -1)
+
     base = dot(w1_ref[...], select_ref[...])
     y_of = lanes_of((32, 128)) % 4
     for y in range(4):
@@ -75,7 +119,7 @@
         result = jnp.zeros((64, 128), F32)
         for place, tap in enumerate(taps):
             if tap is not None:
-                column = w2_ref[:, tap // 4 * 128 : tap // 4 * 128 + 128].astype(F32)
+                column = ordered_ref[:, tap // 4 * 128 : tap // 4 * 128 + 128]
                 result = jnp.where(group == place, turned(column, (place - tap) * 32), result)
         return result
 
@@ -125,18 +169,16 @@
     big2_ref,
     back_ref,
     comb_ref,
-    bias1_ref,
-    bias2_ref,
-    target_ref,
+    wide1_ref,
+    wide2_ref,
     select_ref,
     feature_ref,
-    placed_ref,
+    blocks_ref,
     field_ref,
     pooled_ref,
     delta2_ref,
     pre_ref,
     delta1_ref,
-    blocks_ref,
     order_ref,
 ):
     source = jnp.concatenate(
@@ -150,15 +192,17 @@
             at = layer * 128 + col * 16
             field_ref[at : at + 16, :] = part[layer * 16 : layer * 16 + 16, :]
 
-    bias1 = jnp.broadcast_to(bias1_ref[...], (32, 128))
+    bias1 = wide1_ref[...]
     for half in range(6):
         sums = [None] * 4
+        conv = dot(big1_ref[...], side_by_side(field_ref, 2 * half * 128, 128, 384))
         for deep in range(2):
-            at = (2 * half + deep) * 128
-            conv = dot(big1_ref[...], field_ref[at : at + 384, :])
             for y in range(4):
                 for r in range(4):
-                    block = conv[(y * 4 + r) * 32 : (y * 4 + r) * 32 + 32, :] + bias1
+                    block = (
+                        conv[(y * 4 + r) * 32 : (y * 4 + r) * 32 + 32, deep * 128 : deep * 128 + 128]
+                        + bias1
+                    )
                     if half in (2, 3):
                         row = (2 * (half - 2) + deep) * 512 + (y * 4 + r) * 32
                         pre_ref[row : row + 32, :] = block
@@ -173,10 +217,12 @@
                 [from_left(odd), even, odd, from_right(even)], axis=0
             ).astype(BF16)
 
-    bias2 = jnp.broadcast_to(bias2_ref[...], (64, 128))
+    bias2 = wide2_ref[...]
     total = jnp.zeros((64, 128), F32)
     for half in range(4):
-        conv = dot(big2_ref[...], pooled_ref[half * 256 : half * 256 + 768, :])
+        if half % 2 == 0:
+            conv = dot(big2_ref[...], side_by_side(pooled_ref, half * 256, 256, 768))
+        lane = half % 2 * 128
         upstream_ref = own_ref if half < 2 else next_ref
         upstream = (
             jnp.concatenate(
@@ -187,7 +233,8 @@
         for y in range(2):
             deltas = []
             for ph in range(2):
-                block = conv[(y * 2 + ph) * 64 : (y * 2 + ph) * 64 + 64, :] + bias2
+                row = (y * 2 + ph) * 64
+                block = conv[row : row + 64, lane : lane + 128] + bias2
                 if half < 2:
                     total = total + leaky_relu(block)
                 deltas.append((upstream * slope_mask(block)).astype(BF16).astype(F32))
@@ -200,41 +247,31 @@
         order_ref[pl.ds(u, 16, stride=4), :] = feature[u * 16 : u * 16 + 16, :]
     feature_ref[...] = order_ref[...].astype(BF16)
 
-    ones = jnp.ones((8, 128), BF16)
-    grad2 = None
-    bias_sum2 = None
-    for half in (1, 2):
-        delta = jnp.concatenate(
-            [
-                delta2_ref[half * 512 + 64 : half * 512 + 192, :],
-                delta2_ref[half * 512 + 320 : half * 512 + 448, :],
-            ],
-            axis=0,
-        )
-        term = dot_lanes(delta, pooled_ref[half * 256 : half * 256 + 768, :])
-        bias_term = dot_lanes(ones, delta)
-        grad2 = term if grad2 is None else grad2 + term
-        bias_sum2 = bias_term if bias_sum2 is None else bias_sum2 + bias_term
-
+    ones = jnp.ones((8, 256), BF16)
+    delta = jnp.concatenate(
+        [side_by_side(delta2_ref, 512 + y * 256 + 64, 512, 128) for y in range(2)], axis=0
+    )
+    grad2 = dot_lanes(delta, side_by_side(pooled_ref, 256, 256, 768))
+    bias_sum2 = dot_lanes(ones, delta)
+
+    backs = dot(back_ref[...], side_by_side(delta2_ref, 0, 512, 1536)) * 0.125
     grad1 = None
     bias_sum1 = None
-    for half in (1, 2):
-        back = dot(back_ref[...], delta2_ref[(half - 1) * 512 : (half + 2) * 512, :]) * 0.125
+    for half in range(2):
         for deep in range(2):
-            number = 2 * (half - 1) + deep
             for y in range(4):
                 for r in range(4):
-                    row = number * 512 + (y * 4 + r) * 32
+                    row = (2 * half + deep) * 512 + (y * 4 + r) * 32
                     slot = (y // 2 * 2 + r // 2) * 32
+                    back = backs[slot : slot + 32, half * 128 : half * 128 + 128]
                     delta1_ref[row : row + 32, :] = (
-                        back[slot : slot + 32, :] * slope_mask(pre_ref[row : row + 32, :])
+                        back * slope_mask(pre_ref[row : row + 32, :])
                     ).astype(BF16)
-            delta = delta1_ref[number * 512 : number * 512 + 512, :]
-            at = (number + 4) * 128
-            term = dot_lanes(delta, field_ref[at : at + 384, :])
-            bias_term = dot_lanes(ones, delta)
-            grad1 = term if grad1 is None else grad1 + term
-            bias_sum1 = bias_term if bias_sum1 is None else bias_sum1 + bias_term
+        delta = side_by_side(delta1_ref, half * 1024, 512, 512)
+        term = dot_lanes(delta, side_by_side(field_ref, (2 * half + 4) * 128, 128, 384))
+        bias_term = dot_lanes(ones, delta)
+        grad1 = term if grad1 is None else grad1 + term
+        bias_sum1 = bias_term if bias_sum1 is None else bias_sum1 + bias_term
 
     exact = lax.Precision.HIGHEST
     q = lax.broadcasted_iota(jnp.int32, (512, 128), 0)
@@ -300,27 +337,32 @@
     blocks_ref[459:460, :] = jnp.where(lanes_of((1, 128)) < 32, last[0:1, :], bias_row2[0:1, :])
     blocks_ref[NB:NB_PAD, :] = jnp.zeros((NB_PAD - NB, 128), F32)
 
+
+def owned_kernel(blocks_ref, target_ref, kept_ref, feature_ref, feature_out_ref, owned_ref):
+    feature_out_ref[...] = feature_ref[...]
+    capacity = owned_ref.shape[0]
+    rows = -(-capacity // 16) * 16
     blocks = blocks_ref[...]
     high = blocks.astype(BF16)
     rest = blocks - high.astype(F32)
     middle = rest.astype(BF16)
     low = (rest - middle.astype(F32)).astype(BF16)
-    terms = jnp.concatenate([high, middle, low], axis=1)
-    target = target_ref[...]
-    for tile in range(placed_ref.shape[0] // 128):
-        row_at = lax.broadcasted_iota(jnp.int32, (128, NB_PAD), 0) + tile * 128
-        placing = jnp.where(row_at == target, 1.0, 0.0).astype(BF16)
-        moved = dot(placing, terms)
-        placed_ref[tile * 128 : tile * 128 + 128, :] = (
-            moved[:, 0:128] + moved[:, 128:256] + moved[:, 256:384]
-        )
+    row_at = lax.broadcasted_iota(jnp.int32, (rows, NB_PAD), 0)
+    placing = jnp.where(row_at == target_ref[...], 1.0, 0.0).astype(BF16)
+    moved = dot(placing, jnp.concatenate([high, middle, low], axis=1))
+    total = moved[:, 0:128] + moved[:, 128:256] + moved[:, 256:384]
+    owned_ref[...] = kept_ref[...] + total[0:capacity, :]
 
 
 def whole():
     return pl.BlockSpec(memory_space=pltpu.VMEM)
 
 
-def expand_weights(w1, w2_padded):
+def params():
+    return pltpu.CompilerParams(vmem_limit_bytes=VMEM_LIMIT)
+
+
+def expand_weights(rank, w1, w2, bias1, bias2, owners, accumulated):
     return pl.pallas_call(
         weights_kernel,
         out_shape=(
@@ -328,22 +370,27 @@
             jax.ShapeDtypeStruct((256, 768), BF16),
             jax.ShapeDtypeStruct((128, 1536), BF16),
             jax.ShapeDtypeStruct((512, 768), BF16),
+            jax.ShapeDtypeStruct((32, 128), F32),
+            jax.ShapeDtypeStruct((64, 128), F32),
+            jax.ShapeDtypeStruct((1, NB_PAD), jnp.int32),
+            jax.ShapeDtypeStruct(accumulated.shape, F32),
         ),
-        in_specs=[whole()] * 3,
-        out_specs=(whole(),) * 4,
-        compiler_params=pltpu.CompilerParams(vmem_limit_bytes=VMEM_LIMIT),
+        in_specs=[pl.BlockSpec(memory_space=pltpu.SMEM)] + [whole()] * 7,
+        out_specs=(whole(),) * 8,
+        scratch_shapes=[pltpu.VMEM((64, 896), F32)],
+        compiler_params=params(),
         cost_estimate=pl.CostEstimate(flops=1 << 26, bytes_accessed=4 << 20, transcendentals=0),
-    )(w1, jnp.asarray(tap_selection(), BF16), w2_padded)
-
-
-def forward_backward(packed, weights, bias1, bias2, target, placed_rows):
+    )(rank, w1, jnp.asarray(tap_selection(), BF16), w2, bias1, bias2, owners, accumulated)
+
+
+def forward_backward(spans, weights):
     return pl.pallas_call(
         main_kernel,
         out_shape=(
             jax.ShapeDtypeStruct((64, 128), BF16),
-            jax.ShapeDtypeStruct((placed_rows, 128), F32),
+            jax.ShapeDtypeStruct((NB_PAD, 128), F32),
         ),
-        in_specs=[whole()] * 12,
+        in_specs=[whole()] * 11,
         out_specs=(whole(),) * 2,
         scratch_shapes=[
             pltpu.VMEM((14 * 128, 128), BF16),
@@ -351,80 +398,92 @@
             pltpu.VMEM((4 * 512, 128), BF16),
             pltpu.VMEM((4 * 512, 128), F32),
             pltpu.VMEM((4 * 512, 128), BF16),
-            pltpu.VMEM((NB_PAD, 128), F32),
             pltpu.VMEM((64, 128), F32),
         ],
-        compiler_params=pltpu.CompilerParams(vmem_limit_bytes=VMEM_LIMIT),
+        compiler_params=params(),
         cost_estimate=pl.CostEstimate(flops=1 << 31, bytes_accessed=4 << 20, transcendentals=0),
-    )(
-        *packed,
-        *weights,
-        bias1,
-        bias2,
-        target,
-        jnp.asarray(np.pad(tap_selection().T, ((0, 0), (0, 20))), F32),
-    )
-
-
-def block_targets(owners, ranks, pitch):
-    owner_of = owners[:, 0]
-    member = (owner_of[:, None] == jnp.arange(ranks, dtype=jnp.int32)[None, :]).astype(jnp.int32)
-    before = jnp.cumsum(member, axis=0) - member
-    slot_index = jnp.sum(before * member, axis=1)
-    target = owner_of * pitch + slot_index
-    return jnp.pad(target[None, :], ((0, 0), (0, NB_PAD - NB)), constant_values=-1)
-
-
-def exchange(rows, axis):
-    return lax.all_to_all(rows, axis, 0, 0, tiled=True)
-
-
-def sum_to_owners(placed, ranks, slabs, share):
-    width = placed.shape[1]
-    mine = exchange(placed, "dp").reshape(ranks, -1, width).sum(axis=0)
-    mine = jnp.pad(mine, ((0, slabs * share - mine.shape[0]), (0, 0)))
-    part = exchange(mine, "slab").reshape(slabs, share, width).sum(axis=0)
-    return exchange(jnp.tile(part, (slabs, 1)), "slab")
+    )(*spans, *weights, jnp.asarray(np.pad(tap_selection().T, ((0, 0), (0, 20))), F32))
+
+
+def add_owned(blocks, target, kept, feature):
+    return pl.pallas_call(
+        owned_kernel,
+        out_shape=(
+            jax.ShapeDtypeStruct(feature.shape, feature.dtype),
+            jax.ShapeDtypeStruct(kept.shape, kept.dtype),
+        ),
+        in_specs=[whole()] * 4,
+        out_specs=(whole(),) * 2,
+        compiler_params=params(),
+        cost_estimate=pl.CostEstimate(flops=1 << 27, bytes_accessed=1 << 20, transcendentals=0),
+    )(blocks, target, kept, feature)
+
+
+SLAB = ("z_hi", "y", "core")
+DP = ("z_lo", "x")
+PLANE = ("x", "z_hi", "z_lo")
+REST = ("y", "core")
+
+
+def exchange(rows, axes):
+    return lax.all_to_all(rows, axes, 0, 0, tiled=True)
+
+
+def sum_everywhere(blocks):
+    width = blocks.shape[1]
+    plane, rest = lax.axis_size(PLANE), lax.axis_size(REST)
+    part = exchange(blocks, PLANE).reshape(plane, -1, width).sum(axis=0)
+    part = exchange(jnp.tile(part, (rest, 1)), REST).reshape(rest, -1, width).sum(axis=0)
+    return exchange(jnp.tile(part, (plane, 1)), PLANE)
 
 
 def body(
     universe, cotangent, conv1_weight, conv1_bias, conv2_weight, conv2_bias, owners, accumulated
 ):
-    ranks, slabs = lax.axis_size("dp"), lax.axis_size("slab")
+    slabs = lax.axis_size(SLAB)
     packed = jnp.concatenate(
         [universe[0].transpose(1, 0, 2, 3).reshape(64, 512), cotangent.reshape(16, 512)], axis=0
     )
 
     def from_slab(distance):
         pairs = [(i, (i - distance) % slabs) for i in range(slabs)]
-        return lax.ppermute(packed, "slab", pairs)
+        return lax.ppermute(packed, SLAB, pairs)
 
     spans = (from_slab(-1), packed, from_slab(1), from_slab(2))
-    w2 = conv2_weight.reshape(16, 4, 864).transpose(1, 0, 2).reshape(64, 864)
-    weights = expand_weights(conv1_weight, jnp.pad(w2, ((0, 0), (0, 32))))
-    bias2 = conv2_bias.reshape(16, 4).T.reshape(64, 1)
-    capacity = accumulated.shape[0]
-    step = max(16, 128 // ranks)
-    pitch = -(-capacity // step) * step
-    target = block_targets(owners, ranks, pitch)
-    feature, placed = forward_backward(
-        spans, weights, conv1_bias.reshape(32, 1), bias2, target, ranks * pitch
-    )
-    totals = sum_to_owners(placed, ranks, slabs, -(-pitch // slabs))
-    owned = accumulated + totals[:capacity]
+    *weights, target, kept = expand_weights(
+        lax.axis_index(DP).reshape(1),
+        conv1_weight,
+        conv2_weight,
+        conv1_bias.reshape(1, 32),
+        conv2_bias.reshape(1, 64),
+        owners.reshape(1, NB),
+        accumulated,
+    )
+    feature, blocks = forward_backward(spans, weights)
+    feature, owned = add_owned(sum_everywhere(blocks), target, kept, feature)
     return (feature.reshape(1, 64, 1, 1, 128), owned)
+
+
+def split_mesh(mesh):
+    slabs, ranks = mesh.devices.shape
+    x = min(4, ranks)
+    y = min(8, slabs // 2)
+    shape = (slabs // (2 * y), y, 2, ranks // x, x)
+    return Mesh(mesh.devices.reshape(shape), SLAB + DP)
 
 
 def solution(mesh):
     in_specs = (
-        P("dp", None, "slab", None, None),
-        P("dp", None, "slab", None, None),
+        P(DP, None, SLAB, None, None),
+        P(DP, None, SLAB, None, None),
         P(),
         P(),
         P(),
         P(),
         P(),
-        P("dp", None),
-    )
-    out_specs = (P("dp", None, "slab", None, None), P("dp", None))
-    return jax.shard_map(body, mesh=mesh, in_specs=in_specs, out_specs=out_specs, check_vma=False)
+        P(DP, None),
+    )
+    out_specs = (P(DP, None, SLAB, None, None), P(DP, None))
+    return jax.shard_map(
+        body, mesh=split_mesh(mesh), in_specs=in_specs, out_specs=out_specs, check_vma=False
+    )

time: 86 us -> 79 us (0.919)
  the two profiles are of different devices: /device:TPU:1 before, /device:TPU:64 now
where the time goes in v3:
time: 79 us; the launch traced here: 78.6 us
  blocking collectives  45.4 us (57%)
  starting transfers between devices  17.4 us (22%)
  waiting for transfers between devices  7.16 us (9%)
  Pallas kernels  5.32 us (7%)
  local copies, waits for them, and re-layouts  2.38 us (3%)
  between operations  0.82 us (1%)
    all_to_all x3, blocking collectives, exchange(): return lax.all_to_all(rows, axes, 0, 0, tiled=True)  45.4 us
    ppermute x3, starting transfers between devices, from_slab(): return lax.ppermute(packed, SLAB, pairs)  17.4 us
    ppermute x3, waiting for transfers between devices, from_slab(): return lax.ppermute(packed, SLAB, pairs)  7.16 us
    pallas_call x1, Pallas kernels, forward_backward(): pl.pallas_call(main_kernel, out_shape=(jax.ShapeDtypeStruct((64, 128), BF...  3.49 us
  transfers between devices with their start and end apart: 3, of which 1 were waited for; matrix products, arithmetic and copies ran while one was open for 0% of the time, Pallas kernels for 1%

profile of v3, /device:TPU:64, one launch (start us, length us, event | category | flops | bytes accessed | tf_op | source)
XLA Modules:
  0.0 78.6 jit_solution(1688296244238783277)
XLA Ops:
  0.6 0.0 copy-start.7
  0.6 0.8 reshape.46
  1.4 0.9 %copy.13 = bf16[4,4,4,512]{3,2,1,0:T(4,128)(2,1)S(1)} copy(bf16[4,4,4,512]{3,2,0,1:T(4,128)(2,1)} %bitcast.19) | data formatting | bytes 131072 | tf_op jit(solution)/shard_map/transpose | solution.py:445
  2.3 0.0 copy-start.1
  2.3 0.0 copy-start.2
  2.3 0.0 copy-start
  2.4 13.1 %collective-permute-start.2 = (bf16[80,512]{1,0:T(8,128)(2,1)S(1)}, bf16[80,512]{1,0:T(8,128)(2,1)S(1)}, u32[]{:S(2)}, u32[]{:S(2)}) collective-permute-start(bf16[80,512]{1,0:T(8,128)(2,1)S(1)} %constant_dynamic-update-slice_fusion.own_ref), channel_id=1, source_target_pairs={{0,496},{8,504},{16,0},{24,8},{32,16},{40,24},{48,32},{56,40},{64,... | collective-permute-start | bytes 245768 | tf_op jit(solution)/shard_map/ppermute | solution.py:450
  15.5 2.4 %collective-permute-start.1 = (bf16[80,512]{1,0:T(8,128)(2,1)S(1)}, bf16[80,512]{1,0:T(8,128)(2,1)S(1)}, u32[]{:S(2)}, u32[]{:S(2)}) collective-permute-start(bf16[80,512]{1,0:T(8,128)(2,1)S(1)} %constant_dynamic-update-slice_fusion.own_ref), channel_id=1, source_target_pairs={{0,504},{8,0},{16,8},{24,16},{32,24},{40,32},{48,40},{56,48},{64,5... | collective-permute-start | bytes 245768 | tf_op jit(solution)/shard_map/ppermute | solution.py:450
  17.9 1.9 %collective-permute-start = (bf16[80,512]{1,0:T(8,128)(2,1)S(1)}, bf16[80,512]{1,0:T(8,128)(2,1)S(1)}, u32[]{:S(2)}, u32[]{:S(2)}) collective-permute-start(bf16[80,512]{1,0:T(8,128)(2,1)S(1)} %constant_dynamic-update-slice_fusion.own_ref), channel_id=1, source_target_pairs={{0,8},{8,16},{16,24},{24,32},{32,40},{40,48},{48,56},{56,64},{64,7... | collective-permute-start | bytes 245768 | tf_op jit(solution)/shard_map/ppermute | solution.py:450
  19.8 0.0 copy-start.3
  19.8 0.0 copy-start.4
  19.8 0.0 copy-start.5
  19.9 0.0 copy-start.6
  19.9 0.6 copy-done.3
  20.5 0.0 copy-done.6
  20.5 0.9 %shard_map.113 = (bf16[512,384]{1,0:T(8,128)(2,1)S(1)}, bf16[256,768]{1,0:T(8,128)(2,1)S(1)}, bf16[128,1536]{1,0:T(8,128)(2,1)S(1)}, bf16[512,768]{1,0:T(8,128)(...) custom-call(s32[1]{0:T(128)} %bitcast.2.rank_ref, ...), custom_call_target="tpu_custom_call" | custom-call | flops 67108864 | bytes 4194304 | tf_op jit(solution)/shard_map/pallas_call | solution.py:366
  21.5 0.0 collective-permute-done.2.after_ref
  21.5 0.0 collective-permute-done.1.next_ref
  21.5 7.2 %collective-permute-done.prev_ref = bf16[80,512]{1,0:T(8,128)(2,1)S(1)} collective-permute-done((bf16[80,512]{1,0:T(8,128)(2,1)S(1)}, bf16[80,512]{1,0:T(8,128)(2,1)S(1)}, u32[]{:S(2)}, u32[]{:S(2)}) %collective-permute-start) | collective-permute-done | bytes 81952 | tf_op jit(solution)/shard_map/ppermute | solution.py:450
  28.6 3.5 %shard_map.114 = (bf16[64,128]{1,0:T(8,128)(2,1)S(1)}, f32[512,128]{1,0:T(8,128)S(1)}) custom-call(bf16[80,512]{1,0:T(8,128)(2,1)S(1)} %collective-permute-done.prev_ref, bf16[80,512]{1,0:T(8,128)(2,1)S(1)} %constant_dynamic-update-slice_fusion.own_ref, bf16[80,512]{1,0:T(8,128)(2,1)S(1)} %collective-permute-done.1.next_ref, ...), custom_call_target="tpu_custom_call" | custom-call | flops 2147483648 | bytes 4194304 | tf_op jit(solution)/shard_map/pallas_call | solution.py:387
  32.1 16.7 %all_to_all.23 = f32[32,16,128]{2,1,0:T(8,128)S(1)} all-to-all(f32[32,16,128]{2,1,0:T(8,128)S(1)} %bitcast.14), channel_id=1, replica_groups=mesh['z_hi'=4,'y'=8,'core'=2,'z_lo'=2,'x'=4] {'x','z_hi','z_lo'}, dimensions={0} | all-to-all | bytes 524288 | tf_op jit(solution)/shard_map/all_to_all | solution.py:429
  48.9 11.3 %all_to_all.24 = f32[16,16,128]{2,1,0:T(8,128)S(1)} all-to-all(f32[16,16,128]{2,1,0:T(8,128)S(1)} %tile.4), channel_id=1, replica_groups=mesh['z_hi'=4,'y'=8,'core'=2,'z_lo'=2,'x'=4] {'y','core'}, dimensions={0} | all-to-all | bytes 262144 | tf_op jit(solution)/shard_map/all_to_all | solution.py:429
  60.3 17.4 %all_to_all.25 = f32[32,16,128]{2,1,0:T(8,128)S(1)} all-to-all(f32[32,16,128]{2,1,0:T(8,128)S(1)} %tile.5), channel_id=1, replica_groups=mesh['z_hi'=4,'y'=8,'core'=2,'z_lo'=2,'x'=4] {'x','z_hi','z_lo'}, dimensions={0} | all-to-all | bytes 524288 | tf_op jit(solution)/shard_map/all_to_all | solution.py:429
  77.7 0.9 %shard_map.115 = (bf16[64,128]{1,0:T(8,128)(2,1)}, f32[138,128]{1,0:T(8,128)}) custom-call(f32[512,128]{1,0:T(8,128)S(1)} %bitcast.15, s32[1,512]{1,0:T(1,128)S(1)} %get-tuple-element.21.target_ref, f32[138,128]{1,0:T(8,128)S(1)} %get-tuple-element.22.kept_ref, bf16[64,128]{1,0:T(8,128)(2,1)S(1)} %get-tuple-element.23.feature_ref), custom_call_target="tpu_custom_call" | custom-call | flops 134217728 | bytes 1048576 | tf_op jit(solution)/shard_map/pallas_call | solution.py:409
  (13 shorter events, 0.1 us)
Async XLA Ops:
  0.6 28.0 %copy-start.7 = (f32[384,128]{1,0:T(8,128)S(1)}, f32[384,128]{1,0:T(8,128)}, u32[]{:S(2)}) copy-start(f32[384,128]{1,0:T(8,128)} %constant.18.clone.select_ref) | copy-start | bytes 589828
  2.3 17.6 %copy-start.1 = (bf16[108,384]{1,0:T(8,128)(2,1)S(1)}, bf16[108,384]{1,0:T(8,128)(2,1)}, u32[]{:S(2)}) copy-start(bf16[108,384]{1,0:T(8,128)(2,1)} %constant.17.clone.select_ref) | copy-start | bytes 248836
  2.3 17.6 %copy-start.2 = (f32[138,128]{1,0:T(8,128)S(1)}, f32[138,128]{1,0:T(8,128)}, u32[]{:S(2)}) copy-start(f32[138,128]{1,0:T(8,128)} %accumulated_ref.1) | copy-start | bytes 211972
  2.3 17.6 %copy-start = (bf16[64,864]{1,0:T(8,128)(2,1)S(1)}, bf16[64,864]{1,0:T(8,128)(2,1)}, u32[]{:S(2)}) copy-start(bf16[64,864]{1,0:T(8,128)(2,1)} %w2_ref.1) | copy-start | bytes 331780
  2.4 19.1 %collective-permute-start.2 = (bf16[80,512]{1,0:T(8,128)(2,1)S(1)}, bf16[80,512]{1,0:T(8,128)(2,1)S(1)}, u32[]{:S(2)}, u32[]{:S(2)}) collective-permute-start(bf16[80,512]{1,0:T(8,128)(2,1)S(1)} %constant_dynamic-update-slice_fusion.own_ref), channel_id=1, source_target_pairs={{0,496},{8,504},{16,0},{24,8},{32,16},{40,24},{48,32},{56,40},{64,... | collective-permute-start | bytes 245768 | tf_op jit(solution)/shard_map/ppermute | solution.py:450
  15.5 6.0 %collective-permute-start.1 = (bf16[80,512]{1,0:T(8,128)(2,1)S(1)}, bf16[80,512]{1,0:T(8,128)(2,1)S(1)}, u32[]{:S(2)}, u32[]{:S(2)}) collective-permute-start(bf16[80,512]{1,0:T(8,128)(2,1)S(1)} %constant_dynamic-update-slice_fusion.own_ref), channel_id=1, source_target_pairs={{0,504},{8,0},{16,8},{24,16},{32,24},{40,32},{48,40},{56,48},{64,5... | collective-permute-start | bytes 245768 | tf_op jit(solution)/shard_map/ppermute | solution.py:450
  17.9 10.8 %collective-permute-start = (bf16[80,512]{1,0:T(8,128)(2,1)S(1)}, bf16[80,512]{1,0:T(8,128)(2,1)S(1)}, u32[]{:S(2)}, u32[]{:S(2)}) collective-permute-start(bf16[80,512]{1,0:T(8,128)(2,1)S(1)} %constant_dynamic-update-slice_fusion.own_ref), channel_id=1, source_target_pairs={{0,8},{8,16},{16,24},{24,32},{32,40},{40,48},{48,56},{56,64},{64,7... | collective-permute-start | bytes 245768 | tf_op jit(solution)/shard_map/ppermute | solution.py:450
  19.8 0.7 copy-start.3
  19.8 0.7 copy-start.4
  19.8 0.7 copy-start.5
  19.9 0.7 copy-start.6

commit v4 on v3

--- a/solution.py
+++ b/solution.py
@@ -16,13 +16,14 @@
 
 
 def tap_selection():
-    select = np.zeros((108, 384), np.float32)
+    select = np.zeros((108, 256), np.float32)
     for first in range(3):
         for second in range(3):
             for third in range(3):
                 for chan in range(4):
-                    lane = (third * 16 + chan * 4 + second - 1) % 128
-                    select[(9 * first + 3 * second + third) * 4 + chan, first * 128 + lane] = 1.0
+                    lane = (first % 2 * 64 + third * 16 + chan * 4 + second - 1) % 128
+                    row = (9 * first + 3 * second + third) * 4 + chan
+                    select[row, first // 2 * 128 + lane] = 1.0
     return select
 
 
@@ -66,6 +67,30 @@
 def channel_order():
     row = lax.broadcasted_iota(jnp.int32, (64, 64), 0)
     return jnp.where(lanes_of((64, 64)) == 4 * (row % 16) + row // 16, 1.0, 0.0)
+
+
+def pack_kernel(
+    universe_hbm, cotangent_hbm, own_ref, late_ref, early_ref, universe_ref, cotangent_ref, sems
+):
+    first = pltpu.make_async_copy(universe_hbm, universe_ref, sems.at[0])
+    second = pltpu.make_async_copy(cotangent_hbm, cotangent_ref, sems.at[1])
+    first.start()
+    second.start()
+    first.wait()
+    for deep in range(4):
+        rows = jnp.concatenate(
+            [universe_ref[0, chan, deep].astype(F32) for chan in range(4)], axis=0
+        ).astype(BF16)
+        own_ref[deep * 16 : deep * 16 + 16, :] = rows
+        if deep > 0:
+            late_ref[deep * 16 - 16 : deep * 16, :] = rows
+        if deep < 3:
+            early_ref[deep * 16 : deep * 16 + 16, :] = rows
+    second.wait()
+    for group in range(4):
+        own_ref[64:80, group * 128 : group * 128 + 128] = cotangent_ref[
+            group * 16 : group * 16 + 16, :
+        ]
 
 
 def weights_kernel(
@@ -107,12 +132,12 @@
     y_of = lanes_of((32, 128)) % 4
     for y in range(4):
         near = jnp.abs(y_of - y) <= 1
-        for r in range(4):
-            for first in range(3):
-                part = turned(base[:, first * 128 : first * 128 + 128], r * 16 + y)
-                big1_ref[(y * 4 + r) * 32 : (y * 4 + r) * 32 + 32, first * 128 : first * 128 + 128] = (
-                    jnp.where(near, part, 0.0).astype(BF16)
-                )
+        for r in range(2):
+            for at in (0, 128):
+                part = turned(base[:, at : at + 128], r * 16 + y)
+                big1_ref[(y * 2 + r) * 32 : (y * 2 + r) * 32 + 32, at : at + 128] = jnp.where(
+                    near, part, 0.0
+                ).astype(BF16)
     group = lanes_of((64, 128)) // 32
 
     def gathered(taps):
@@ -182,36 +207,42 @@
     order_ref,
 ):
     source = jnp.concatenate(
-        [prev_ref[16:64, :], own_ref[0:64, :], next_ref[0:64, :], after_ref[0:48, :]], axis=0
-    )
-    for layer in range(14):
-        field_ref[layer * 128 + 96 : layer * 128 + 128, :] = jnp.zeros((32, 128), BF16)
+        [prev_ref[...], own_ref[0:64, :], next_ref[0:64, :], after_ref[...]], axis=0
+    )
     for col in range(6):
         part = dot(source, comb_ref[:, col * 128 : col * 128 + 128]).astype(BF16)
         for layer in range(14):
-            at = layer * 128 + col * 16
+            at = layer * 96 + col * 16
             field_ref[at : at + 16, :] = part[layer * 16 : layer * 16 + 16, :]
+    empty = jnp.zeros((64, 128), BF16)
+
+    def around(half):
+        parts = []
+        for deep in range(2):
+            for pair in range(2):
+                at = (2 * half + deep) * 96 + pair * 32
+                layers = [field_ref[at + first * 96 : at + first * 96 + 64, :] for first in range(3)]
+                parts.append(jnp.concatenate(layers + [empty], axis=0))
+        return jnp.concatenate(parts, axis=1)
 
     bias1 = wide1_ref[...]
     for half in range(6):
-        sums = [None] * 4
-        conv = dot(big1_ref[...], side_by_side(field_ref, 2 * half * 128, 128, 384))
-        for deep in range(2):
-            for y in range(4):
-                for r in range(4):
-                    block = (
-                        conv[(y * 4 + r) * 32 : (y * 4 + r) * 32 + 32, deep * 128 : deep * 128 + 128]
-                        + bias1
-                    )
-                    if half in (2, 3):
-                        row = (2 * (half - 2) + deep) * 512 + (y * 4 + r) * 32
-                        pre_ref[row : row + 32, :] = block
-                    value = leaky_relu(block)
-                    slot = y // 2 * 2 + r // 2
-                    sums[slot] = value if sums[slot] is None else sums[slot] + value
+        conv = dot(big1_ref[...], around(half))
         for y in range(2):
-            even = (sums[2 * y] * 0.125).astype(BF16).astype(F32)
-            odd = (sums[2 * y + 1] * 0.125).astype(BF16).astype(F32)
+            means = []
+            for pair in range(2):
+                total = None
+                for deep in range(2):
+                    lane = (deep * 2 + pair) * 128
+                    for row in range(y * 128, y * 128 + 128, 32):
+                        block = conv[row : row + 32, lane : lane + 128] + bias1
+                        if half in (2, 3):
+                            at = (half - 2) * 256 + row
+                            pre_ref[at : at + 32, lane : lane + 128] = block
+                        value = leaky_relu(block)
+                        total = value if total is None else total + value
+                means.append((total * 0.125).astype(BF16).astype(F32))
+            even, odd = means
             at = half * 256 + y * 128
             pooled_ref[at : at + 128, :] = jnp.concatenate(
                 [from_left(odd), even, odd, from_right(even)], axis=0
@@ -219,17 +250,19 @@
 
     bias2 = wide2_ref[...]
     total = jnp.zeros((64, 128), F32)
+    plain = jnp.concatenate(
+        [
+            jnp.concatenate([ref[64:80, g * 128 : g * 128 + 128] for g in range(4)], axis=0)
+            for ref in (own_ref, next_ref)
+        ],
+        axis=1,
+    )
+    upstreams = dot(channel_order().astype(BF16), plain) * 0.125
     for half in range(4):
         if half % 2 == 0:
             conv = dot(big2_ref[...], side_by_side(pooled_ref, half * 256, 256, 768))
         lane = half % 2 * 128
-        upstream_ref = own_ref if half < 2 else next_ref
-        upstream = (
-            jnp.concatenate(
-                [upstream_ref[64:80, u * 128 : u * 128 + 128] for u in range(4)], axis=0
-            ).astype(F32)
-            * 0.125
-        )
+        upstream = upstreams[:, half // 2 * 128 : half // 2 * 128 + 128]
         for y in range(2):
             deltas = []
             for ph in range(2):
@@ -255,40 +288,47 @@
     bias_sum2 = dot_lanes(ones, delta)
 
     backs = dot(back_ref[...], side_by_side(delta2_ref, 0, 512, 1536)) * 0.125
+    ones = jnp.ones((8, 512), BF16)
     grad1 = None
     bias_sum1 = None
     for half in range(2):
         for deep in range(2):
-            for y in range(4):
-                for r in range(4):
-                    row = (2 * half + deep) * 512 + (y * 4 + r) * 32
-                    slot = (y // 2 * 2 + r // 2) * 32
+            for pair in range(2):
+                lane = (deep * 2 + pair) * 128
+                for row in range(0, 256, 32):
+                    slot = (row // 128 * 2 + pair) * 32
                     back = backs[slot : slot + 32, half * 128 : half * 128 + 128]
-                    delta1_ref[row : row + 32, :] = (
-                        back * slope_mask(pre_ref[row : row + 32, :])
+                    at = half * 256 + row
+                    delta1_ref[at : at + 32, lane : lane + 128] = (
+                        back * slope_mask(pre_ref[at : at + 32, lane : lane + 128])
                     ).astype(BF16)
-        delta = side_by_side(delta1_ref, half * 1024, 512, 512)
-        term = dot_lanes(delta, side_by_side(field_ref, (2 * half + 4) * 128, 128, 384))
+        delta = delta1_ref[half * 256 : half * 256 + 256, :]
+        term = dot_lanes(delta, around(half + 2))
         bias_term = dot_lanes(ones, delta)
         grad1 = term if grad1 is None else grad1 + term
         bias_sum1 = bias_term if bias_sum1 is None else bias_sum1 + bias_term
 
     exact = lax.Precision.HIGHEST
-    q = lax.broadcasted_iota(jnp.int32, (512, 128), 0)
-    bias_row1 = dot(bias_sum1, jnp.where(q % 32 == lanes_of((512, 128)), 1.0, 0.0), exact)
-    q = lax.broadcasted_iota(jnp.int32, (256, 128), 0)
+    bias_row1 = bias_sum1[:, 0:128] + bias_sum1[:, 128:256]
+    bias_row1 = bias_row1 + turned(bias_row1, 64)
+    bias_row1 = bias_row1 + turned(bias_row1, 32)
+    q = lax.broadcasted_iota(jnp.int32, (128, 128), 0)
     lane = 32 + 4 * (q % 16) + q % 64 // 16
-    bias_row2 = dot(bias_sum2, jnp.where(lane == lanes_of((256, 128)), 1.0, 0.0), exact)
+    bias_row2 = dot(
+        bias_sum2[:, 0:128] + bias_sum2[:, 128:256],
+        jnp.where(lane == lanes_of((128, 128)), 1.0, 0.0),
+        exact,
+    )
 
     y_of = lanes_of((32, 128)) % 4
     parts = []
-    for first in range(3):
+    for at in (0, 128):
         part = jnp.zeros((32, 128), F32)
         for y in range(4):
             near = jnp.abs(y_of - y) <= 1
-            for r in range(4):
-                row = (y * 4 + r) * 32
-                block = grad1[row : row + 32, first * 128 : first * 128 + 128]
+            for r in range(2):
+                row = (y * 2 + r) * 32
+                block = grad1[row : row + 32, at : at + 128]
                 part = part + turned(jnp.where(near, block, 0.0), -(r * 16 + y))
         parts.append(part)
     flat1 = dot(jnp.concatenate(parts, axis=1), select_ref[...], exact)
@@ -362,11 +402,31 @@
     return pltpu.CompilerParams(vmem_limit_bytes=VMEM_LIMIT)
 
 
+def pack(universe, cotangent):
+    return pl.pallas_call(
+        pack_kernel,
+        out_shape=(
+            jax.ShapeDtypeStruct((80, 512), BF16),
+            jax.ShapeDtypeStruct((48, 512), BF16),
+            jax.ShapeDtypeStruct((48, 512), BF16),
+        ),
+        in_specs=[pl.BlockSpec(memory_space=pltpu.HBM)] * 2,
+        out_specs=(whole(),) * 3,
+        scratch_shapes=[
+            pltpu.VMEM(universe.shape, BF16),
+            pltpu.VMEM(cotangent.shape, BF16),
+            pltpu.SemaphoreType.DMA((2,)),
+        ],
+        compiler_params=params(),
+        cost_estimate=pl.CostEstimate(flops=1 << 16, bytes_accessed=1 << 18, transcendentals=0),
+    )(universe, cotangent)
+
+
 def expand_weights(rank, w1, w2, bias1, bias2, owners, accumulated):
     return pl.pallas_call(
         weights_kernel,
         out_shape=(
-            jax.ShapeDtypeStruct((512, 384), BF16),
+            jax.ShapeDtypeStruct((256, 256), BF16),
             jax.ShapeDtypeStruct((256, 768), BF16),
             jax.ShapeDtypeStruct((128, 1536), BF16),
             jax.ShapeDtypeStruct((512, 768), BF16),
@@ -393,11 +453,11 @@
         in_specs=[whole()] * 11,
         out_specs=(whole(),) * 2,
         scratch_shapes=[
-            pltpu.VMEM((14 * 128, 128), BF16),
+            pltpu.VMEM((14 * 96, 128), BF16),
             pltpu.VMEM((6 * 256, 128), BF16),
             pltpu.VMEM((4 * 512, 128), BF16),
-            pltpu.VMEM((4 * 512, 128), F32),
-            pltpu.VMEM((4 * 512, 128), BF16),
+            pltpu.VMEM((2 * 256, 512), F32),
+            pltpu.VMEM((2 * 256, 512), BF16),
             pltpu.VMEM((64, 128), F32),
         ],
         compiler_params=params(),
@@ -422,7 +482,7 @@
 SLAB = ("z_hi", "y", "core")
 DP = ("z_lo", "x")
 PLANE = ("x", "z_hi", "z_lo")
-REST = ("y", "core")
+REST = ("core", "y")
 
 
 def exchange(rows, axes):
@@ -441,15 +501,13 @@
     universe, cotangent, conv1_weight, conv1_bias, conv2_weight, conv2_bias, owners, accumulated
 ):
     slabs = lax.axis_size(SLAB)
-    packed = jnp.concatenate(
-        [universe[0].transpose(1, 0, 2, 3).reshape(64, 512), cotangent.reshape(16, 512)], axis=0
-    )
-
-    def from_slab(distance):
+    packed, late, early = pack(universe, cotangent.reshape(64, 128))
+
+    def from_slab(distance, rows):
         pairs = [(i, (i - distance) % slabs) for i in range(slabs)]
-        return lax.ppermute(packed, SLAB, pairs)
-
-    spans = (from_slab(-1), packed, from_slab(1), from_slab(2))
+        return lax.ppermute(rows, SLAB, pairs)
+
+    spans = (from_slab(-1, late), packed, from_slab(1, packed), from_slab(2, early))
     *weights, target, kept = expand_weights(
         lax.axis_index(DP).reshape(1),
         conv1_weight,

time: 79 us -> 77.2 us (0.977)
  the two profiles are of different devices: /device:TPU:64 before, /device:TPU:8 now
where the time goes in v4:
time: 77.2 us; the launch traced here: 76.7 us
  blocking collectives  49.4 us (64%)
  starting transfers between devices  17.6 us (23%)
  Pallas kernels  4.85 us (6%)
  local copies, waits for them, and re-layouts  4.01 us (5%)
  between operations  0.79 us (1%)
    all_to_all x3, blocking collectives, exchange(): return lax.all_to_all(rows, axes, 0, 0, tiled=True)  49.4 us
    ppermute x3, starting transfers between devices, from_slab(): return lax.ppermute(rows, SLAB, pairs)  17.6 us
    unnamed x20, local copies, waits for them, and re-layouts  3.98 us
    pallas_call x1, Pallas kernels, forward_backward(): pl.pallas_call(main_kernel, out_shape=(jax.ShapeDtypeStruct((64, 128), BF...  2.98 us
  transfers between devices with their start and end apart: 3, of which 0 were waited for; matrix products, arithmetic and copies ran while one was open for 0% of the time, Pallas kernels for 1%

profile of v4, /device:TPU:8, one launch (start us, length us, event | category | flops | bytes accessed | tf_op | source)
XLA Modules:
  0.0 76.7 jit_solution(13102526469568626321)
XLA Ops:
  0.6 0.9 %copy-done.2 = bf16[1,4,4,4,512]{4,3,2,1,0:T(4,128)(2,1)S(1)} copy-done((bf16[1,4,4,4,512]{4,3,2,1,0:T(4,128)(2,1)S(1)}, bf16[1,4,4,4,512]{4,3,2,1,0:T(4,128)(2,1)}, u32[]{:S(2)}) %copy-start.2) | copy-done | bytes 65560
  1.5 0.7 copy-done.4
  2.2 0.1 shard_map.113
  2.3 1.9 %collective-permute-start.1 = (bf16[80,512]{1,0:T(8,128)(2,1)S(1)}, bf16[80,512]{1,0:T(8,128)(2,1)S(1)}, u32[]{:S(2)}, u32[]{:S(2)}) collective-permute-start(bf16[80,512]{1,0:T(8,128)(2,1)S(1)} %get-tuple-element.18.own_ref), channel_id=1, source_target_pairs={{0,504},{8,0},{16,8},{24,16},{32,24},{40,32},{48,40},{56,48},{64,5... | collective-permute-start | bytes 245768 | tf_op jit(solution)/shard_map/ppermute | solution.py:508
  4.3 2.4 %collective-permute-start = (bf16[48,512]{1,0:T(8,128)(2,1)S(1)}, bf16[48,512]{1,0:T(8,128)(2,1)S(1)}, u32[]{:S(2)}, u32[]{:S(2)}) collective-permute-start(bf16[48,512]{1,0:T(8,128)(2,1)S(1)} %get-tuple-element.17), channel_id=1, source_target_pairs={{0,8},{8,16},{16,24},{24,32},{32,40},{40,48},{48,56},{56,64},{64,7... | collective-permute-start | bytes 147464 | tf_op jit(solution)/shard_map/ppermute | solution.py:508
  6.7 13.2 %collective-permute-start.2 = (bf16[48,512]{1,0:T(8,128)(2,1)S(1)}, bf16[48,512]{1,0:T(8,128)(2,1)S(1)}, u32[]{:S(2)}, u32[]{:S(2)}) collective-permute-start(bf16[48,512]{1,0:T(8,128)(2,1)S(1)} %get-tuple-element.19), channel_id=1, source_target_pairs={{0,496},{8,504},{16,0},{24,8},{32,16},{40,24},{48,32},{56,40},{64,... | collective-permute-start | bytes 147464 | tf_op jit(solution)/shard_map/ppermute | solution.py:508
  19.9 0.0 copy-start.5
  20.0 0.0 copy-start.6
  20.0 0.0 copy-start.7
  20.0 0.0 copy-start.8
  20.0 0.6 copy-done.5
  20.6 0.0 copy-done.6
  20.7 0.9 %copy-done = bf16[64,864]{1,0:T(8,128)(2,1)S(1)} copy-done((bf16[64,864]{1,0:T(8,128)(2,1)S(1)}, bf16[64,864]{1,0:T(8,128)(2,1)}, u32[]{:S(2)}) %copy-start) | copy-done | bytes 110616
  21.5 0.8 %copy-done.3 = bf16[108,256]{1,0:T(8,128)(2,1)S(1)} copy-done((bf16[108,256]{1,0:T(8,128)(2,1)S(1)}, bf16[108,256]{1,0:T(8,128)(2,1)}, u32[]{:S(2)}) %copy-start.3) | copy-done | bytes 55320
  22.4 0.8 %shard_map.114 = (bf16[256,256]{1,0:T(8,128)(2,1)S(1)}, bf16[256,768]{1,0:T(8,128)(2,1)S(1)}, bf16[128,1536]{1,0:T(8,128)(2,1)S(1)}, bf16[512,768]{1,0:T(8,128)(...) custom-call(s32[1]{0:T(128)} %bitcast.1.rank_ref, ...), custom_call_target="tpu_custom_call" | custom-call | flops 67108864 | bytes 4194304 | tf_op jit(solution)/shard_map/pallas_call | solution.py:426
  23.2 0.0 collective-permute-done.prev_ref
  23.2 0.0 collective-permute-done.2.after_ref
  23.2 0.0 collective-permute-done.1.next_ref
  23.3 0.0 copy-done.9
  23.3 3.0 %shard_map.115 = (bf16[64,128]{1,0:T(8,128)(2,1)S(1)}, f32[512,128]{1,0:T(8,128)S(1)}) custom-call(bf16[48,512]{1,0:T(8,128)(2,1)S(1)} %collective-permute-done.prev_ref, bf16[80,512]{1,0:T(8,128)(2,1)S(1)} %get-tuple-element.18.own_ref, bf16[80,512]{1,0:T(8,128)(2,1)S(1)} %collective-permute-done.1.next_ref, ...), custom_call_target="tpu_custom_call" | custom-call | flops 2147483648 | bytes 4194304 | tf_op jit(solution)/shard_map/pallas_call | solution.py:447
  26.3 16.4 %all_to_all.23 = f32[32,16,128]{2,1,0:T(8,128)S(1)} all-to-all(f32[32,16,128]{2,1,0:T(8,128)S(1)} %bitcast.8), channel_id=1, replica_groups=mesh['z_hi'=4,'y'=8,'core'=2,'z_lo'=2,'x'=4] {'x','z_hi','z_lo'}, dimensions={0} | all-to-all | bytes 524288 | tf_op jit(solution)/shard_map/all_to_all | solution.py:489
  42.7 17.0 %all_to_all.24 = f32[16,16,128]{2,1,0:T(8,128)S(1)} all-to-all(f32[16,16,128]{2,1,0:T(8,128)S(1)} %tile.4), channel_id=1, replica_groups=mesh['z_hi'=4,'y'=8,'core'=2,'z_lo'=2,'x'=4] {'core','y'}, dimensions={0} | all-to-all | bytes 262144 | tf_op jit(solution)/shard_map/all_to_all | solution.py:489
  59.8 16.0 %all_to_all.25 = f32[32,16,128]{2,1,0:T(8,128)S(1)} all-to-all(f32[32,16,128]{2,1,0:T(8,128)S(1)} %tile.5), channel_id=1, replica_groups=mesh['z_hi'=4,'y'=8,'core'=2,'z_lo'=2,'x'=4] {'x','z_hi','z_lo'}, dimensions={0} | all-to-all | bytes 524288 | tf_op jit(solution)/shard_map/all_to_all | solution.py:489
  75.8 0.9 %shard_map.116 = (bf16[64,128]{1,0:T(8,128)(2,1)}, f32[138,128]{1,0:T(8,128)}) custom-call(f32[512,128]{1,0:T(8,128)S(1)} %bitcast.9, s32[1,512]{1,0:T(1,128)S(1)} %get-tuple-element.27.target_ref, f32[138,128]{1,0:T(8,128)S(1)} %get-tuple-element.28.kept_ref, bf16[64,128]{1,0:T(8,128)(2,1)S(1)} %get-tuple-element.29.feature_ref), custom_call_target="tpu_custom_call" | custom-call | flops 134217728 | bytes 1048576 | tf_op jit(solution)/shard_map/pallas_call | solution.py:469
  (13 shorter events, 0.1 us)
Async XLA Ops:
  0.6 19.4 %copy-start.1 = (f32[138,128]{1,0:T(8,128)S(1)}, f32[138,128]{1,0:T(8,128)}, u32[]{:S(2)}) copy-start(f32[138,128]{1,0:T(8,128)} %accumulated_ref.1) | copy-start | bytes 211972
  0.6 0.9 %copy-start.2 = (bf16[1,4,4,4,512]{4,3,2,1,0:T(4,128)(2,1)S(1)}, bf16[1,4,4,4,512]{4,3,2,1,0:T(4,128)(2,1)}, u32[]{:S(2)}) copy-start(bf16[1,4,4,4,512]{4,3,2,1,0:T(4,128)(2,1)} %universe_hbm.1) | copy-start | bytes 196612
  1.5 0.7 copy-start.4
  2.3 20.9 %collective-permute-start.1 = (bf16[80,512]{1,0:T(8,128)(2,1)S(1)}, bf16[80,512]{1,0:T(8,128)(2,1)S(1)}, u32[]{:S(2)}, u32[]{:S(2)}) collective-permute-start(bf16[80,512]{1,0:T(8,128)(2,1)S(1)} %get-tuple-element.18.own_ref), channel_id=1, source_target_pairs={{0,504},{8,0},{16,8},{24,16},{32,24},{40,32},{48,40},{56,48},{64,5... | collective-permute-start | bytes 245768 | tf_op jit(solution)/shard_map/ppermute | solution.py:508
  4.3 18.9 %collective-permute-start = (bf16[48,512]{1,0:T(8,128)(2,1)S(1)}, bf16[48,512]{1,0:T(8,128)(2,1)S(1)}, u32[]{:S(2)}, u32[]{:S(2)}) collective-permute-start(bf16[48,512]{1,0:T(8,128)(2,1)S(1)} %get-tuple-element.17), channel_id=1, source_target_pairs={{0,8},{8,16},{16,24},{24,32},{32,40},{40,48},{48,56},{56,64},{64,7... | collective-permute-start | bytes 147464 | tf_op jit(solution)/shard_map/ppermute | solution.py:508
  6.7 16.5 %collective-permute-start.2 = (bf16[48,512]{1,0:T(8,128)(2,1)S(1)}, bf16[48,512]{1,0:T(8,128)(2,1)S(1)}, u32[]{:S(2)}, u32[]{:S(2)}) collective-permute-start(bf16[48,512]{1,0:T(8,128)(2,1)S(1)} %get-tuple-element.19), channel_id=1, source_target_pairs={{0,496},{8,504},{16,0},{24,8},{32,16},{40,24},{48,32},{56,40},{64,... | collective-permute-start | bytes 147464 | tf_op jit(solution)/shard_map/ppermute | solution.py:508
  19.9 0.7 copy-start.5
  20.0 0.7 copy-start.6
  20.0 0.7 copy-start.7
  20.0 0.7 copy-start.8
  20.6 0.9 %copy-start = (bf16[64,864]{1,0:T(8,128)(2,1)S(1)}, bf16[64,864]{1,0:T(8,128)(2,1)}, u32[]{:S(2)}) copy-start(bf16[64,864]{1,0:T(8,128)(2,1)} %w2_ref.1) | copy-start | bytes 331780
  21.5 0.8 %copy-start.3 = (bf16[108,256]{1,0:T(8,128)(2,1)S(1)}, bf16[108,256]{1,0:T(8,128)(2,1)}, u32[]{:S(2)}) copy-start(bf16[108,256]{1,0:T(8,128)(2,1)} %constant.17.clone.select_ref) | copy-start | bytes 165892
  22.4 0.9 %copy-start.9 = (f32[256,128]{1,0:T(8,128)S(1)}, f32[256,128]{1,0:T(8,128)}, u32[]{:S(2)}) copy-start(f32[256,128]{1,0:T(8,128)} %constant.18.clone.select_ref) | copy-start | bytes 393220

commit v5 on v4

--- a/solution.py
+++ b/solution.py
@@ -95,13 +95,12 @@
 
 def weights_kernel(
     rank_ref,
-    w1_ref,
-    select_ref,
-    w2_ref,
-    bias1_ref,
-    bias2_ref,
-    owners_ref,
-    accumulated_ref,
+    w1_hbm,
+    w2_hbm,
+    bias1_hbm,
+    bias2_hbm,
+    owners_hbm,
+    accumulated_hbm,
     big1_ref,
     big2_ref,
     back_ref,
@@ -111,8 +110,31 @@
     target_ref,
     kept_ref,
     ordered_ref,
+    w1_ref,
+    w2_ref,
+    bias1_ref,
+    bias2_ref,
+    owners_ref,
+    sems,
 ):
-    kept_ref[...] = accumulated_ref[...]
+    pairs = (
+        (w2_hbm, w2_ref),
+        (w1_hbm, w1_ref),
+        (bias1_hbm, bias1_ref),
+        (bias2_hbm, bias2_ref),
+        (owners_hbm, owners_ref),
+        (accumulated_hbm, kept_ref),
+    )
+    copies = [pltpu.make_async_copy(*pair, sems.at[i]) for i, pair in enumerate(pairs)]
+    for copy in copies:
+        copy.start()
+    for col in range(6):
+        cell = lax.broadcasted_iota(jnp.int32, (512, 128), 0)
+        comb_ref[:, col * 128 : col * 128 + 128] = jnp.where(
+            cell == 4 * lanes_of((512, 128)) + col - 1, 1.0, 0.0
+        ).astype(BF16)
+    for copy in copies:
+        copy.wait()
     ordered_ref[:, 768:896] = jnp.zeros((64, 128), F32)
     ordered_ref[:, 0:864] = dot(channel_order().astype(BF16), w2_ref[...])
     place = lax.broadcasted_iota(jnp.int32, (32, 32), 0) == lanes_of((32, 32))
@@ -128,7 +150,15 @@
     target_ref[:, 384:NB_PAD] = jnp.full((1, 128), -1, jnp.int32)
     target_ref[:, 0:NB] = jnp.where(mine, before.astype(jnp.int32), -1)
 
-    base = dot(w1_ref[...], select_ref[...])
+    q = lax.broadcasted_iota(jnp.int32, (108, 256), 0)
+    tap, chan = q >> 2, q & 3
+    first = (tap >= 9).astype(jnp.int32) + (tap >= 18).astype(jnp.int32)
+    tap = tap - 9 * first
+    second = (tap >= 3).astype(jnp.int32) + (tap >= 6).astype(jnp.int32)
+    lane = (first & 1) * 64 + (tap - 3 * second) * 16 + chan * 4 + second - 1
+    lane = (first >> 1) * 128 + (lane & 127)
+    select = jnp.where(lane == lanes_of((108, 256)), 1.0, 0.0).astype(BF16)
+    base = dot(w1_ref[...], select)
     y_of = lanes_of((32, 128)) % 4
     for y in range(4):
         near = jnp.abs(y_of - y) <= 1
@@ -178,11 +208,6 @@
                     tiles.append(gathered(taps))
                 at = first * 512 + other * 256 + pair * 128
                 back_ref[:, at : at + 128] = jnp.concatenate(tiles, axis=0).T.astype(BF16)
-    for col in range(6):
-        cell = lax.broadcasted_iota(jnp.int32, (512, 128), 0)
-        comb_ref[:, col * 128 : col * 128 + 128] = jnp.where(
-            cell == 4 * lanes_of((512, 128)) + col - 1, 1.0, 0.0
-        ).astype(BF16)
 
 
 def main_kernel(
@@ -419,7 +444,7 @@
         ],
         compiler_params=params(),
         cost_estimate=pl.CostEstimate(flops=1 << 16, bytes_accessed=1 << 18, transcendentals=0),
-    )(universe, cotangent)
+    )(*(pltpu.with_memory_space_constraint(x, pltpu.HBM) for x in (universe, cotangent)))
 
 
 def expand_weights(rank, w1, w2, bias1, bias2, owners, accumulated):
@@ -435,12 +460,20 @@
             jax.ShapeDtypeStruct((1, NB_PAD), jnp.int32),
             jax.ShapeDtypeStruct(accumulated.shape, F32),
         ),
-        in_specs=[pl.BlockSpec(memory_space=pltpu.SMEM)] + [whole()] * 7,
+        in_specs=[pl.BlockSpec(memory_space=pltpu.SMEM)] + [pl.BlockSpec(memory_space=pltpu.HBM)] * 6,
         out_specs=(whole(),) * 8,
-        scratch_shapes=[pltpu.VMEM((64, 896), F32)],
+        scratch_shapes=[
+            pltpu.VMEM((64, 896), F32),
+            pltpu.VMEM((32, 108), BF16),
+            pltpu.VMEM((64, 864), BF16),
+            pltpu.VMEM((1, 32), F32),
+            pltpu.VMEM((1, 64), F32),
+            pltpu.VMEM((1, NB), jnp.int32),
+            pltpu.SemaphoreType.DMA((6,)),
+        ],
         compiler_params=params(),
         cost_estimate=pl.CostEstimate(flops=1 << 26, bytes_accessed=4 << 20, transcendentals=0),
-    )(rank, w1, jnp.asarray(tap_selection(), BF16), w2, bias1, bias2, owners, accumulated)
+    )(rank, *(pltpu.with_memory_space_constraint(x, pltpu.HBM) for x in (w1, w2, bias1, bias2, owners, accumulated)))
 
 
 def forward_backward(spans, weights):

time: 77.2 us -> 76.2 us (0.987)
  local copies, waits for them, and re-layouts: 4.01 us -> 0.04 us
  Pallas kernels: 4.85 us -> 6.63 us
  blocking collectives: 49.4 us -> 50.8 us
    unnamed x20 -> x2, local copies, waits for them, and re-layouts: 3.98 us -> 0.01 us
    all_to_all x3, blocking collectives: 49.4 us -> 50.8 us  [exchange(): return lax.all_to_all(rows, axes, 0, 0, tiled=True)]
    pallas_call x1, Pallas kernels: 0.85 us -> 1.89 us  [expand_weights(): pl.pallas_call(weights_kernel, out_shape=(jax.ShapeDtypeStruct((256, 256)...]
  transfers between devices with their start and end apart: 3 -> 3, of which waited for: 0 -> 0; matrix products, arithmetic and copies ran while one was open for 0% -> 0% of each run, Pallas kernels for 1% -> 2%
where the time goes in v5:
time: 76.2 us; the launch traced here: 75.8 us
  blocking collectives  50.8 us (67%)
  starting transfers between devices  17.6 us (23%)
  Pallas kernels  6.63 us (9%)
    all_to_all x3, blocking collectives, exchange(): return lax.all_to_all(rows, axes, 0, 0, tiled=True)  50.8 us
    ppermute x3, starting transfers between devices, from_slab(): return lax.ppermute(rows, SLAB, pairs)  17.6 us
    pallas_call x1, Pallas kernels, forward_backward(): pl.pallas_call(main_kernel, out_shape=(jax.ShapeDtypeStruct((64, 128), BF...  2.97 us
    pallas_call x1, Pallas kernels, expand_weights(): pl.pallas_call(weights_kernel, out_shape=(jax.ShapeDtypeStruct((256, 256)...  1.89 us
  transfers between devices with their start and end apart: 3, of which 0 were waited for; matrix products, arithmetic and copies ran while one was open for 0% of the time, Pallas kernels for 2%

profile of v5, /device:TPU:8, one launch (start us, length us, event | category | flops | bytes accessed | tf_op | source)
XLA Modules:
  0.0 75.8 jit_solution(5246471045610042041)
XLA Ops:
  0.6 0.9 %shard_map.104 = (bf16[80,512]{1,0:T(8,128)(2,1)S(1)}, bf16[48,512]{1,0:T(8,128)(2,1)S(1)}, bf16[48,512]{1,0:T(8,128)(2,1)S(1)}) custom-call(bf16[1,4,4,4,512]{4,3,2,1,0:T(4,128)(2,1)} %universe_hbm.1, bf16[64,128]{1,0:T(8,128)(2,1)} %bitcast.10), custom_call_target="tpu_custom_call" | custom-call | flops 65536 | bytes 262144 | tf_op jit(solution)/shard_map/pallas_call | solution.py:431
  1.5 1.9 %collective-permute-start.1 = (bf16[80,512]{1,0:T(8,128)(2,1)S(1)}, bf16[80,512]{1,0:T(8,128)(2,1)S(1)}, u32[]{:S(2)}, u32[]{:S(2)}) collective-permute-start(bf16[80,512]{1,0:T(8,128)(2,1)S(1)} %get-tuple-element.18.own_ref), channel_id=1, source_target_pairs={{0,504},{8,0},{16,8},{24,16},{32,24},{40,32},{48,40},{56,48},{64,5... | collective-permute-start | bytes 245768 | tf_op jit(solution)/shard_map/ppermute | solution.py:541
  3.4 2.4 %collective-permute-start = (bf16[48,512]{1,0:T(8,128)(2,1)S(1)}, bf16[48,512]{1,0:T(8,128)(2,1)S(1)}, u32[]{:S(2)}, u32[]{:S(2)}) collective-permute-start(bf16[48,512]{1,0:T(8,128)(2,1)S(1)} %get-tuple-element.17), channel_id=1, source_target_pairs={{0,8},{8,16},{16,24},{24,32},{32,40},{40,48},{48,56},{56,64},{64,7... | collective-permute-start | bytes 147464 | tf_op jit(solution)/shard_map/ppermute | solution.py:541
  5.9 13.2 %collective-permute-start.2 = (bf16[48,512]{1,0:T(8,128)(2,1)S(1)}, bf16[48,512]{1,0:T(8,128)(2,1)S(1)}, u32[]{:S(2)}, u32[]{:S(2)}) collective-permute-start(bf16[48,512]{1,0:T(8,128)(2,1)S(1)} %get-tuple-element.19), channel_id=1, source_target_pairs={{0,496},{8,504},{16,0},{24,8},{32,16},{40,24},{48,32},{56,40},{64,... | collective-permute-start | bytes 147464 | tf_op jit(solution)/shard_map/ppermute | solution.py:541
  19.1 0.0 copy-start
  19.1 1.9 %shard_map.105 = (bf16[256,256]{1,0:T(8,128)(2,1)S(1)}, bf16[256,768]{1,0:T(8,128)(2,1)S(1)}, bf16[128,1536]{1,0:T(8,128)(2,1)S(1)}, bf16[512,768]{1,0:T(8,128)(...) custom-call(s32[1]{0:T(128)} %bitcast.1.rank_ref, ...), custom_call_target="tpu_custom_call" | custom-call | flops 67108864 | bytes 4194304 | tf_op jit(solution)/shard_map/pallas_call | solution.py:451
  21.0 0.0 collective-permute-done.prev_ref
  21.0 0.0 collective-permute-done.2.after_ref
  21.0 0.0 collective-permute-done.1.next_ref
  21.0 0.0 copy-done
  21.1 3.0 %shard_map.106 = (bf16[64,128]{1,0:T(8,128)(2,1)S(1)}, f32[512,128]{1,0:T(8,128)S(1)}) custom-call(bf16[48,512]{1,0:T(8,128)(2,1)S(1)} %collective-permute-done.prev_ref, bf16[80,512]{1,0:T(8,128)(2,1)S(1)} %get-tuple-element.18.own_ref, bf16[80,512]{1,0:T(8,128)(2,1)S(1)} %collective-permute-done.1.next_ref, ...), custom_call_target="tpu_custom_call" | custom-call | flops 2147483648 | bytes 4194304 | tf_op jit(solution)/shard_map/pallas_call | solution.py:480
  24.0 16.7 %all_to_all.23 = f32[32,16,128]{2,1,0:T(8,128)S(1)} all-to-all(f32[32,16,128]{2,1,0:T(8,128)S(1)} %bitcast.8), channel_id=1, replica_groups=mesh['z_hi'=4,'y'=8,'core'=2,'z_lo'=2,'x'=4] {'x','z_hi','z_lo'}, dimensions={0} | all-to-all | bytes 524288 | tf_op jit(solution)/shard_map/all_to_all | solution.py:522
  40.8 18.1 %all_to_all.24 = f32[16,16,128]{2,1,0:T(8,128)S(1)} all-to-all(f32[16,16,128]{2,1,0:T(8,128)S(1)} %tile.4), channel_id=1, replica_groups=mesh['z_hi'=4,'y'=8,'core'=2,'z_lo'=2,'x'=4] {'core','y'}, dimensions={0} | all-to-all | bytes 262144 | tf_op jit(solution)/shard_map/all_to_all | solution.py:522
  58.9 16.0 %all_to_all.25 = f32[32,16,128]{2,1,0:T(8,128)S(1)} all-to-all(f32[32,16,128]{2,1,0:T(8,128)S(1)} %tile.5), channel_id=1, replica_groups=mesh['z_hi'=4,'y'=8,'core'=2,'z_lo'=2,'x'=4] {'x','z_hi','z_lo'}, dimensions={0} | all-to-all | bytes 524288 | tf_op jit(solution)/shard_map/all_to_all | solution.py:522
  74.9 0.9 %shard_map.107 = (bf16[64,128]{1,0:T(8,128)(2,1)}, f32[138,128]{1,0:T(8,128)}) custom-call(f32[512,128]{1,0:T(8,128)S(1)} %bitcast.9, s32[1,512]{1,0:T(1,128)S(1)} %get-tuple-element.27.target_ref, f32[138,128]{1,0:T(8,128)S(1)} %get-tuple-element.28.kept_ref, bf16[64,128]{1,0:T(8,128)(2,1)S(1)} %get-tuple-element.29.feature_ref), custom_call_target="tpu_custom_call" | custom-call | flops 134217728 | bytes 1048576 | tf_op jit(solution)/shard_map/pallas_call | solution.py:502
  (4 shorter events, 0.1 us)
Async XLA Ops:
  1.5 19.5 %collective-permute-start.1 = (bf16[80,512]{1,0:T(8,128)(2,1)S(1)}, bf16[80,512]{1,0:T(8,128)(2,1)S(1)}, u32[]{:S(2)}, u32[]{:S(2)}) collective-permute-start(bf16[80,512]{1,0:T(8,128)(2,1)S(1)} %get-tuple-element.18.own_ref), channel_id=1, source_target_pairs={{0,504},{8,0},{16,8},{24,16},{32,24},{40,32},{48,40},{56,48},{64,5... | collective-permute-start | bytes 245768 | tf_op jit(solution)/shard_map/ppermute | solution.py:541
  3.4 17.6 %collective-permute-start = (bf16[48,512]{1,0:T(8,128)(2,1)S(1)}, bf16[48,512]{1,0:T(8,128)(2,1)S(1)}, u32[]{:S(2)}, u32[]{:S(2)}) collective-permute-start(bf16[48,512]{1,0:T(8,128)(2,1)S(1)} %get-tuple-element.17), channel_id=1, source_target_pairs={{0,8},{8,16},{16,24},{24,32},{32,40},{40,48},{48,56},{56,64},{64,7... | collective-permute-start | bytes 147464 | tf_op jit(solution)/shard_map/ppermute | solution.py:541
  5.9 15.2 %collective-permute-start.2 = (bf16[48,512]{1,0:T(8,128)(2,1)S(1)}, bf16[48,512]{1,0:T(8,128)(2,1)S(1)}, u32[]{:S(2)}, u32[]{:S(2)}) collective-permute-start(bf16[48,512]{1,0:T(8,128)(2,1)S(1)} %get-tuple-element.19), channel_id=1, source_target_pairs={{0,496},{8,504},{16,0},{24,8},{32,16},{40,24},{48,32},{56,40},{64,... | collective-permute-start | bytes 147464 | tf_op jit(solution)/shard_map/ppermute | solution.py:541
  19.1 1.9 %copy-start = (f32[256,128]{1,0:T(8,128)S(1)}, f32[256,128]{1,0:T(8,128)}, u32[]{:S(2)}) copy-start(f32[256,128]{1,0:T(8,128)} %constant.15.clone.select_ref) | copy-start | bytes 393220

commit v6 on v4

--- a/solution.py
+++ b/solution.py
@@ -52,10 +52,6 @@
     return jnp.where(lanes_of(value.shape) == 127, 0.0, pltpu.roll(value, 127, 1))
 
 
-def side_by_side(ref, at, step, rows):
-    return jnp.concatenate([ref[at : at + rows, :], ref[at + step : at + step + rows, :]], axis=1)
-
-
 def leaky_relu(value):
     return jnp.where(value > 0, value, SLOPE * value)
 
@@ -70,12 +66,42 @@
 
 
 def pack_kernel(
-    universe_hbm, cotangent_hbm, own_ref, late_ref, early_ref, universe_ref, cotangent_ref, sems
+    universe_hbm,
+    cotangent_hbm,
+    w1_hbm,
+    w2_hbm,
+    bias1_hbm,
+    bias2_hbm,
+    owners_hbm,
+    accumulated_hbm,
+    own_ref,
+    late_ref,
+    early_ref,
+    w1_ref,
+    w2_ref,
+    bias1_ref,
+    bias2_ref,
+    owners_ref,
+    kept_ref,
+    universe_ref,
+    cotangent_ref,
+    sems,
 ):
     first = pltpu.make_async_copy(universe_hbm, universe_ref, sems.at[0])
     second = pltpu.make_async_copy(cotangent_hbm, cotangent_ref, sems.at[1])
     first.start()
     second.start()
+    pairs = (
+        (w1_hbm, w1_ref),
+        (w2_hbm, w2_ref),
+        (bias1_hbm, bias1_ref),
+        (bias2_hbm, bias2_ref),
+        (owners_hbm, owners_ref),
+        (accumulated_hbm, kept_ref),
+    )
+    others = [pltpu.make_async_copy(*pair, sems.at[i + 2]) for i, pair in enumerate(pairs)]
+    for copy in others:
+        copy.start()
     first.wait()
     for deep in range(4):
         rows = jnp.concatenate(
@@ -84,24 +110,23 @@
         own_ref[deep * 16 : deep * 16 + 16, :] = rows
         if deep > 0:
             late_ref[deep * 16 - 16 : deep * 16, :] = rows
-        if deep < 3:
-            early_ref[deep * 16 : deep * 16 + 16, :] = rows
+        early_ref[deep * 16 : deep * 16 + 16, :] = rows
     second.wait()
     for group in range(4):
         own_ref[64:80, group * 128 : group * 128 + 128] = cotangent_ref[
             group * 16 : group * 16 + 16, :
         ]
+    for copy in others:
+        copy.wait()
 
 
 def weights_kernel(
     rank_ref,
     w1_ref,
-    select_ref,
     w2_ref,
     bias1_ref,
     bias2_ref,
     owners_ref,
-    accumulated_ref,
     big1_ref,
     big2_ref,
     back_ref,
@@ -109,10 +134,13 @@
     wide1_ref,
     wide2_ref,
     target_ref,
-    kept_ref,
     ordered_ref,
 ):
-    kept_ref[...] = accumulated_ref[...]
+    for col in range(6):
+        cell = lax.broadcasted_iota(jnp.int32, (512, 128), 0)
+        comb_ref[:, col * 128 : col * 128 + 128] = jnp.where(
+            cell == 4 * lanes_of((512, 128)) + col - 1, 1.0, 0.0
+        ).astype(BF16)
     ordered_ref[:, 768:896] = jnp.zeros((64, 128), F32)
     ordered_ref[:, 0:864] = dot(channel_order().astype(BF16), w2_ref[...])
     place = lax.broadcasted_iota(jnp.int32, (32, 32), 0) == lanes_of((32, 32))
@@ -128,7 +156,15 @@
     target_ref[:, 384:NB_PAD] = jnp.full((1, 128), -1, jnp.int32)
     target_ref[:, 0:NB] = jnp.where(mine, before.astype(jnp.int32), -1)
 
-    base = dot(w1_ref[...], select_ref[...])
+    q = lax.broadcasted_iota(jnp.int32, (108, 256), 0)
+    tap, chan = q >> 2, q & 3
+    first = (tap >= 9).astype(jnp.int32) + (tap >= 18).astype(jnp.int32)
+    tap = tap - 9 * first
+    second = (tap >= 3).astype(jnp.int32) + (tap >= 6).astype(jnp.int32)
+    lane = (first & 1) * 64 + (tap - 3 * second) * 16 + chan * 4 + second - 1
+    lane = (first >> 1) * 128 + (lane & 127)
+    select = jnp.where(lane == lanes_of((108, 256)), 1.0, 0.0).astype(BF16)
+    base = dot(w1_ref[...], select)
     y_of = lanes_of((32, 128)) % 4
     for y in range(4):
         near = jnp.abs(y_of - y) <= 1
@@ -178,18 +214,118 @@
                     tiles.append(gathered(taps))
                 at = first * 512 + other * 256 + pair * 128
                 back_ref[:, at : at + 128] = jnp.concatenate(tiles, axis=0).T.astype(BF16)
+
+
+def expand(source, comb_ref, field_ref):
     for col in range(6):
-        cell = lax.broadcasted_iota(jnp.int32, (512, 128), 0)
-        comb_ref[:, col * 128 : col * 128 + 128] = jnp.where(
-            cell == 4 * lanes_of((512, 128)) + col - 1, 1.0, 0.0
+        part = dot(source, comb_ref[:, col * 128 : col * 128 + 128]).astype(BF16)
+        for layer in range(source.shape[0] // 16):
+            at = layer * 96 + col * 16
+            field_ref[at : at + 16, :] = part[layer * 16 : layer * 16 + 16, :]
+
+
+def around(layers, half):
+    empty = jnp.zeros((64, 128), BF16)
+    parts = []
+    for deep in range(2):
+        for pair in range(2):
+            pieces = []
+            for first in range(3):
+                ref, at = layers(2 * half + deep + first)
+                pieces.append(ref[at + pair * 32 : at + pair * 32 + 64, :])
+            parts.append(jnp.concatenate(pieces + [empty], axis=0))
+    return jnp.concatenate(parts, axis=1)
+
+
+def stacks(pieces, begin):
+    columns = [
+        jnp.concatenate([pieces(half) for half in range(at, at + 3)], axis=0)
+        for at in (begin, begin + 1)
+    ]
+    return jnp.concatenate(columns, axis=1)
+
+
+def pool_first(conv, bias1, pooled_ref, at, pre_ref, pre_at):
+    for y in range(2):
+        means = []
+        for pair in range(2):
+            total = None
+            for deep in range(2):
+                lane = (deep * 2 + pair) * 128
+                for row in range(y * 128, y * 128 + 128, 32):
+                    block = conv[row : row + 32, lane : lane + 128] + bias1
+                    if pre_ref is not None:
+                        pre_ref[pre_at + row : pre_at + row + 32, lane : lane + 128] = block
+                    value = leaky_relu(block)
+                    total = value if total is None else total + value
+            means.append((total * 0.125).astype(BF16).astype(F32))
+        even, odd = means
+        pooled_ref[at + y * 128 : at + y * 128 + 128, :] = jnp.concatenate(
+            [from_left(odd), even, odd, from_right(even)], axis=0
         ).astype(BF16)
+
+
+def delta_second(conv, bias2, cotangent_ref, delta2_ref):
+    plain = [cotangent_ref[64:80, g * 128 : g * 128 + 128] for g in range(4)]
+    upstream = dot(channel_order().astype(BF16), jnp.concatenate(plain, axis=0)) * 0.125
+    total = jnp.zeros((64, 128), F32)
+    for half in range(2):
+        lane = half * 128
+        for y in range(2):
+            deltas = []
+            for ph in range(2):
+                row = (y * 2 + ph) * 64
+                block = conv[row : row + 64, lane : lane + 128] + bias2
+                total = total + leaky_relu(block)
+                deltas.append((upstream * slope_mask(block)).astype(BF16).astype(F32))
+            at = half * 512 + y * 256
+            delta2_ref[at : at + 256, :] = jnp.concatenate(
+                [from_left(deltas[1]), deltas[0], deltas[1], from_right(deltas[0])], axis=0
+            ).astype(BF16)
+    return total
+
+
+def late_kernel(
+    own_ref,
+    next_ref,
+    after_ref,
+    big1_ref,
+    big2_ref,
+    comb_ref,
+    wide1_ref,
+    wide2_ref,
+    field_ref,
+    pooled_ref,
+    pre_ref,
+    delta2_ref,
+):
+    source = jnp.concatenate(
+        [own_ref[0:64, :], next_ref[0:64, :], after_ref[0:48, :]], axis=0
+    )
+    expand(source, comb_ref, field_ref)
+
+    def layers(layer):
+        return field_ref, (layer - 3) * 96
+
+    for half in range(2, 6):
+        conv = dot(big1_ref[...], around(layers, half))
+        kept = pre_ref if half < 4 else None
+        pool_first(conv, wide1_ref[...], pooled_ref, (half - 2) * 256, kept, (half - 2) * 256)
+
+    def pooled(half):
+        return pooled_ref[(half - 2) * 256 : (half - 1) * 256, :]
+
+    conv = dot(big2_ref[...], stacks(pooled, 2))
+    delta_second(conv, wide2_ref[...], next_ref, delta2_ref)
 
 
 def main_kernel(
     prev_ref,
     own_ref,
-    next_ref,
-    after_ref,
+    late_field_ref,
+    late_pooled_ref,
+    pre_ref,
+    late_delta2_ref,
     big1_ref,
     big2_ref,
     back_ref,
@@ -202,92 +338,43 @@
     field_ref,
     pooled_ref,
     delta2_ref,
-    pre_ref,
     delta1_ref,
     order_ref,
 ):
-    source = jnp.concatenate(
-        [prev_ref[...], own_ref[0:64, :], next_ref[0:64, :], after_ref[...]], axis=0
-    )
-    for col in range(6):
-        part = dot(source, comb_ref[:, col * 128 : col * 128 + 128]).astype(BF16)
-        for layer in range(14):
-            at = layer * 96 + col * 16
-            field_ref[at : at + 16, :] = part[layer * 16 : layer * 16 + 16, :]
-    empty = jnp.zeros((64, 128), BF16)
-
-    def around(half):
-        parts = []
-        for deep in range(2):
-            for pair in range(2):
-                at = (2 * half + deep) * 96 + pair * 32
-                layers = [field_ref[at + first * 96 : at + first * 96 + 64, :] for first in range(3)]
-                parts.append(jnp.concatenate(layers + [empty], axis=0))
-        return jnp.concatenate(parts, axis=1)
-
-    bias1 = wide1_ref[...]
-    for half in range(6):
-        conv = dot(big1_ref[...], around(half))
-        for y in range(2):
-            means = []
-            for pair in range(2):
-                total = None
-                for deep in range(2):
-                    lane = (deep * 2 + pair) * 128
-                    for row in range(y * 128, y * 128 + 128, 32):
-                        block = conv[row : row + 32, lane : lane + 128] + bias1
-                        if half in (2, 3):
-                            at = (half - 2) * 256 + row
-                            pre_ref[at : at + 32, lane : lane + 128] = block
-                        value = leaky_relu(block)
-                        total = value if total is None else total + value
-                means.append((total * 0.125).astype(BF16).astype(F32))
-            even, odd = means
-            at = half * 256 + y * 128
-            pooled_ref[at : at + 128, :] = jnp.concatenate(
-                [from_left(odd), even, odd, from_right(even)], axis=0
-            ).astype(BF16)
-
-    bias2 = wide2_ref[...]
-    total = jnp.zeros((64, 128), F32)
-    plain = jnp.concatenate(
-        [
-            jnp.concatenate([ref[64:80, g * 128 : g * 128 + 128] for g in range(4)], axis=0)
-            for ref in (own_ref, next_ref)
-        ],
-        axis=1,
-    )
-    upstreams = dot(channel_order().astype(BF16), plain) * 0.125
-    for half in range(4):
-        if half % 2 == 0:
-            conv = dot(big2_ref[...], side_by_side(pooled_ref, half * 256, 256, 768))
-        lane = half % 2 * 128
-        upstream = upstreams[:, half // 2 * 128 : half // 2 * 128 + 128]
-        for y in range(2):
-            deltas = []
-            for ph in range(2):
-                row = (y * 2 + ph) * 64
-                block = conv[row : row + 64, lane : lane + 128] + bias2
-                if half < 2:
-                    total = total + leaky_relu(block)
-                deltas.append((upstream * slope_mask(block)).astype(BF16).astype(F32))
-            at = half * 512 + y * 256
-            delta2_ref[at : at + 256, :] = jnp.concatenate(
-                [from_left(deltas[1]), deltas[0], deltas[1], from_right(deltas[0])], axis=0
-            ).astype(BF16)
-    feature = total * 0.125
+    expand(prev_ref[...], comb_ref, field_ref)
+
+    def layers(layer):
+        return (field_ref, layer * 96) if layer < 3 else (late_field_ref, (layer - 3) * 96)
+
+    def pooled(half):
+        ref, at = (pooled_ref, half * 256) if half < 2 else (late_pooled_ref, (half - 2) * 256)
+        return ref[at : at + 256, :]
+
+    def delta_rows(half, begin, rows):
+        ref, at = (delta2_ref, half * 512) if half < 2 else (late_delta2_ref, (half - 2) * 512)
+        return ref[at + begin : at + begin + rows, :]
+
+    for half in range(2):
+        conv = dot(big1_ref[...], around(layers, half))
+        pool_first(conv, wide1_ref[...], pooled_ref, half * 256, None, 0)
+    conv = dot(big2_ref[...], stacks(pooled, 0))
+    feature = delta_second(conv, wide2_ref[...], own_ref, delta2_ref) * 0.125
     for u in range(4):
         order_ref[pl.ds(u, 16, stride=4), :] = feature[u * 16 : u * 16 + 16, :]
     feature_ref[...] = order_ref[...].astype(BF16)
 
     ones = jnp.ones((8, 256), BF16)
     delta = jnp.concatenate(
-        [side_by_side(delta2_ref, 512 + y * 256 + 64, 512, 128) for y in range(2)], axis=0
+        [
+            jnp.concatenate([delta_rows(half, y * 256 + 64, 128) for half in (1, 2)], axis=1)
+            for y in range(2)
+        ],
+        axis=0,
     )
-    grad2 = dot_lanes(delta, side_by_side(pooled_ref, 256, 256, 768))
+    grad2 = dot_lanes(delta, stacks(pooled, 1))
     bias_sum2 = dot_lanes(ones, delta)
 
-    backs = dot(back_ref[...], side_by_side(delta2_ref, 0, 512, 1536)) * 0.125
+    backs = dot(back_ref[...], stacks(lambda half: delta_rows(half, 0, 512), 0)) * 0.125
     ones = jnp.ones((8, 512), BF16)
     grad1 = None
     bias_sum1 = None
@@ -303,7 +390,7 @@
                         back * slope_mask(pre_ref[at : at + 32, lane : lane + 128])
                     ).astype(BF16)
         delta = delta1_ref[half * 256 : half * 256 + 256, :]
-        term = dot_lanes(delta, around(half + 2))
+        term = dot_lanes(delta, around(layers, half + 2))
         bias_term = dot_lanes(ones, delta)
         grad1 = term if grad1 is None else grad1 + term
         bias_sum1 = bias_term if bias_sum1 is None else bias_sum1 + bias_term
@@ -402,27 +489,29 @@
     return pltpu.CompilerParams(vmem_limit_bytes=VMEM_LIMIT)
 
 
-def pack(universe, cotangent):
+def pack(*operands):
+    universe, cotangent, *others = operands
     return pl.pallas_call(
         pack_kernel,
         out_shape=(
             jax.ShapeDtypeStruct((80, 512), BF16),
             jax.ShapeDtypeStruct((48, 512), BF16),
-            jax.ShapeDtypeStruct((48, 512), BF16),
+            jax.ShapeDtypeStruct((64, 512), BF16),
+            *(jax.ShapeDtypeStruct(x.shape, x.dtype) for x in others),
         ),
-        in_specs=[pl.BlockSpec(memory_space=pltpu.HBM)] * 2,
-        out_specs=(whole(),) * 3,
+        in_specs=[pl.BlockSpec(memory_space=pltpu.HBM)] * 8,
+        out_specs=(whole(),) * 9,
         scratch_shapes=[
             pltpu.VMEM(universe.shape, BF16),
             pltpu.VMEM(cotangent.shape, BF16),
-            pltpu.SemaphoreType.DMA((2,)),
+            pltpu.SemaphoreType.DMA((8,)),
         ],
         compiler_params=params(),
         cost_estimate=pl.CostEstimate(flops=1 << 16, bytes_accessed=1 << 18, transcendentals=0),
-    )(universe, cotangent)
-
-
-def expand_weights(rank, w1, w2, bias1, bias2, owners, accumulated):
+    )(*(pltpu.with_memory_space_constraint(x, pltpu.HBM) for x in operands))
+
+
+def expand_weights(rank, *operands):
     return pl.pallas_call(
         weights_kernel,
         out_shape=(
@@ -433,36 +522,50 @@
             jax.ShapeDtypeStruct((32, 128), F32),
             jax.ShapeDtypeStruct((64, 128), F32),
             jax.ShapeDtypeStruct((1, NB_PAD), jnp.int32),
-            jax.ShapeDtypeStruct(accumulated.shape, F32),
         ),
-        in_specs=[pl.BlockSpec(memory_space=pltpu.SMEM)] + [whole()] * 7,
-        out_specs=(whole(),) * 8,
+        in_specs=[pl.BlockSpec(memory_space=pltpu.SMEM)] + [whole()] * 5,
+        out_specs=(whole(),) * 7,
         scratch_shapes=[pltpu.VMEM((64, 896), F32)],
         compiler_params=params(),
         cost_estimate=pl.CostEstimate(flops=1 << 26, bytes_accessed=4 << 20, transcendentals=0),
-    )(rank, w1, jnp.asarray(tap_selection(), BF16), w2, bias1, bias2, owners, accumulated)
-
-
-def forward_backward(spans, weights):
+    )(rank, *operands)
+
+
+def forward_late(own, following, after, big1, big2, comb, wide1, wide2):
+    return pl.pallas_call(
+        late_kernel,
+        out_shape=(
+            jax.ShapeDtypeStruct((11 * 96, 128), BF16),
+            jax.ShapeDtypeStruct((4 * 256, 128), BF16),
+            jax.ShapeDtypeStruct((2 * 256, 512), F32),
+            jax.ShapeDtypeStruct((2 * 512, 128), BF16),
+        ),
+        in_specs=[whole()] * 8,
+        out_specs=(whole(),) * 4,
+        compiler_params=params(),
+        cost_estimate=pl.CostEstimate(flops=1 << 30, bytes_accessed=4 << 20, transcendentals=0),
+    )(own, following, after, big1, big2, comb, wide1, wide2)
+
+
+def forward_backward(before, own, late, weights):
     return pl.pallas_call(
         main_kernel,
         out_shape=(
             jax.ShapeDtypeStruct((64, 128), BF16),
             jax.ShapeDtypeStruct((NB_PAD, 128), F32),
         ),
-        in_specs=[whole()] * 11,
+        in_specs=[whole()] * 13,
         out_specs=(whole(),) * 2,
         scratch_shapes=[
-            pltpu.VMEM((14 * 96, 128), BF16),
-            pltpu.VMEM((6 * 256, 128), BF16),
-            pltpu.VMEM((4 * 512, 128), BF16),
-            pltpu.VMEM((2 * 256, 512), F32),
+            pltpu.VMEM((3 * 96, 128), BF16),
+            pltpu.VMEM((2 * 256, 128), BF16),
+            pltpu.VMEM((2 * 512, 128), BF16),
             pltpu.VMEM((2 * 256, 512), BF16),
             pltpu.VMEM((64, 128), F32),
         ],
         compiler_params=params(),
-        cost_estimate=pl.CostEstimate(flops=1 << 31, bytes_accessed=4 << 20, transcendentals=0),
-    )(*spans, *weights, jnp.asarray(np.pad(tap_selection().T, ((0, 0), (0, 20))), F32))
+        cost_estimate=pl.CostEstimate(flops=1 << 30, bytes_accessed=4 << 20, transcendentals=0),
+    )(before, own, *late, *weights, jnp.asarray(np.pad(tap_selection().T, ((0, 0), (0, 20))), F32))
 
 
 def add_owned(blocks, target, kept, feature):
@@ -481,7 +584,7 @@
 
 SLAB = ("z_hi", "y", "core")
 DP = ("z_lo", "x")
-PLANE = ("x", "z_hi", "z_lo")
+PLANE = ("x", "z_lo", "z_hi")
 REST = ("core", "y")
 
 
@@ -501,15 +604,9 @@
     universe, cotangent, conv1_weight, conv1_bias, conv2_weight, conv2_bias, owners, accumulated
 ):
     slabs = lax.axis_size(SLAB)
-    packed, late, early = pack(universe, cotangent.reshape(64, 128))
-
-    def from_slab(distance, rows):
-        pairs = [(i, (i - distance) % slabs) for i in range(slabs)]
-        return lax.ppermute(rows, SLAB, pairs)
-
-    spans = (from_slab(-1, late), packed, from_slab(1, packed), from_slab(2, early))
-    *weights, target, kept = expand_weights(
-        lax.axis_index(DP).reshape(1),
+    packed, late, early, *others, kept = pack(
+        universe,
+        cotangent.reshape(64, 128),
         conv1_weight,
         conv2_weight,
         conv1_bias.reshape(1, 32),
@@ -517,7 +614,15 @@
         owners.reshape(1, NB),
         accumulated,
     )
-    feature, blocks = forward_backward(spans, weights)
+    def from_slab(distance, rows):
+        pairs = [(i, (i - distance) % slabs) for i in range(slabs)]
+        return lax.ppermute(rows, SLAB, pairs)
+
+    before, following, after = from_slab(-1, late), from_slab(1, packed), from_slab(2, early)
+    *weights, target = expand_weights(lax.axis_index(DP).reshape(1), *others)
+    big1, big2, _, comb, wide1, wide2 = weights
+    ahead = forward_late(packed, following, after, big1, big2, comb, wide1, wide2)
+    feature, blocks = forward_backward(before, packed, ahead, weights)
     feature, owned = add_owned(sum_everywhere(blocks), target, kept, feature)
     return (feature.reshape(1, 64, 1, 1, 128), owned)
 

time: 77.2 us -> 75 us (0.972)
  local copies, waits for them, and re-layouts: 4.01 us -> 0.04 us
  Pallas kernels: 4.85 us -> 6.65 us
  waiting for transfers between devices: 0.01 us -> 1.15 us
  blocking collectives: 49.4 us -> 48.5 us
    unnamed x20 -> x2, local copies, waits for them, and re-layouts: 3.98 us -> 0.01 us
    pallas_call x0 -> x1, Pallas kernels: none -> 1.37 us  [forward_late(): pl.pallas_call(late_kernel, out_shape=(jax.ShapeDtypeStruct((11 * 96, 128...]
    ppermute x3, waiting for transfers between devices: 0.01 us -> 1.15 us  [from_slab(): return lax.ppermute(rows, SLAB, pairs)]
    pallas_call x1, Pallas kernels: 0.11 us -> 1.14 us  [pack(): pl.pallas_call(pack_kernel, out_shape=(jax.ShapeDtypeStruct((80, 512), BF...]
    all_to_all x3, blocking collectives: 49.4 us -> 48.5 us  [exchange(): return lax.all_to_all(rows, axes, 0, 0, tiled=True)]
  transfers between devices with their start and end apart: 3 -> 3, of which waited for: 0 -> 1; matrix products, arithmetic and copies ran while one was open for 0% -> 0% of each run, Pallas kernels for 1% -> 3%
where the time goes in v6:
time: 75 us; the launch traced here: 74.7 us
  blocking collectives  48.5 us (65%)
  starting transfers between devices  17.6 us (23%)
  Pallas kernels  6.65 us (9%)
  waiting for transfers between devices  1.15 us (2%)
    all_to_all x3, blocking collectives, exchange(): return lax.all_to_all(rows, axes, 0, 0, tiled=True)  48.5 us
    ppermute x3, starting transfers between devices, from_slab(): return lax.ppermute(rows, SLAB, pairs)  17.6 us
    pallas_call x1, Pallas kernels, forward_backward(): pl.pallas_call(main_kernel, out_shape=(jax.ShapeDtypeStruct((64, 128), BF...  2.33 us
  transfers between devices with their start and end apart: 3, of which 1 were waited for; matrix products, arithmetic and copies ran while one was open for 0% of the time, Pallas kernels for 3%

profile of v6, /device:TPU:8, one launch (start us, length us, event | category | flops | bytes accessed | tf_op | source)
XLA Modules:
  0.0 74.7 jit_solution(1548877222330875152)
XLA Ops:
  0.6 1.1 %shard_map.104 = (bf16[80,512]{1,0:T(8,128)(2,1)S(1)}, bf16[48,512]{1,0:T(8,128)(2,1)S(1)}, bf16[64,512]{1,0:T(8,128)(2,1)S(1)}, bf16[32,108]{1,0:T(8,128)(2,1)S...) custom-call(bf16[1,4,4,4,512]{4,3,2,1,0:T(4,128)(2,1)} %universe_hbm, ...), custom_call_target="tpu_custom_call" | custom-call | flops 65536 | bytes 262144 | tf_op jit(solution)/shard_map/pallas_call | solution.py:494
  1.8 1.9 %collective-permute-start.1 = (bf16[80,512]{1,0:T(8,128)(2,1)S(1)}, bf16[80,512]{1,0:T(8,128)(2,1)S(1)}, u32[]{:S(2)}, u32[]{:S(2)}) collective-permute-start(bf16[80,512]{1,0:T(8,128)(2,1)S(1)} %get-tuple-element.27.own_ref), channel_id=1, source_target_pairs={{0,504},{8,0},{16,8},{24,16},{32,24},{40,32},{48,40},{56,48},{64,5... | collective-permute-start | bytes 245768 | tf_op jit(solution)/shard_map/ppermute | solution.py:619
  3.7 13.7 %collective-permute-start.2 = (bf16[64,512]{1,0:T(8,128)(2,1)S(1)}, bf16[64,512]{1,0:T(8,128)(2,1)S(1)}, u32[]{:S(2)}, u32[]{:S(2)}) collective-permute-start(bf16[64,512]{1,0:T(8,128)(2,1)S(1)} %get-tuple-element.28), channel_id=1, source_target_pairs={{0,496},{8,504},{16,0},{24,8},{32,16},{40,24},{48,32},{56,40},{64,... | collective-permute-start | bytes 196616 | tf_op jit(solution)/shard_map/ppermute | solution.py:619
  17.4 1.9 %collective-permute-start = (bf16[48,512]{1,0:T(8,128)(2,1)S(1)}, bf16[48,512]{1,0:T(8,128)(2,1)S(1)}, u32[]{:S(2)}, u32[]{:S(2)}) collective-permute-start(bf16[48,512]{1,0:T(8,128)(2,1)S(1)} %get-tuple-element.26), channel_id=1, source_target_pairs={{0,8},{8,16},{16,24},{24,32},{32,40},{40,48},{48,56},{56,64},{64,7... | collective-permute-start | bytes 147464 | tf_op jit(solution)/shard_map/ppermute | solution.py:619
  19.4 0.9 %shard_map.105 = (bf16[256,256]{1,0:T(8,128)(2,1)S(1)}, bf16[256,768]{1,0:T(8,128)(2,1)S(1)}, bf16[128,1536]{1,0:T(8,128)(2,1)S(1)}, bf16[512,768]{1,0:T(8,128)(...) custom-call(s32[1]{0:T(128)} %bitcast.4.rank_ref, ...), custom_call_target="tpu_custom_call" | custom-call | flops 67108864 | bytes 4194304 | tf_op jit(solution)/shard_map/pallas_call | solution.py:515
  20.3 0.0 collective-permute-done.2.after_ref
  20.3 0.0 collective-permute-done.1.next_ref
  20.3 0.0 copy-start
  20.3 1.4 %shard_map.106 = (bf16[1056,128]{1,0:T(8,128)(2,1)S(1)}, bf16[1024,128]{1,0:T(8,128)(2,1)S(1)}, f32[512,512]{1,0:T(8,128)S(1)}, bf16[1024,128]{1,0:T(8,128)(2,1)S(1)}) custom-call(bf16[80,512]{1,0:T(8,128)(2,1)S(1)} %get-tuple-element.27.own_ref, bf16[80,512]{1,0:T(8,128)(2,1)S(1)} %collective-permute-done.1.next_ref, ...), custom_call_target="tpu_custom_call" | custom-call | flops 1073741824 | bytes 4194304 | tf_op jit(solution)/shard_map/pallas_call | solution.py:535
  21.7 1.1 %collective-permute-done.prev_ref = bf16[48,512]{1,0:T(8,128)(2,1)S(1)} collective-permute-done((bf16[48,512]{1,0:T(8,128)(2,1)S(1)}, bf16[48,512]{1,0:T(8,128)(2,1)S(1)}, u32[]{:S(2)}, u32[]{:S(2)}) %collective-permute-start) | collective-permute-done | bytes 49184 | tf_op jit(solution)/shard_map/ppermute | solution.py:619
  22.8 0.0 copy-done
  22.8 2.3 %shard_map.107 = (bf16[64,128]{1,0:T(8,128)(2,1)S(1)}, f32[512,128]{1,0:T(8,128)S(1)}) custom-call(bf16[48,512]{1,0:T(8,128)(2,1)S(1)} %collective-permute-done.prev_ref, bf16[80,512]{1,0:T(8,128)(2,1)S(1)} %get-tuple-element.27.own_ref, bf16[1056,128]{1,0:T(8,128)(2,1)S(1)} %get-tuple-element.39.late_field_ref, ...), custom_call_target="tpu_custom_call" | custom-call | flops 1073741824 | bytes 4194304 | tf_op jit(solution)/shard_map/pallas_call | solution.py:551
  25.2 16.0 %all_to_all.23 = f32[32,16,128]{2,1,0:T(8,128)S(1)} all-to-all(f32[32,16,128]{2,1,0:T(8,128)S(1)} %bitcast.8), channel_id=1, replica_groups=mesh['z_hi'=4,'y'=8,'core'=2,'z_lo'=2,'x'=4] {'x','z_lo','z_hi'}, dimensions={0} | all-to-all | bytes 524288 | tf_op jit(solution)/shard_map/all_to_all | solution.py:592
  41.2 16.4 %all_to_all.24 = f32[16,16,128]{2,1,0:T(8,128)S(1)} all-to-all(f32[16,16,128]{2,1,0:T(8,128)S(1)} %tile.4), channel_id=1, replica_groups=mesh['z_hi'=4,'y'=8,'core'=2,'z_lo'=2,'x'=4] {'core','y'}, dimensions={0} | all-to-all | bytes 262144 | tf_op jit(solution)/shard_map/all_to_all | solution.py:592
  57.7 16.1 %all_to_all.25 = f32[32,16,128]{2,1,0:T(8,128)S(1)} all-to-all(f32[32,16,128]{2,1,0:T(8,128)S(1)} %tile.5), channel_id=1, replica_groups=mesh['z_hi'=4,'y'=8,'core'=2,'z_lo'=2,'x'=4] {'x','z_lo','z_hi'}, dimensions={0} | all-to-all | bytes 524288 | tf_op jit(solution)/shard_map/all_to_all | solution.py:592
  73.8 0.9 %shard_map.108 = (bf16[64,128]{1,0:T(8,128)(2,1)}, f32[138,128]{1,0:T(8,128)}) custom-call(f32[512,128]{1,0:T(8,128)S(1)} %bitcast.9, s32[1,512]{1,0:T(1,128)S(1)} %get-tuple-element.45.target_ref, f32[138,128]{1,0:T(8,128)S(1)} %get-tuple-element.46.kept_ref, bf16[64,128]{1,0:T(8,128)(2,1)S(1)} %get-tuple-element.47.feature_ref), custom_call_target="tpu_custom_call" | custom-call | flops 134217728 | bytes 1048576 | tf_op jit(solution)/shard_map/pallas_call | solution.py:572
  (4 shorter events, 0.1 us)
Async XLA Ops:
  1.8 18.5 %collective-permute-start.1 = (bf16[80,512]{1,0:T(8,128)(2,1)S(1)}, bf16[80,512]{1,0:T(8,128)(2,1)S(1)}, u32[]{:S(2)}, u32[]{:S(2)}) collective-permute-start(bf16[80,512]{1,0:T(8,128)(2,1)S(1)} %get-tuple-element.27.own_ref), channel_id=1, source_target_pairs={{0,504},{8,0},{16,8},{24,16},{32,24},{40,32},{48,40},{56,48},{64,5... | collective-permute-start | bytes 245768 | tf_op jit(solution)/shard_map/ppermute | solution.py:619
  3.7 16.6 %collective-permute-start.2 = (bf16[64,512]{1,0:T(8,128)(2,1)S(1)}, bf16[64,512]{1,0:T(8,128)(2,1)S(1)}, u32[]{:S(2)}, u32[]{:S(2)}) collective-permute-start(bf16[64,512]{1,0:T(8,128)(2,1)S(1)} %get-tuple-element.28), channel_id=1, source_target_pairs={{0,496},{8,504},{16,0},{24,8},{32,16},{40,24},{48,32},{56,40},{64,... | collective-permute-start | bytes 196616 | tf_op jit(solution)/shard_map/ppermute | solution.py:619
  17.4 5.4 %collective-permute-start = (bf16[48,512]{1,0:T(8,128)(2,1)S(1)}, bf16[48,512]{1,0:T(8,128)(2,1)S(1)}, u32[]{:S(2)}, u32[]{:S(2)}) collective-permute-start(bf16[48,512]{1,0:T(8,128)(2,1)S(1)} %get-tuple-element.26), channel_id=1, source_target_pairs={{0,8},{8,16},{16,24},{24,32},{32,40},{40,48},{48,56},{56,64},{64,7... | collective-permute-start | bytes 147464 | tf_op jit(solution)/shard_map/ppermute | solution.py:619
  20.3 2.5 %copy-start = (f32[256,128]{1,0:T(8,128)S(1)}, f32[256,128]{1,0:T(8,128)}, u32[]{:S(2)}) copy-start(f32[256,128]{1,0:T(8,128)} %constant.15.clone.select_ref) | copy-start | bytes 393220

commit v7 on v6

--- a/solution.py
+++ b/solution.py
@@ -136,10 +136,10 @@
     target_ref,
     ordered_ref,
 ):
-    for col in range(6):
+    for r in range(4):
         cell = lax.broadcasted_iota(jnp.int32, (512, 128), 0)
-        comb_ref[:, col * 128 : col * 128 + 128] = jnp.where(
-            cell == 4 * lanes_of((512, 128)) + col - 1, 1.0, 0.0
+        comb_ref[:, r * 128 : r * 128 + 128] = jnp.where(
+            cell == 4 * lanes_of((512, 128)) + r, 1.0, 0.0
         ).astype(BF16)
     ordered_ref[:, 768:896] = jnp.zeros((64, 128), F32)
     ordered_ref[:, 0:864] = dot(channel_order().astype(BF16), w2_ref[...])
@@ -217,11 +217,23 @@
 
 
 def expand(source, comb_ref, field_ref):
-    for col in range(6):
-        part = dot(source, comb_ref[:, col * 128 : col * 128 + 128]).astype(BF16)
+    phases = [dot(source, comb_ref[:, r * 128 : r * 128 + 128]) for r in range(4)]
+    columns = [from_left(phases[3])] + phases + [from_right(phases[0])]
+    for col, part in enumerate(columns):
+        part = part.astype(BF16)
         for layer in range(source.shape[0] // 16):
             at = layer * 96 + col * 16
             field_ref[at : at + 16, :] = part[layer * 16 : layer * 16 + 16, :]
+
+
+def exact_pick(value, select):
+    high = value.astype(BF16)
+    rest = value - high.astype(F32)
+    middle = rest.astype(BF16)
+    low = (rest - middle.astype(F32)).astype(BF16)
+    rows = value.shape[0]
+    moved = dot(jnp.concatenate([high, middle, low], axis=0), select)
+    return moved[0:rows] + moved[rows : 2 * rows] + moved[2 * rows : 3 * rows]
 
 
 def around(layers, half):
@@ -518,7 +530,7 @@
             jax.ShapeDtypeStruct((256, 256), BF16),
             jax.ShapeDtypeStruct((256, 768), BF16),
             jax.ShapeDtypeStruct((128, 1536), BF16),
-            jax.ShapeDtypeStruct((512, 768), BF16),
+            jax.ShapeDtypeStruct((512, 512), BF16),
             jax.ShapeDtypeStruct((32, 128), F32),
             jax.ShapeDtypeStruct((64, 128), F32),
             jax.ShapeDtypeStruct((1, NB_PAD), jnp.int32),

time: 75 us -> 75.1 us (level)
  no operation moved by 1% of the time
where the time goes in v7:
time: 75.1 us; the launch traced here: 74.8 us
  blocking collectives  48.5 us (65%)
  starting transfers between devices  17.6 us (23%)
  Pallas kernels  6.62 us (9%)
  waiting for transfers between devices  1.23 us (2%)
    all_to_all x3, blocking collectives, exchange(): return lax.all_to_all(rows, axes, 0, 0, tiled=True)  48.5 us
    ppermute x3, starting transfers between devices, from_slab(): return lax.ppermute(rows, SLAB, pairs)  17.6 us
    pallas_call x1, Pallas kernels, forward_backward(): pl.pallas_call(main_kernel, out_shape=(jax.ShapeDtypeStruct((64, 128), BF...  2.38 us
  transfers between devices with their start and end apart: 3, of which 1 were waited for; matrix products, arithmetic and copies ran while one was open for 0% of the time, Pallas kernels for 3%

profile of v7, /device:TPU:8, one launch (start us, length us, event | category | flops | bytes accessed | tf_op | source)
XLA Modules:
  0.0 74.8 jit_solution(3895139167717617252)
XLA Ops:
  0.6 1.1 %shard_map.104 = (bf16[80,512]{1,0:T(8,128)(2,1)S(1)}, bf16[48,512]{1,0:T(8,128)(2,1)S(1)}, bf16[64,512]{1,0:T(8,128)(2,1)S(1)}, bf16[32,108]{1,0:T(8,128)(2,1)S...) custom-call(bf16[1,4,4,4,512]{4,3,2,1,0:T(4,128)(2,1)} %universe_hbm, ...), custom_call_target="tpu_custom_call" | custom-call | flops 65536 | bytes 262144 | tf_op jit(solution)/shard_map/pallas_call | solution.py:506
  1.8 1.9 %collective-permute-start.1 = (bf16[80,512]{1,0:T(8,128)(2,1)S(1)}, bf16[80,512]{1,0:T(8,128)(2,1)S(1)}, u32[]{:S(2)}, u32[]{:S(2)}) collective-permute-start(bf16[80,512]{1,0:T(8,128)(2,1)S(1)} %get-tuple-element.27.own_ref), channel_id=1, source_target_pairs={{0,504},{8,0},{16,8},{24,16},{32,24},{40,32},{48,40},{56,48},{64,5... | collective-permute-start | bytes 245768 | tf_op jit(solution)/shard_map/ppermute | solution.py:631
  3.7 13.7 %collective-permute-start.2 = (bf16[64,512]{1,0:T(8,128)(2,1)S(1)}, bf16[64,512]{1,0:T(8,128)(2,1)S(1)}, u32[]{:S(2)}, u32[]{:S(2)}) collective-permute-start(bf16[64,512]{1,0:T(8,128)(2,1)S(1)} %get-tuple-element.28), channel_id=1, source_target_pairs={{0,496},{8,504},{16,0},{24,8},{32,16},{40,24},{48,32},{56,40},{64,... | collective-permute-start | bytes 196616 | tf_op jit(solution)/shard_map/ppermute | solution.py:631
  17.4 1.9 %collective-permute-start = (bf16[48,512]{1,0:T(8,128)(2,1)S(1)}, bf16[48,512]{1,0:T(8,128)(2,1)S(1)}, u32[]{:S(2)}, u32[]{:S(2)}) collective-permute-start(bf16[48,512]{1,0:T(8,128)(2,1)S(1)} %get-tuple-element.26), channel_id=1, source_target_pairs={{0,8},{8,16},{16,24},{24,32},{32,40},{40,48},{48,56},{56,64},{64,7... | collective-permute-start | bytes 147464 | tf_op jit(solution)/shard_map/ppermute | solution.py:631
  19.4 0.9 %shard_map.105 = (bf16[256,256]{1,0:T(8,128)(2,1)S(1)}, bf16[256,768]{1,0:T(8,128)(2,1)S(1)}, bf16[128,1536]{1,0:T(8,128)(2,1)S(1)}, bf16[512,512]{1,0:T(8,128)(...) custom-call(s32[1]{0:T(128)} %bitcast.4.rank_ref, ...), custom_call_target="tpu_custom_call" | custom-call | flops 67108864 | bytes 4194304 | tf_op jit(solution)/shard_map/pallas_call | solution.py:527
  20.2 0.0 collective-permute-done.2.after_ref
  20.2 0.0 collective-permute-done.1.next_ref
  20.2 0.0 copy-start
  20.3 1.3 %shard_map.106 = (bf16[1056,128]{1,0:T(8,128)(2,1)S(1)}, bf16[1024,128]{1,0:T(8,128)(2,1)S(1)}, f32[512,512]{1,0:T(8,128)S(1)}, bf16[1024,128]{1,0:T(8,128)(2,1)S(1)}) custom-call(bf16[80,512]{1,0:T(8,128)(2,1)S(1)} %get-tuple-element.27.own_ref, bf16[80,512]{1,0:T(8,128)(2,1)S(1)} %collective-permute-done.1.next_ref, ...), custom_call_target="tpu_custom_call" | custom-call | flops 1073741824 | bytes 4194304 | tf_op jit(solution)/shard_map/pallas_call | solution.py:547
  21.6 1.2 %collective-permute-done.prev_ref = bf16[48,512]{1,0:T(8,128)(2,1)S(1)} collective-permute-done((bf16[48,512]{1,0:T(8,128)(2,1)S(1)}, bf16[48,512]{1,0:T(8,128)(2,1)S(1)}, u32[]{:S(2)}, u32[]{:S(2)}) %collective-permute-start) | collective-permute-done | bytes 49184 | tf_op jit(solution)/shard_map/ppermute | solution.py:631
  22.8 0.0 copy-done
  22.8 2.4 %shard_map.107 = (bf16[64,128]{1,0:T(8,128)(2,1)S(1)}, f32[512,128]{1,0:T(8,128)S(1)}) custom-call(bf16[48,512]{1,0:T(8,128)(2,1)S(1)} %collective-permute-done.prev_ref, bf16[80,512]{1,0:T(8,128)(2,1)S(1)} %get-tuple-element.27.own_ref, bf16[1056,128]{1,0:T(8,128)(2,1)S(1)} %get-tuple-element.39.late_field_ref, ...), custom_call_target="tpu_custom_call" | custom-call | flops 1073741824 | bytes 4194304 | tf_op jit(solution)/shard_map/pallas_call | solution.py:563
  25.2 16.0 %all_to_all.23 = f32[32,16,128]{2,1,0:T(8,128)S(1)} all-to-all(f32[32,16,128]{2,1,0:T(8,128)S(1)} %bitcast.8), channel_id=1, replica_groups=mesh['z_hi'=4,'y'=8,'core'=2,'z_lo'=2,'x'=4] {'x','z_lo','z_hi'}, dimensions={0} | all-to-all | bytes 524288 | tf_op jit(solution)/shard_map/all_to_all | solution.py:604
  41.3 16.4 %all_to_all.24 = f32[16,16,128]{2,1,0:T(8,128)S(1)} all-to-all(f32[16,16,128]{2,1,0:T(8,128)S(1)} %tile.4), channel_id=1, replica_groups=mesh['z_hi'=4,'y'=8,'core'=2,'z_lo'=2,'x'=4] {'core','y'}, dimensions={0} | all-to-all | bytes 262144 | tf_op jit(solution)/shard_map/all_to_all | solution.py:604
  57.8 16.1 %all_to_all.25 = f32[32,16,128]{2,1,0:T(8,128)S(1)} all-to-all(f32[32,16,128]{2,1,0:T(8,128)S(1)} %tile.5), channel_id=1, replica_groups=mesh['z_hi'=4,'y'=8,'core'=2,'z_lo'=2,'x'=4] {'x','z_lo','z_hi'}, dimensions={0} | all-to-all | bytes 524288 | tf_op jit(solution)/shard_map/all_to_all | solution.py:604
  73.9 0.9 %shard_map.108 = (bf16[64,128]{1,0:T(8,128)(2,1)}, f32[138,128]{1,0:T(8,128)}) custom-call(f32[512,128]{1,0:T(8,128)S(1)} %bitcast.9, s32[1,512]{1,0:T(1,128)S(1)} %get-tuple-element.45.target_ref, f32[138,128]{1,0:T(8,128)S(1)} %get-tuple-element.46.kept_ref, bf16[64,128]{1,0:T(8,128)(2,1)S(1)} %get-tuple-element.47.feature_ref), custom_call_target="tpu_custom_call" | custom-call | flops 134217728 | bytes 1048576 | tf_op jit(solution)/shard_map/pallas_call | solution.py:584
  (4 shorter events, 0.1 us)
Async XLA Ops:
  1.8 18.5 %collective-permute-start.1 = (bf16[80,512]{1,0:T(8,128)(2,1)S(1)}, bf16[80,512]{1,0:T(8,128)(2,1)S(1)}, u32[]{:S(2)}, u32[]{:S(2)}) collective-permute-start(bf16[80,512]{1,0:T(8,128)(2,1)S(1)} %get-tuple-element.27.own_ref), channel_id=1, source_target_pairs={{0,504},{8,0},{16,8},{24,16},{32,24},{40,32},{48,40},{56,48},{64,5... | collective-permute-start | bytes 245768 | tf_op jit(solution)/shard_map/ppermute | solution.py:631
  3.7 16.5 %collective-permute-start.2 = (bf16[64,512]{1,0:T(8,128)(2,1)S(1)}, bf16[64,512]{1,0:T(8,128)(2,1)S(1)}, u32[]{:S(2)}, u32[]{:S(2)}) collective-permute-start(bf16[64,512]{1,0:T(8,128)(2,1)S(1)} %get-tuple-element.28), channel_id=1, source_target_pairs={{0,496},{8,504},{16,0},{24,8},{32,16},{40,24},{48,32},{56,40},{64,... | collective-permute-start | bytes 196616 | tf_op jit(solution)/shard_map/ppermute | solution.py:631
  17.4 5.4 %collective-permute-start = (bf16[48,512]{1,0:T(8,128)(2,1)S(1)}, bf16[48,512]{1,0:T(8,128)(2,1)S(1)}, u32[]{:S(2)}, u32[]{:S(2)}) collective-permute-start(bf16[48,512]{1,0:T(8,128)(2,1)S(1)} %get-tuple-element.26), channel_id=1, source_target_pairs={{0,8},{8,16},{16,24},{24,32},{32,40},{40,48},{48,56},{56,64},{64,7... | collective-permute-start | bytes 147464 | tf_op jit(solution)/shard_map/ppermute | solution.py:631
  20.2 2.6 %copy-start = (f32[256,128]{1,0:T(8,128)S(1)}, f32[256,128]{1,0:T(8,128)}, u32[]{:S(2)}) copy-start(f32[256,128]{1,0:T(8,128)} %constant.15.clone.select_ref) | copy-start | bytes 393220

commit v8 on v7

--- a/solution.py
+++ b/solution.py
@@ -407,17 +407,14 @@
         grad1 = term if grad1 is None else grad1 + term
         bias_sum1 = bias_term if bias_sum1 is None else bias_sum1 + bias_term
 
-    exact = lax.Precision.HIGHEST
     bias_row1 = bias_sum1[:, 0:128] + bias_sum1[:, 128:256]
     bias_row1 = bias_row1 + turned(bias_row1, 64)
     bias_row1 = bias_row1 + turned(bias_row1, 32)
     q = lax.broadcasted_iota(jnp.int32, (128, 128), 0)
     lane = 32 + 4 * (q % 16) + q % 64 // 16
-    bias_row2 = dot(
-        bias_sum2[:, 0:128] + bias_sum2[:, 128:256],
-        jnp.where(lane == lanes_of((128, 128)), 1.0, 0.0),
-        exact,
-    )
+    both = jnp.concatenate([bias_sum2[:, 0:128] + bias_sum2[:, 128:256]] * 2, axis=0)
+    order = jnp.where(lane == lanes_of((128, 128)), 1.0, 0.0).astype(BF16)
+    bias_row2 = exact_pick(both, order)
 
     y_of = lanes_of((32, 128)) % 4
     parts = []
@@ -430,7 +427,7 @@
                 block = grad1[row : row + 32, at : at + 128]
                 part = part + turned(jnp.where(near, block, 0.0), -(r * 16 + y))
         parts.append(part)
-    flat1 = dot(jnp.concatenate(parts, axis=1), select_ref[...], exact)
+    flat1 = exact_pick(jnp.concatenate(parts, axis=1), select_ref[...])
     rows = [None] * 28
     lane8 = lanes_of((8, 128))
     for o in range(32):
@@ -577,7 +574,7 @@
         ],
         compiler_params=params(),
         cost_estimate=pl.CostEstimate(flops=1 << 30, bytes_accessed=4 << 20, transcendentals=0),
-    )(before, own, *late, *weights, jnp.asarray(np.pad(tap_selection().T, ((0, 0), (0, 20))), F32))
+    )(before, own, *late, *weights, jnp.asarray(np.pad(tap_selection().T, ((0, 0), (0, 20))), BF16))
 
 
 def add_owned(blocks, target, kept, feature):

time: 75.1 us -> 75.1 us (level)
  no operation moved by 1% of the time
where the time goes in v8:
time: 75.1 us; the launch traced here: 74.7 us
  blocking collectives  48.5 us (65%)
  starting transfers between devices  17.6 us (23%)
  Pallas kernels  6.6 us (9%)
  waiting for transfers between devices  1.23 us (2%)
    all_to_all x3, blocking collectives, exchange(): return lax.all_to_all(rows, axes, 0, 0, tiled=True)  48.5 us
    ppermute x3, starting transfers between devices, from_slab(): return lax.ppermute(rows, SLAB, pairs)  17.6 us
    pallas_call x1, Pallas kernels, forward_backward(): pl.pallas_call(main_kernel, out_shape=(jax.ShapeDtypeStruct((64, 128), BF...  2.37 us
  transfers between devices with their start and end apart: 3, of which 1 were waited for; matrix products, arithmetic and copies ran while one was open for 0% of the time, Pallas kernels for 3%

profile of v8, /device:TPU:8, one launch (start us, length us, event | category | flops | bytes accessed | tf_op | source)
XLA Modules:
  0.0 74.7 jit_solution(15823775639307888089)
XLA Ops:
  0.6 1.1 %shard_map.104 = (bf16[80,512]{1,0:T(8,128)(2,1)S(1)}, bf16[48,512]{1,0:T(8,128)(2,1)S(1)}, bf16[64,512]{1,0:T(8,128)(2,1)S(1)}, bf16[32,108]{1,0:T(8,128)(2,1)S...) custom-call(bf16[1,4,4,4,512]{4,3,2,1,0:T(4,128)(2,1)} %universe_hbm, ...), custom_call_target="tpu_custom_call" | custom-call | flops 65536 | bytes 262144 | tf_op jit(solution)/shard_map/pallas_call | solution.py:503
  1.8 1.9 %collective-permute-start.1 = (bf16[80,512]{1,0:T(8,128)(2,1)S(1)}, bf16[80,512]{1,0:T(8,128)(2,1)S(1)}, u32[]{:S(2)}, u32[]{:S(2)}) collective-permute-start(bf16[80,512]{1,0:T(8,128)(2,1)S(1)} %get-tuple-element.27.own_ref), channel_id=1, source_target_pairs={{0,504},{8,0},{16,8},{24,16},{32,24},{40,32},{48,40},{56,48},{64,5... | collective-permute-start | bytes 245768 | tf_op jit(solution)/shard_map/ppermute | solution.py:628
  3.7 13.7 %collective-permute-start.2 = (bf16[64,512]{1,0:T(8,128)(2,1)S(1)}, bf16[64,512]{1,0:T(8,128)(2,1)S(1)}, u32[]{:S(2)}, u32[]{:S(2)}) collective-permute-start(bf16[64,512]{1,0:T(8,128)(2,1)S(1)} %get-tuple-element.28), channel_id=1, source_target_pairs={{0,496},{8,504},{16,0},{24,8},{32,16},{40,24},{48,32},{56,40},{64,... | collective-permute-start | bytes 196616 | tf_op jit(solution)/shard_map/ppermute | solution.py:628
  17.4 1.9 %collective-permute-start = (bf16[48,512]{1,0:T(8,128)(2,1)S(1)}, bf16[48,512]{1,0:T(8,128)(2,1)S(1)}, u32[]{:S(2)}, u32[]{:S(2)}) collective-permute-start(bf16[48,512]{1,0:T(8,128)(2,1)S(1)} %get-tuple-element.26), channel_id=1, source_target_pairs={{0,8},{8,16},{16,24},{24,32},{32,40},{40,48},{48,56},{56,64},{64,7... | collective-permute-start | bytes 147464 | tf_op jit(solution)/shard_map/ppermute | solution.py:628
  19.4 0.9 %shard_map.105 = (bf16[256,256]{1,0:T(8,128)(2,1)S(1)}, bf16[256,768]{1,0:T(8,128)(2,1)S(1)}, bf16[128,1536]{1,0:T(8,128)(2,1)S(1)}, bf16[512,512]{1,0:T(8,128)(...) custom-call(s32[1]{0:T(128)} %bitcast.4.rank_ref, ...), custom_call_target="tpu_custom_call" | custom-call | flops 67108864 | bytes 4194304 | tf_op jit(solution)/shard_map/pallas_call | solution.py:524
  20.2 0.0 collective-permute-done.2.after_ref
  20.2 0.0 collective-permute-done.1.next_ref
  20.2 0.0 copy-start
  20.3 1.3 %shard_map.106 = (bf16[1056,128]{1,0:T(8,128)(2,1)S(1)}, bf16[1024,128]{1,0:T(8,128)(2,1)S(1)}, f32[512,512]{1,0:T(8,128)S(1)}, bf16[1024,128]{1,0:T(8,128)(2,1)S(1)}) custom-call(bf16[80,512]{1,0:T(8,128)(2,1)S(1)} %get-tuple-element.27.own_ref, bf16[80,512]{1,0:T(8,128)(2,1)S(1)} %collective-permute-done.1.next_ref, ...), custom_call_target="tpu_custom_call" | custom-call | flops 1073741824 | bytes 4194304 | tf_op jit(solution)/shard_map/pallas_call | solution.py:544
  21.6 1.2 %collective-permute-done.prev_ref = bf16[48,512]{1,0:T(8,128)(2,1)S(1)} collective-permute-done((bf16[48,512]{1,0:T(8,128)(2,1)S(1)}, bf16[48,512]{1,0:T(8,128)(2,1)S(1)}, u32[]{:S(2)}, u32[]{:S(2)}) %collective-permute-start) | collective-permute-done | bytes 49184 | tf_op jit(solution)/shard_map/ppermute | solution.py:628
  22.8 0.0 copy-done
  22.8 2.4 %shard_map.107 = (bf16[64,128]{1,0:T(8,128)(2,1)S(1)}, f32[512,128]{1,0:T(8,128)S(1)}) custom-call(bf16[48,512]{1,0:T(8,128)(2,1)S(1)} %collective-permute-done.prev_ref, bf16[80,512]{1,0:T(8,128)(2,1)S(1)} %get-tuple-element.27.own_ref, bf16[1056,128]{1,0:T(8,128)(2,1)S(1)} %get-tuple-element.39.late_field_ref, ...), custom_call_target="tpu_custom_call" | custom-call | flops 1073741824 | bytes 4194304 | tf_op jit(solution)/shard_map/pallas_call | solution.py:560
  25.2 16.0 %all_to_all.23 = f32[32,16,128]{2,1,0:T(8,128)S(1)} all-to-all(f32[32,16,128]{2,1,0:T(8,128)S(1)} %bitcast.8), channel_id=1, replica_groups=mesh['z_hi'=4,'y'=8,'core'=2,'z_lo'=2,'x'=4] {'x','z_lo','z_hi'}, dimensions={0} | all-to-all | bytes 524288 | tf_op jit(solution)/shard_map/all_to_all | solution.py:601
  41.3 16.4 %all_to_all.24 = f32[16,16,128]{2,1,0:T(8,128)S(1)} all-to-all(f32[16,16,128]{2,1,0:T(8,128)S(1)} %tile.4), channel_id=1, replica_groups=mesh['z_hi'=4,'y'=8,'core'=2,'z_lo'=2,'x'=4] {'core','y'}, dimensions={0} | all-to-all | bytes 262144 | tf_op jit(solution)/shard_map/all_to_all | solution.py:601
  57.7 16.1 %all_to_all.25 = f32[32,16,128]{2,1,0:T(8,128)S(1)} all-to-all(f32[32,16,128]{2,1,0:T(8,128)S(1)} %tile.5), channel_id=1, replica_groups=mesh['z_hi'=4,'y'=8,'core'=2,'z_lo'=2,'x'=4] {'x','z_lo','z_hi'}, dimensions={0} | all-to-all | bytes 524288 | tf_op jit(solution)/shard_map/all_to_all | solution.py:601
  73.8 0.9 %shard_map.108 = (bf16[64,128]{1,0:T(8,128)(2,1)}, f32[138,128]{1,0:T(8,128)}) custom-call(f32[512,128]{1,0:T(8,128)S(1)} %bitcast.9, s32[1,512]{1,0:T(1,128)S(1)} %get-tuple-element.45.target_ref, f32[138,128]{1,0:T(8,128)S(1)} %get-tuple-element.46.kept_ref, bf16[64,128]{1,0:T(8,128)(2,1)S(1)} %get-tuple-element.47.feature_ref), custom_call_target="tpu_custom_call" | custom-call | flops 134217728 | bytes 1048576 | tf_op jit(solution)/shard_map/pallas_call | solution.py:581
  (4 shorter events, 0.1 us)
Async XLA Ops:
  1.8 18.5 %collective-permute-start.1 = (bf16[80,512]{1,0:T(8,128)(2,1)S(1)}, bf16[80,512]{1,0:T(8,128)(2,1)S(1)}, u32[]{:S(2)}, u32[]{:S(2)}) collective-permute-start(bf16[80,512]{1,0:T(8,128)(2,1)S(1)} %get-tuple-element.27.own_ref), channel_id=1, source_target_pairs={{0,504},{8,0},{16,8},{24,16},{32,24},{40,32},{48,40},{56,48},{64,5... | collective-permute-start | bytes 245768 | tf_op jit(solution)/shard_map/ppermute | solution.py:628
  3.7 16.5 %collective-permute-start.2 = (bf16[64,512]{1,0:T(8,128)(2,1)S(1)}, bf16[64,512]{1,0:T(8,128)(2,1)S(1)}, u32[]{:S(2)}, u32[]{:S(2)}) collective-permute-start(bf16[64,512]{1,0:T(8,128)(2,1)S(1)} %get-tuple-element.28), channel_id=1, source_target_pairs={{0,496},{8,504},{16,0},{24,8},{32,16},{40,24},{48,32},{56,40},{64,... | collective-permute-start | bytes 196616 | tf_op jit(solution)/shard_map/ppermute | solution.py:628
  17.4 5.4 %collective-permute-start = (bf16[48,512]{1,0:T(8,128)(2,1)S(1)}, bf16[48,512]{1,0:T(8,128)(2,1)S(1)}, u32[]{:S(2)}, u32[]{:S(2)}) collective-permute-start(bf16[48,512]{1,0:T(8,128)(2,1)S(1)} %get-tuple-element.26), channel_id=1, source_target_pairs={{0,8},{8,16},{16,24},{24,32},{32,40},{40,48},{48,56},{56,64},{64,7... | collective-permute-start | bytes 147464 | tf_op jit(solution)/shard_map/ppermute | solution.py:628
  20.2 2.6 %copy-start = (bf16[256,128]{1,0:T(8,128)(2,1)S(1)}, bf16[256,128]{1,0:T(8,128)(2,1)}, u32[]{:S(2)}) copy-start(bf16[256,128]{1,0:T(8,128)(2,1)} %constant.15.clone.select_ref) | copy-start | bytes 196612
